TPU v7x, 32 devices: a whole 2x2x4 slice. The times are simulated.
32 devices in a mesh: tm: 8 (over z, x), row: 4 (over y, core).
Axes of the slice: x: 2, y: 2, z: 4, core: 2. Of those that a mesh axis runs over, the one named last changes fastest.
Arguments:
- inputs: bfloat16 [1, 512, 16, 16, 256], P(None, 'tm', 'row'), may hold values from -6 to 6
- decays: float32 [512, 256], P('tm'), may hold values from 0.4 to 0.999999, as said below
- in_kernel: bfloat16 [3, 3, 256, 256], replicated, may hold values from -0.125 to 0.125
- out_kernel: bfloat16 [3, 3, 256, 256], replicated, may hold values from -0.125 to 0.125
- skip: float32 [256], replicated, may hold values from -1 to 1
- cotangent: bfloat16 [1, 512, 16, 16, 256], P(None, 'tm', 'row'), may hold values from -6 to 6
Outputs:
- outputs: bfloat16 [1, 512, 16, 16, 256], P(None, 'tm', 'row')
- in_kernel_grad: float32 [3, 3, 256, 256], replicated
- out_kernel_grad: float32 [3, 3, 256, 256], replicated
Inputs may be any that keep to these rules, and one draw needn't show every extreme that they name: `decays`: strictly below one.
All inputs are finite; a program needn't handle non-finite values.
Results may differ from a plain program's by a relative error of at most 0.0043.
Values may be sent and summed in bfloat16 or wider, within the bound.
No kernel may reach another device: no remote copies, remote signals or barrier semaphores. Data moves between devices by JAX's collectives and lax.ppermute only.
A program may use at most 128 MiB of HBM per device.

v0:
```python
import functools
import math

import jax
import jax.numpy as jnp
from jax import lax
from jax.experimental import pallas as pl
from jax.experimental.pallas import tpu as pltpu
from jax.sharding import PartitionSpec as P

BF16 = jnp.bfloat16
F32 = jnp.float32


SCALARS = pl.BlockSpec(memory_space=pltpu.SMEM)
ANYWHERE = pl.BlockSpec(memory_space=pl.ANY)
TOKEN = jax.ShapeDtypeStruct((8, 128), F32)
TOKEN_SPEC = pl.BlockSpec((8, 128), lambda *b: (0, 0))


def params(mib=20):
    return pltpu.CompilerParams(
        dimension_semantics=("arbitrary",), vmem_limit_bytes=mib * 1024 * 1024
    )


def cost(flops, nbytes):
    return pl.CostEstimate(flops=int(flops), bytes_accessed=int(nbytes), transcendentals=0)


def shifted(cells, width):
    count = cells.shape[0]
    wide = cells.astype(F32)
    column = lax.broadcasted_iota(jnp.int32, (count, 1), 0) % width
    left = jnp.where(column == 0, 0.0, pltpu.roll(wide, 1, 0))
    right = jnp.where(column == width - 1, 0.0, pltpu.roll(wide, count - 1, 0))
    return jnp.concatenate([left.astype(BF16), cells, right.astype(BF16)], axis=1)


def flat(block):
    return block.reshape(-1, block.shape[-1])


def dot(a, b):
    return jnp.dot(a, b, preferred_element_type=F32)


def interior_body(x_ref, w_ref, out_ref, s_ref):
    frames, rows, width, _ = x_ref.shape
    lines = frames * width
    for r in range(rows):
        s_ref[r] = shifted(flat(x_ref[:, r]), width)

    def conv(first, count, taps):
        lhs = jnp.concatenate(
            [flat(s_ref[first + i - 1 : first + i - 1 + count]) for i in taps], axis=1
        )
        rhs = w_ref[taps[0] : taps[-1] + 1].reshape(len(taps) * w_ref.shape[1], w_ref.shape[2])
        out_ref[first : first + count] = dot(lhs, rhs).reshape(count, frames, width, -1)

    conv(1, rows - 2, (0, 1, 2))
    conv(0, 1, (1, 2))
    conv(rows - 1, 1, (0, 1))


def interior_plain_kernel(x_ref, w_ref, out_ref, s_ref):
    interior_body(x_ref, w_ref, out_ref, s_ref)


def interior_flipped_kernel(x_ref, w_ref, out_ref, wt_ref, s_ref):
    @pl.when(pl.program_id(0) == 0)
    def _():
        for i in range(3):
            for j in range(3):
                c = w_ref.shape[3]
                wt_ref[i, j * c : (j + 1) * c, :] = w_ref[2 - i, 2 - j].T

    interior_body(x_ref, wt_ref, out_ref, s_ref)


def interior_conv(x, w, flipped, block):
    frames, rows, width, c = x.shape
    p = w.shape[2] if flipped else w.shape[3]
    part_shape = jax.ShapeDtypeStruct((rows, frames, width, p), F32)
    part_spec = pl.BlockSpec((rows, block, width, p), lambda b: (0, b, 0, 0))
    x_spec = pl.BlockSpec((block, rows, width, c), lambda b: (b, 0, 0, 0))
    scratch = [pltpu.VMEM((rows, block * width, 3 * c), BF16)]
    estimate = cost(2 * frames * rows * width * 9 * c * p, 8 * 2**20)
    taps_spec = pl.BlockSpec((3, 3 * c, p), lambda b: (0, 0, 0))
    if flipped:
        return pl.pallas_call(
            interior_flipped_kernel,
            grid=(frames // block,),
            in_specs=[
                x_spec,
                pl.BlockSpec(w.shape, lambda b: (0, 0, 0, 0)),
            ],
            out_specs=[part_spec, taps_spec],
            out_shape=[part_shape, jax.ShapeDtypeStruct((3, 3 * c, p), BF16)],
            scratch_shapes=scratch,
            compiler_params=params(),
            cost_estimate=estimate,
            name="interior_cot",
        )(x, w)
    taps = w.reshape(3, 3 * c, p)
    part = pl.pallas_call(
        interior_plain_kernel,
        grid=(frames // block,),
        in_specs=[x_spec, taps_spec],
        out_specs=part_spec,
        out_shape=part_shape,
        scratch_shapes=scratch,
        compiler_params=params(),
        cost_estimate=estimate,
        name="interior_in",
    )(x, taps)
    return part, taps


def scan_kernel(backward, part_ref, up_ref, down_ref, w_ref, decay_ref, after_ref, local_ref, product_ref, end_ref, carry_ref, run_ref):
    rows, frames, width, p = part_ref.shape
    lines = rows * width

    @pl.when(pl.program_id(0) == 0)
    def _():
        carry_ref[...] = jnp.zeros_like(carry_ref)
        run_ref[...] = jnp.ones_like(run_ref)

    top = dot(shifted(flat(up_ref[...]), width), w_ref[0]).reshape(frames, width, p)
    low = dot(shifted(flat(down_ref[...]), width), w_ref[2]).reshape(frames, width, p)
    decay = decay_ref[...]
    scale = jnp.sqrt((1.0 - decay) * (1.0 + decay))
    state = [carry_ref[r * width : (r + 1) * width] for r in range(rows)]
    run = run_ref[0:1]
    for step in range(frames):
        t = frames - 1 - step if backward else step
        factor = decay[t : t + 1]
        gain = scale[t : t + 1]
        if backward:
            product_ref[t : t + 1] = run
        run = run * factor
        if not backward:
            product_ref[t : t + 1] = run
        for r in range(rows):
            term = part_ref[r, t]
            if r == 0:
                term = term + top[t]
            if r == rows - 1:
                term = term + low[t]
            if backward:
                full = term + state[r]
                local_ref[r, t] = full
                state[r] = factor * full
            else:
                state[r] = factor * state[r] + gain * term
                local_ref[r, t] = state[r]
    for r in range(rows):
        carry_ref[r * width : (r + 1) * width] = state[r]
    run_ref[...] = jnp.broadcast_to(run, run_ref.shape)

    @pl.when(pl.program_id(0) == pl.num_programs(0) - 1)
    def _():
        high = run.astype(BF16).astype(F32)
        products = [jnp.broadcast_to(high, (8, p)), jnp.broadcast_to(run - high, (8, p))]
        message = jnp.concatenate(state + products, axis=0).astype(BF16)
        for k in range(end_ref.shape[0]):
            end_ref[k] = message


def local_scan(part, up, down, half, taps, decays, block, backward, after):
    rows, frames, width, p = part.shape
    c = up.shape[-1]
    blocks = frames // block
    at = (lambda b: blocks - 1 - b) if backward else (lambda b: b)
    halo_spec = pl.BlockSpec((None, block, width, c), lambda b: (half, at(b), 0, 0))
    part_spec = pl.BlockSpec((rows, block, width, p), lambda b: (0, at(b), 0, 0))
    frame_spec = pl.BlockSpec((block, p), lambda b: (at(b), 0))
    lines = rows * width
    count = lax.axis_size("a") * lax.axis_size("x")
    return pl.pallas_call(
        functools.partial(scan_kernel, backward),
        grid=(blocks,),
        in_specs=[
            part_spec,
            halo_spec,
            halo_spec,
            pl.BlockSpec(taps.shape, lambda b: (0, 0, 0)),
            frame_spec,
            ANYWHERE,
        ],
        out_specs=[
            part_spec,
            frame_spec,
            pl.BlockSpec((count, lines + 16, p), lambda b: (0, 0, 0)),
        ],
        out_shape=[
            jax.ShapeDtypeStruct(part.shape, F32),
            jax.ShapeDtypeStruct((frames, p), F32),
            jax.ShapeDtypeStruct((count, lines + 16, p), BF16),
        ],
        scratch_shapes=[pltpu.VMEM((lines, p), F32), pltpu.VMEM((8, p), F32)],
        compiler_params=params(),
        cost_estimate=cost(4 * frames * width * 3 * c * p, 12 * 2**20),
        name="scan_back" if backward else "scan_fwd",
    )(part, up, down, taps, decays, after)


def combine(place_ref, ends_ref, total_ref, backward):
    place = place_ref[0]
    count = ends_ref.shape[0]
    lines = total_ref.shape[0]
    total = jnp.zeros(total_ref.shape, F32)
    order = range(count - 1, -1, -1) if backward else range(count)
    for k in order:
        block = ends_ref[k].astype(F32)
        product = block[lines : lines + 1] + block[lines + 8 : lines + 9]
        passed = product * total + block[0:lines]
        total = jnp.where(k > place if backward else k < place, passed, total)
    total_ref[...] = total


def split_halves(place_ref, sum_ref, sent_ref, kept_ref):
    half = kept_ref.shape[0]
    side = place_ref[1]
    sent_ref[...] = sum_ref[pl.ds(pl.multiple_of((1 - side) * half, 8), half)].astype(BF16)
    kept_ref[...] = sum_ref[pl.ds(pl.multiple_of(side * half, 8), half)]


def fill_rim(s_ref, up_ref, x_ref, down_ref):
    _, rows, width, _ = x_ref.shape
    s_ref[0] = shifted(flat(up_ref[...]), width)
    for r in range(rows):
        s_ref[r + 1] = shifted(flat(x_ref[:, r]), width)
    s_ref[rows + 1] = shifted(flat(down_ref[...]), width)


def out_grad_kernel(place_ref, ends_ref, local_ref, product_ref, cot_ref, up_ref, down_ref, after_ref, low_ref, first_ref, last_ref, sent_ref, kept_ref, token_ref, s_ref, total_ref, sum_ref):
    rows, frames, width, p = local_ref.shape
    c = cot_ref.shape[-1]

    @pl.when(pl.program_id(0) == 0)
    def _():
        combine(place_ref, ends_ref, total_ref, False)
        sum_ref[...] = jnp.zeros_like(sum_ref)
        token_ref[...] = jnp.zeros_like(token_ref)

    fill_rim(s_ref, up_ref, cot_ref, down_ref)
    product = product_ref[...]
    turned = []
    for r in range(rows):
        state = local_ref[r] + product[:, None, :] * total_ref[r * width : (r + 1) * width][None]
        low = state.astype(BF16)
        low_ref[r] = low
        if r == 0:
            first_ref[...] = low
        if r == rows - 1:
            last_ref[...] = low
        turned.append(flat(low).T)
    turned = jnp.concatenate(turned, axis=1)
    for i in range(3):
        gain = dot(turned, flat(s_ref[2 - i : 2 - i + rows]))
        for j in range(3):
            tap = 3 * i + j
            sum_ref[tap * p : (tap + 1) * p] += gain[:, (2 - j) * c : (3 - j) * c]

    @pl.when(pl.program_id(0) == pl.num_programs(0) - 1)
    def _():
        split_halves(place_ref, sum_ref, sent_ref, kept_ref)


def in_grad_kernel(place_ref, ends_ref, local_ref, product_ref, decay_ref, x_ref, up_ref, down_ref, after_ref, sent_ref, kept_ref, token_ref, s_ref, total_ref, sum_ref, flat_ref):
    rows, frames, width, p = local_ref.shape
    c = x_ref.shape[-1]

    @pl.when(pl.program_id(0) == 0)
    def _():
        combine(place_ref, ends_ref, total_ref, True)
        sum_ref[...] = jnp.zeros_like(sum_ref)
        token_ref[...] = jnp.zeros_like(token_ref)

    fill_rim(s_ref, up_ref, x_ref, down_ref)
    product = product_ref[...]
    decay = decay_ref[...]
    scale = jnp.sqrt((1.0 - decay) * (1.0 + decay))[:, None, :]
    turned = []
    for r in range(rows):
        adjoint = local_ref[r] + product[:, None, :] * total_ref[r * width : (r + 1) * width][None]
        turned.append(flat((scale * adjoint).astype(BF16)).T)
    turned = jnp.concatenate(turned, axis=1)
    for i in range(3):
        sum_ref[i] += dot(turned, flat(s_ref[i : i + rows]))

    @pl.when(pl.program_id(0) == pl.num_programs(0) - 1)
    def _():
        for i in range(3):
            for j in range(3):
                tap = 3 * i + j
                flat_ref[tap * c : (tap + 1) * c] = sum_ref[i, :, j * c : (j + 1) * c].T
        split_halves(place_ref, flat_ref, sent_ref, kept_ref)


def kernel_grads(places, ends, local, product, x, up, down, half, decays, block, after):
    rows, frames, width, p = local.shape
    c = x.shape[-1]
    halo_spec = pl.BlockSpec((None, block, width, c), lambda b: (half, b, 0, 0))
    local_spec = pl.BlockSpec((rows, block, width, p), lambda b: (0, b, 0, 0))
    frame_spec = pl.BlockSpec((block, p), lambda b: (b, 0))
    x_spec = pl.BlockSpec((block, rows, width, c), lambda b: (b, 0, 0, 0))
    lead = [SCALARS, pl.BlockSpec(ends.shape, lambda b: (0, 0, 0)), local_spec, frame_spec]
    tail = [x_spec, halo_spec, halo_spec]
    scratch = [
        pltpu.VMEM((rows + 2, block * width, 3 * c), BF16),
        pltpu.VMEM((rows * width, p), F32),
    ]
    estimate = cost(2 * frames * rows * width * 9 * c * p, 10 * 2**20)
    forward = decays is None
    lines, columns = (9 * p // 2, c) if forward else (9 * c // 2, p)
    grad_specs = [pl.BlockSpec((lines, columns), lambda b: (0, 0))] * 2 + [TOKEN_SPEC]
    grad_shapes = [
        jax.ShapeDtypeStruct((lines, columns), BF16),
        jax.ShapeDtypeStruct((lines, columns), F32),
        TOKEN,
    ]
    if forward:
        line_spec = pl.BlockSpec((block, width, p), lambda b: (b, 0, 0))
        line = jax.ShapeDtypeStruct((frames, width, p), BF16)
        return pl.pallas_call(
            out_grad_kernel,
            grid=(frames // block,),
            in_specs=lead + tail + [ANYWHERE],
            out_specs=[local_spec, line_spec, line_spec] + grad_specs,
            out_shape=[jax.ShapeDtypeStruct(local.shape, BF16), line, line] + grad_shapes,
            scratch_shapes=scratch + [pltpu.VMEM((2 * lines, columns), F32)],
            compiler_params=params(),
            cost_estimate=estimate,
            name="out_grad",
        )(places, ends, local, product, x, up, down, after)
    return pl.pallas_call(
        in_grad_kernel,
        grid=(frames // block,),
        in_specs=lead + [frame_spec] + tail + [ANYWHERE],
        out_specs=grad_specs,
        out_shape=grad_shapes,
        scratch_shapes=scratch
        + [pltpu.VMEM((3, p, 3 * c), F32), pltpu.VMEM((2 * lines, columns), F32)],
        compiler_params=params(),
        cost_estimate=estimate,
        name="in_grad",
    )(places, ends, local, product, decays, x, up, down, after)


def outputs_kernel(low_ref, up_ref, down_ref, w_ref, x_ref, skip_ref, after_ref, out_ref, token_ref, s_ref):
    token_ref[...] = jnp.zeros_like(token_ref)
    rows, frames, width, p = low_ref.shape
    s_ref[0] = shifted(flat(up_ref[...]), width)
    for r in range(rows):
        s_ref[r + 1] = shifted(flat(low_ref[r]), width)
    s_ref[rows + 1] = shifted(flat(down_ref[...]), width)
    lhs = jnp.concatenate([flat(s_ref[i : i + rows]) for i in range(3)], axis=1)
    mixed = dot(lhs, flat(w_ref[...])).reshape(rows, frames, width, -1)
    skip = skip_ref[...][0:1].reshape(1, 1, -1)
    for r in range(rows):
        out_ref[:, r] = (mixed[r] + skip * x_ref[:, r].astype(F32)).astype(BF16)


def outputs_conv(low, up, down, taps, x, skip, block, after):
    rows, frames, width, p = low.shape
    c = x.shape[-1]
    halo_spec = pl.BlockSpec((block, width, p), lambda b: (b, 0, 0))
    x_spec = pl.BlockSpec((block, rows, width, c), lambda b: (b, 0, 0, 0))
    return pl.pallas_call(
        outputs_kernel,
        grid=(frames // block,),
        in_specs=[
            pl.BlockSpec((rows, block, width, p), lambda b: (0, b, 0, 0)),
            halo_spec,
            halo_spec,
            pl.BlockSpec(taps.shape, lambda b: (0, 0, 0)),
            x_spec,
            pl.BlockSpec((1, c), lambda b: (0, 0)),
            ANYWHERE,
        ],
        out_specs=[x_spec, TOKEN_SPEC],
        out_shape=[jax.ShapeDtypeStruct(x.shape, BF16), TOKEN],
        scratch_shapes=[pltpu.VMEM((rows + 2, block * width, 3 * p), BF16)],
        compiler_params=params(),
        cost_estimate=cost(2 * frames * rows * width * 9 * c * p, 8 * 2**20),
        name="outputs_conv",
    )(low, up, down, taps, x, skip, after)


def edge_rows_kernel(x_ref, cot_ref, first_ref, last_ref, sems):
    rows = x_ref.shape[1]
    copies = []
    for k, ref in enumerate((x_ref, cot_ref)):
        copies.append(pltpu.make_async_copy(ref.at[:, 0], first_ref.at[k], sems.at[k, 0]))
        copies.append(pltpu.make_async_copy(ref.at[:, rows - 1], last_ref.at[k], sems.at[k, 1]))
    for copy in copies:
        copy.start()
    for copy in copies:
        copy.wait()


def edge_rows(x, cot):
    frames, rows, width, c = x.shape
    line = jax.ShapeDtypeStruct((2, frames, width, c), x.dtype)
    return pl.pallas_call(
        edge_rows_kernel,
        in_specs=[pl.BlockSpec(memory_space=pltpu.HBM)] * 2,
        out_specs=[ANYWHERE, ANYWHERE],
        out_shape=[line, line],
        scratch_shapes=[pltpu.SemaphoreType.DMA((2, 2))],
        compiler_params=pltpu.CompilerParams(vmem_limit_bytes=2**20),
        cost_estimate=cost(0, 2**22),
        name="edge_rows",
    )(x, cot)


def row_halo(first, last):
    axes = ("y", "core")
    count = lax.axis_size("y") * lax.axis_size("core")
    up = lax.ppermute(last, axes, [(i, i + 1) for i in range(count - 1)])
    down = lax.ppermute(first, axes, [(i + 1, i) for i in range(count - 1)])
    return up, down


CORES = [(0, 1), (1, 0)]


def small_call(body, name, out_shapes, operands, after, places=None):
    extra = [] if places is None else [places]

    def kernel(*refs):
        body(*refs[1 : len(extra) + len(operands) + 1], *refs[len(extra) + len(operands) + 1 : -1])
        refs[-1][...] = jnp.zeros_like(refs[-1])

    whole = pl.BlockSpec(memory_space=pltpu.VMEM)
    return pl.pallas_call(
        kernel,
        in_specs=[ANYWHERE] + [SCALARS] * len(extra) + [whole] * len(operands),
        out_specs=[whole] * (len(out_shapes) + 1),
        out_shape=[jax.ShapeDtypeStruct(*shape) for shape in out_shapes] + [TOKEN],
        compiler_params=pltpu.CompilerParams(vmem_limit_bytes=8 * 2**20),
        cost_estimate=cost(0, 2**21),
        name=name,
    )(after, *extra, *operands)


def add_kernel(kept_ref, got_ref, sent_ref, sum_ref):
    total = kept_ref[...] + got_ref[...].astype(F32)
    sum_ref[...] = total
    sent_ref[...] = total.astype(BF16)


def share_kernel(places_ref, kept_ref, parts_ref, out_ref):
    own = places_ref[2]
    total = kept_ref[own]
    for k in range(parts_ref.shape[0]):
        total = total + jnp.where(k == own, 0.0, parts_ref[k].astype(F32))
    total = total.astype(BF16)
    for k in range(out_ref.shape[0]):
        out_ref[k] = total


def total_kernel(scale, parts_ref, out_ref):
    total = parts_ref[0].astype(F32)
    for k in range(1, parts_ref.shape[0]):
        total = total + parts_ref[k].astype(F32)
    total = (total * scale).astype(BF16)
    for k in range(out_ref.shape[0]):
        out_ref[k] = total


def exchange(parts, axes):
    return lax.all_to_all(parts, axes, 0, 0)


def pieces(array, count):
    return array.reshape(count, array.shape[0] // count, array.shape[1])


def merge_kernel(places_ref, own_ref, other_ref, out_ref):
    @pl.when(pl.program_id(0) == 0)
    def _():
        out_ref[...] = own_ref[...].astype(F32)

    @pl.when(pl.program_id(0) == 1)
    def _():
        out_ref[...] = other_ref[...].astype(F32)


def merged(own, other, places):
    half, c = own.shape
    part_spec = pl.BlockSpec((half, c), lambda g, places: (0, 0))
    return pl.pallas_call(
        merge_kernel,
        grid_spec=pltpu.PrefetchScalarGridSpec(
            num_scalar_prefetch=1,
            grid=(2,),
            in_specs=[part_spec, part_spec],
            out_specs=pl.BlockSpec((half, c), lambda g, places: (jnp.bitwise_xor(g, places[1]), 0)),
        ),
        out_shape=jax.ShapeDtypeStruct((2 * half, c), F32),
        compiler_params=params(12),
        cost_estimate=cost(0, 10 * half * c),
        name="merge",
    )(places, own, other)


def per_device(inputs, decays, in_kernel, out_kernel, skip, cotangent):
    clips, frames, rows, width, c = inputs.shape
    p = in_kernel.shape[3]
    block = 16
    devices = math.prod(lax.axis_size(name) for name in ("a", "x", "y", "core"))
    grad_scale = 1.0 / math.sqrt(clips * frames * rows * width * devices)
    x = inputs.reshape(frames, rows, width, c)
    cot = cotangent.reshape(frames, rows, width, c)
    places = jnp.stack(
        [lax.axis_index(("a", "x")), lax.axis_index("core"), lax.axis_index(("x", "y"))]
    ).astype(jnp.int32)
    four = lax.axis_size("x") * lax.axis_size("y")
    deep = lax.axis_size("a")

    up, down = row_halo(*edge_rows(x, cot))
    x_part, x_taps = interior_conv(x, in_kernel, False, block)
    cot_part, cot_taps = interior_conv(cot, out_kernel, True, block)
    states, running, ends = local_scan(x_part, up, down, 0, x_taps, decays, block, False, decays)
    ends_all = exchange(ends, ("a", "x"))
    adjoint, trailing, starts = local_scan(
        cot_part, up, down, 1, cot_taps, decays, block, True, running
    )
    starts_all = exchange(starts, ("a", "x"))

    low, low_first, low_last, sent, kept, token = kernel_grads(
        places, ends_all, states, running, cot, up, down, 1, None, block, trailing
    )
    got = lax.ppermute(sent, "core", CORES)
    low_up, low_down = row_halo(low_first, low_last)

    def add(name, kept, got, token):
        return small_call(
            add_kernel, name, [(kept.shape, BF16), (kept.shape, F32)], [kept, got], token
        )

    def share(name, kept, parts, token):
        shape = (deep,) + parts.shape[1:]
        kept = pieces(kept, four)
        return small_call(share_kernel, name, [(shape, BF16)], [kept, parts], token, places)

    def total(name, parts, token):
        body = functools.partial(total_kernel, grad_scale)
        return small_call(body, name, [((four,) + parts.shape[1:], BF16)], [parts], token)

    sent, out_kept, out_token = add("out_add", kept, got, token)
    out_parts = exchange(pieces(sent, four), ("x", "y"))
    sent, kept, token = kernel_grads(
        places, starts_all, adjoint, trailing, x, up, down, 0, decays, block, out_token
    )
    got = lax.ppermute(sent, "core", CORES)
    out_parts, token = share("out_share", out_kept, out_parts, token)
    out_parts = exchange(out_parts, ("a",))
    sent, in_kept, token = add("in_add", kept, got, token)
    in_parts = exchange(pieces(sent, four), ("x", "y"))
    outputs, token = outputs_conv(
        low, low_up, low_down, out_kernel.reshape(3, 3 * p, c), x, skip.reshape(1, c), block, token
    )
    in_parts, token = share("in_share", in_kept, in_parts, token)
    in_parts = exchange(in_parts, ("a",))
    out_parts, token = total("out_total", out_parts, token)
    out_half = flat(exchange(out_parts, ("x", "y")))
    in_parts, token = total("in_total", in_parts, token)
    in_half = flat(exchange(in_parts, ("x", "y")))
    out_other = lax.ppermute(out_half, "core", CORES)
    in_other = lax.ppermute(in_half, "core", CORES)
    out_grad = merged(out_half, out_other, places)
    in_grad = merged(in_half, in_other, places)
    return (
        outputs.reshape(inputs.shape),
        in_grad.reshape(in_kernel.shape),
        out_grad.reshape(out_kernel.shape),
    )


def solution(mesh):
    frames = mesh.shape["tm"]
    rows = mesh.shape["row"]
    fine = jax.sharding.Mesh(
        mesh.devices.reshape(frames // 2, 2, rows // 2, 2), ("a", "x", "y", "core")
    )
    cells = P(None, ("a", "x"), ("y", "core"), None, None)
    return jax.shard_map(
        per_device,
        mesh=fine,
        in_specs=(cells, P(("a", "x"), None), P(), P(), P(), cells),
        out_specs=(cells, P(), P()),
        check_vma=False,
    )
```

profile of v0, /device:TPU:1, one launch (start us, length us, event | category | flops | bytes accessed | tf_op | source)
XLA Modules:
  0.0 189.4 jit_solution(7093428400988294960)
XLA Ops:
  5.2 4.5 %collective-permute-start = (bf16[2,64,16,256]{3,2,1,0:T(8,128)(2,1)}, bf16[2,64,16,256]{3,2,1,0:T(8,128)(2,1)S(1)}, u32[]{:S(2)}, u32[]{:S(2)}) collective-permute-start(bf16[2,64,16,256]{3,2,1,0:T(8,128)(2,1)} %get-tuple-element.37), channel_id=1, source_target_pairs={{0,1},{1,2},{2,3},{4,5},{5,6},{6,7},{8,9},{9,10},{10,11},{12,13},{... | collective-permute-start | bytes 3145736 | tf_op jit(solution)/shard_map/ppermute | solution.py:422
  13.3 5.0 %interior_in.1.part_ref = f32[4,64,16,256]{3,2,1,0:T(8,128)S(1)} custom-call(bf16[64,4,16,256]{3,2,1,0:T(8,128)(2,1)S(1)} %bitcast.25, bf16[3,768,256]{2,1,0:T(8,128)(2,1)S(1)} %bitcast.30), custom_call_target="tpu_custom_call" | custom-call | flops 4831838208 | bytes 8388608 | tf_op jit(solution)/shard_map/interior_in/pallas_call | solution.py:106
  18.3 3.4 %collective-permute-done.up_ref = bf16[2,64,16,256]{3,2,1,0:T(8,128)(2,1)S(1)} collective-permute-done((bf16[2,64,16,256]{3,2,1,0:T(8,128)(2,1)}, bf16[2,64,16,256]{3,2,1,0:T(8,128)(2,1)S(1)}, u32[]{:S(2)}, u32[]{:S(2)}) %collective-permute-start) | collective-permute-done | bytes 1048608 | tf_op jit(solution)/shard_map/ppermute | solution.py:422
  21.8 4.3 %collective-permute-done.1.down_ref = bf16[2,64,16,256]{3,2,1,0:T(8,128)(2,1)S(1)} collective-permute-done((bf16[2,64,16,256]{3,2,1,0:T(8,128)(2,1)}, bf16[2,64,16,256]{3,2,1,0:T(8,128)(2,1)S(1)}, u32[]{:S(2)}, u32[]{:S(2)}) %collective-permute-start.1) | collective-permute-done | bytes 1048608 | tf_op jit(solution)/shard_map/ppermute | solution.py:423
  31.0 5.5 %all-to-all-start = ((bf16[8,80,256]{2,1,0:T(8,128)(2,1)}), bf16[8,80,256]{2,1,0:T(8,128)(2,1)S(1)}, u32[]{:S(2)}, u32[]{:S(2)}) async-start(bf16[8,80,256]{2,1,0:T(8,128)(2,1)} %copy-done.18), calls=%async_computation | async-start | bytes 655360 | tf_op jit(solution)/shard_map/all_to_all | solution.py:475
  39.5 5.4 %interior_cot.1 = (f32[4,64,16,256]{3,2,1,0:T(8,128)S(1)}, bf16[3,768,256]{2,1,0:T(8,128)(2,1)S(1)}) custom-call(bf16[64,4,16,256]{3,2,1,0:T(8,128)(2,1)S(1)} %bitcast.22, bf16[3,3,256,256]{3,2,1,0:T(8,128)(2,1)S(1)} %copy-done.23), custom_call_target="tpu_custom_call" | custom-call | flops 4831838208 | bytes 8388608 | tf_op jit(solution)/shard_map/interior_cot/pallas_call | solution.py:91
  44.9 3.2 %scan_back.1 = (f32[4,64,16,256]{3,2,1,0:T(8,128)S(1)}, f32[64,256]{1,0:T(8,128)S(1)}, bf16[8,80,256]{2,1,0:T(8,128)(2,1)}) custom-call(f32[4,64,16,256]{3,2,1,0:T(8,128)S(1)} %get-tuple-element.42.part_ref, bf16[2,64,16,256]{3,2,1,0:T(8,128)(2,1)S(1)} %collective-permute-done.up_ref, bf16[2,64,16,256]{3,2,1,0:T(8,128)(2,1)S(1)} %collective-permute-done.1.down_ref, ...), custom_call_target="tpu_custom_call" | custom-call | flops 805306368 | bytes 12582912 | tf_op jit(solution)/shard_map/scan_back/pallas_call | solution.py:180
  53.9 8.6 %out_grad.1 = (bf16[4,64,16,256]{3,2,1,0:T(8,128)(2,1)S(1)}, bf16[64,16,256]{2,1,0:T(8,128)(2,1)}, bf16[64,16,256]{2,1,0:T(8,128)(2,1)}, bf16[1152,256]{1,0:T(8,...) custom-call(s32[3]{0:T(128)S(1)} %pad_add_fusion.place_ref.refs_1_.places_ref, ...), custom_call_target="tpu_custom_call" | custom-call | flops 4831838208 | bytes 10485760 | tf_op jit(solution)/shard_map/out_grad/pallas_call | solution.py:327
  64.8 5.4 %all-to-all-start.1 = ((bf16[8,80,256]{2,1,0:T(8,128)(2,1)}), bf16[8,80,256]{2,1,0:T(8,128)(2,1)}, u32[]{:S(2)}, u32[]{:S(2)}) async-start(bf16[8,80,256]{2,1,0:T(8,128)(2,1)} %get-tuple-element.48), calls=%async_computation.1 | async-start | bytes 655360 | tf_op jit(solution)/shard_map/all_to_all | solution.py:475
  74.4 4.4 %all-to-all-done.1.ends_ref = bf16[8,80,256]{2,1,0:T(8,128)(2,1)} async-done(((bf16[8,80,256]{2,1,0:T(8,128)(2,1)}), bf16[8,80,256]{2,1,0:T(8,128)(2,1)}, u32[]{:S(2)}, u32[]{:S(2)}) %all-to-all-start.1) | async-done | bytes 327712 | tf_op jit(solution)/shard_map/all_to_all | solution.py:475
  82.6 8.9 %in_grad.1 = (bf16[1152,256]{1,0:T(8,128)(2,1)S(1)}, f32[1152,256]{1,0:T(8,128)S(1)}, f32[8,128]{1,0:T(8,128)S(1)}) custom-call(s32[3]{0:T(128)S(1)} %pad_add_fusion.place_ref.refs_1_.places_ref, bf16[8,80,256]{2,1,0:T(8,128)(2,1)} %all-to-all-done.1.ends_ref, f32[4,64,16,256]{3,2,1,0:T(8,128)S(1)} %copy-done.20, ...), custom_call_target="tpu_custom_call" | custom-call | flops 4831838208 | bytes 10485760 | tf_op jit(solution)/shard_map/in_grad/pallas_call | solution.py:338
  91.5 2.9 %collective-permute-start.5 = (bf16[1152,256]{1,0:T(8,128)(2,1)S(1)}, bf16[1152,256]{1,0:T(8,128)(2,1)S(1)}, u32[]{:S(2)}, u32[]{:S(2)}) collective-permute-start(bf16[1152,256]{1,0:T(8,128)(2,1)S(1)} %get-tuple-element.59), channel_id=1, source_target_pairs={{0,1},{1,0},{2,3},{3,2},{4,5},{5,4},{6,7},{7,6},{8,9},{9,8},{10,11... | collective-permute-start | bytes 1769480 | tf_op jit(solution)/shard_map/ppermute | solution.py:559
  94.4 11.6 %all_to_all.40.refs_3_ = bf16[4,288,256]{2,1,0:T(8,128)(2,1)S(1)} all-to-all(bf16[4,288,256]{2,1,0:T(8,128)(2,1)S(1)} %bitcast.32), channel_id=1, replica_groups=mesh['a'=4,'x'=2,'y'=2,'core'=2] {'x','y'}, dimensions={0} | all-to-all | bytes 1179648 | tf_op jit(solution)/shard_map/all_to_all | solution.py:475
  109.4 3.5 %all-to-all-start.3 = ((bf16[4,288,256]{2,1,0:T(8,128)(2,1)}), bf16[4,288,256]{2,1,0:T(8,128)(2,1)S(1)}, u32[]{:S(2)}, u32[]{:S(2)}) async-start(bf16[4,288,256]{2,1,0:T(8,128)(2,1)} %bitcast.12), calls=%async_computation.3 | async-start | bytes 1179648 | tf_op jit(solution)/shard_map/all_to_all | solution.py:475
  112.9 4.8 %collective-permute-start.2 = (bf16[64,16,256]{2,1,0:T(8,128)(2,1)}, bf16[64,16,256]{2,1,0:T(8,128)(2,1)}, u32[]{:S(2)}, u32[]{:S(2)}) collective-permute-start(bf16[64,16,256]{2,1,0:T(8,128)(2,1)} %get-tuple-element.46), channel_id=1, source_target_pairs={{0,1},{1,2},{2,3},{4,5},{5,6},{6,7},{8,9},{9,10},{10,11},{12,13},{... | collective-permute-start | bytes 1572872 | tf_op jit(solution)/shard_map/ppermute | solution.py:422
  120.4 3.5 %all-to-all-start.4 = ((bf16[4,288,256]{2,1,0:T(8,128)(2,1)}), bf16[4,288,256]{2,1,0:T(8,128)(2,1)S(1)}, u32[]{:S(2)}, u32[]{:S(2)}) async-start(bf16[4,288,256]{2,1,0:T(8,128)(2,1)} %copy-done.14), calls=%async_computation.4 | async-start | bytes 1179648 | tf_op jit(solution)/shard_map/all_to_all | solution.py:475
  125.7 2.9 %collective-permute-done.3.down_ref = bf16[64,16,256]{2,1,0:T(8,128)(2,1)} collective-permute-done((bf16[64,16,256]{2,1,0:T(8,128)(2,1)}, bf16[64,16,256]{2,1,0:T(8,128)(2,1)}, u32[]{:S(2)}, u32[]{:S(2)}) %collective-permute-start.3) | collective-permute-done | bytes 524320 | tf_op jit(solution)/shard_map/ppermute | solution.py:423
  131.4 7.6 %outputs_conv.1 = (bf16[64,4,16,256]{3,2,1,0:T(8,128)(2,1)}, f32[8,128]{1,0:T(8,128)S(1)}) custom-call(bf16[4,64,16,256]{3,2,1,0:T(8,128)(2,1)S(1)} %copy-done.27, bf16[64,16,256]{2,1,0:T(8,128)(2,1)} %collective-permute-done.2.up_ref, bf16[64,16,256]{2,1,0:T(8,128)(2,1)} %collective-permute-done.3.down_ref, bf16[3,768,256]{2,1,0:T(8,128)(2,1)S(1)} %bitcast.33, ...), custom_call_target="tpu_custom_call" | custom-call | flops 4831838208 | bytes 8388608 | tf_op jit(solution)/shard_map/outputs_conv/pallas_call | solution.py:371
  140.5 3.5 %all-to-all-start.5 = ((bf16[4,288,256]{2,1,0:T(8,128)(2,1)}), bf16[4,288,256]{2,1,0:T(8,128)(2,1)S(1)}, u32[]{:S(2)}, u32[]{:S(2)}) async-start(bf16[4,288,256]{2,1,0:T(8,128)(2,1)} %get-tuple-element.68), calls=%async_computation.5 | async-start | bytes 1179648 | tf_op jit(solution)/shard_map/all_to_all | solution.py:475
  144.9 14.9 %all-to-all-done.5.refs_1_ = bf16[4,288,256]{2,1,0:T(8,128)(2,1)S(1)} async-done(((bf16[4,288,256]{2,1,0:T(8,128)(2,1)}), bf16[4,288,256]{2,1,0:T(8,128)(2,1)S(1)}, u32[]{:S(2)}, u32[]{:S(2)}) %all-to-all-start.5) | async-done | bytes 589856 | tf_op jit(solution)/shard_map/all_to_all | solution.py:475
  159.8 3.5 %all-to-all-start.7 = ((bf16[4,288,256]{2,1,0:T(8,128)(2,1)}), bf16[4,288,256]{2,1,0:T(8,128)(2,1)S(1)}, u32[]{:S(2)}, u32[]{:S(2)}) async-start(bf16[4,288,256]{2,1,0:T(8,128)(2,1)} %get-tuple-element.70), calls=%async_computation.7 | async-start | bytes 1179648 | tf_op jit(solution)/shard_map/all_to_all | solution.py:475
  164.2 6.9 %all-to-all-done.7 = bf16[4,288,256]{2,1,0:T(8,128)(2,1)S(1)} async-done(((bf16[4,288,256]{2,1,0:T(8,128)(2,1)}), bf16[4,288,256]{2,1,0:T(8,128)(2,1)S(1)}, u32[]{:S(2)}, u32[]{:S(2)}) %all-to-all-start.7) | async-done | bytes 589856 | tf_op jit(solution)/shard_map/all_to_all | solution.py:475
  171.1 3.7 %all-to-all-start.6 = ((bf16[4,288,256]{2,1,0:T(8,128)(2,1)}), bf16[4,288,256]{2,1,0:T(8,128)(2,1)S(1)}, u32[]{:S(2)}, u32[]{:S(2)}) async-start(bf16[4,288,256]{2,1,0:T(8,128)(2,1)} %get-tuple-element.69), calls=%async_computation.6 | async-start | bytes 1179648 | tf_op jit(solution)/shard_map/all_to_all | solution.py:475
  176.5 7.1 %all-to-all-done.6 = bf16[4,288,256]{2,1,0:T(8,128)(2,1)S(1)} async-done(((bf16[4,288,256]{2,1,0:T(8,128)(2,1)}), bf16[4,288,256]{2,1,0:T(8,128)(2,1)S(1)}, u32[]{:S(2)}, u32[]{:S(2)}) %all-to-all-start.6) | async-done | bytes 589856 | tf_op jit(solution)/shard_map/all_to_all | solution.py:475
  (80 shorter events, 53.4 us)
Async XLA Ops:
  3.8 7.8 %copy-start.11 = (bf16[3,3,256,256]{3,2,1,0:T(8,128)(2,1)S(1)}, bf16[3,3,256,256]{3,2,1,0:T(8,128)(2,1)}, u32[]{:S(2)}) copy-start(bf16[3,3,256,256]{3,2,1,0:T(8,128)(2,1)} %param.8) | copy-start | bytes 3538948
  5.2 16.6 %collective-permute-start = (bf16[2,64,16,256]{3,2,1,0:T(8,128)(2,1)}, bf16[2,64,16,256]{3,2,1,0:T(8,128)(2,1)S(1)}, u32[]{:S(2)}, u32[]{:S(2)}) collective-permute-start(bf16[2,64,16,256]{3,2,1,0:T(8,128)(2,1)} %get-tuple-element.37), channel_id=1, source_target_pairs={{0,1},{1,2},{2,3},{4,5},{5,6},{6,7},{8,9},{9,10},{10,11},{12,13},{... | collective-permute-start | bytes 3145736 | tf_op jit(solution)/shard_map/ppermute | solution.py:422
  9.7 16.3 %collective-permute-start.1 = (bf16[2,64,16,256]{3,2,1,0:T(8,128)(2,1)}, bf16[2,64,16,256]{3,2,1,0:T(8,128)(2,1)S(1)}, u32[]{:S(2)}, u32[]{:S(2)}) collective-permute-start(bf16[2,64,16,256]{3,2,1,0:T(8,128)(2,1)} %get-tuple-element.38), channel_id=1, source_target_pairs={{1,0},{2,1},{3,2},{5,4},{6,5},{7,6},{9,8},{10,9},{11,10},{13,12},{... | collective-permute-start | bytes 3145736 | tf_op jit(solution)/shard_map/ppermute | solution.py:423
  13.3 12.8 %copy-start.17 = (f32[64,256]{1,0:T(8,128)S(1)}, f32[64,256]{1,0:T(8,128)}, u32[]{:S(2)}) copy-start(f32[64,256]{1,0:T(8,128)} %decay_ref.5) | copy-start | bytes 196612
  29.0 2.0 %copy-start.21 = (f32[4,64,16,256]{3,2,1,0:T(8,128)}, f32[4,64,16,256]{3,2,1,0:T(8,128)S(1)}, u32[]{:S(2)}) copy-start(f32[4,64,16,256]{3,2,1,0:T(8,128)S(1)} %get-tuple-element.40.local_ref) | copy-start | bytes 12582916
  31.0 19.1 %all-to-all-start = ((bf16[8,80,256]{2,1,0:T(8,128)(2,1)}), bf16[8,80,256]{2,1,0:T(8,128)(2,1)S(1)}, u32[]{:S(2)}, u32[]{:S(2)}) async-start(bf16[8,80,256]{2,1,0:T(8,128)(2,1)} %copy-done.18), calls=%async_computation | async-start | bytes 655360 | tf_op jit(solution)/shard_map/all_to_all | solution.py:475
  51.7 2.2 %copy-start.22 = (f32[4,64,16,256]{3,2,1,0:T(8,128)S(1)}, f32[4,64,16,256]{3,2,1,0:T(8,128)}, u32[]{:S(2)}) copy-start(f32[4,64,16,256]{3,2,1,0:T(8,128)} %copy-done.21) | copy-start | bytes 12582916
  64.8 5.4 %collective-permute-start.4 = (bf16[1152,256]{1,0:T(8,128)(2,1)S(1)}, bf16[1152,256]{1,0:T(8,128)(2,1)S(1)}, u32[]{:S(2)}, u32[]{:S(2)}) collective-permute-start(bf16[1152,256]{1,0:T(8,128)(2,1)S(1)} %get-tuple-element.52), channel_id=1, source_target_pairs={{0,1},{1,0},{2,3},{3,2},{4,5},{5,4},{6,7},{7,6},{8,9},{9,8},{10,11... | collective-permute-start | bytes 1769480 | tf_op jit(solution)/shard_map/ppermute | solution.py:537
  64.8 14.0 %all-to-all-start.1 = ((bf16[8,80,256]{2,1,0:T(8,128)(2,1)}), bf16[8,80,256]{2,1,0:T(8,128)(2,1)}, u32[]{:S(2)}, u32[]{:S(2)}) async-start(bf16[8,80,256]{2,1,0:T(8,128)(2,1)} %get-tuple-element.48), calls=%async_computation.1 | async-start | bytes 655360 | tf_op jit(solution)/shard_map/all_to_all | solution.py:475
  80.4 2.2 %copy-start.20 = (f32[4,64,16,256]{3,2,1,0:T(8,128)S(1)}, f32[4,64,16,256]{3,2,1,0:T(8,128)}, u32[]{:S(2)}) copy-start(f32[4,64,16,256]{3,2,1,0:T(8,128)} %copy-done.19) | copy-start | bytes 12582916
  82.6 11.8 %copy-start.16 = (bf16[1152,256]{1,0:T(8,128)(2,1)S(1)}, bf16[1152,256]{1,0:T(8,128)(2,1)}, u32[]{:S(2)}) copy-start(bf16[1152,256]{1,0:T(8,128)(2,1)} %copy-done.15) | copy-start | bytes 1769476
  91.5 16.0 %collective-permute-start.5 = (bf16[1152,256]{1,0:T(8,128)(2,1)S(1)}, bf16[1152,256]{1,0:T(8,128)(2,1)S(1)}, u32[]{:S(2)}, u32[]{:S(2)}) collective-permute-start(bf16[1152,256]{1,0:T(8,128)(2,1)S(1)} %get-tuple-element.59), channel_id=1, source_target_pairs={{0,1},{1,0},{2,3},{3,2},{4,5},{5,4},{6,7},{7,6},{8,9},{9,8},{10,11... | collective-permute-start | bytes 1769480 | tf_op jit(solution)/shard_map/ppermute | solution.py:559
  107.5 21.1 %copy-start.6 = (bf16[1,64,4,16,256]{4,3,2,1,0:T(8,128)(2,1)S(1)}, bf16[1,64,4,16,256]{4,3,2,1,0:T(8,128)(2,1)}, u32[]{:S(2)}) copy-start(bf16[1,64,4,16,256]{4,3,2,1,0:T(8,128)(2,1)} %param.6) | copy-start | bytes 6291460
  107.5 21.1 %copy-start.25 = (f32[256]{0:T(256)S(1)}, f32[256]{0:T(256)}, u32[]{:S(2)}) copy-start(f32[256]{0:T(256)} %param.10) | copy-start | bytes 3076
  109.4 11.0 %all-to-all-start.3 = ((bf16[4,288,256]{2,1,0:T(8,128)(2,1)}), bf16[4,288,256]{2,1,0:T(8,128)(2,1)S(1)}, u32[]{:S(2)}, u32[]{:S(2)}) async-start(bf16[4,288,256]{2,1,0:T(8,128)(2,1)} %bitcast.12), calls=%async_computation.3 | async-start | bytes 1179648 | tf_op jit(solution)/shard_map/all_to_all | solution.py:475
  112.9 12.7 %collective-permute-start.2 = (bf16[64,16,256]{2,1,0:T(8,128)(2,1)}, bf16[64,16,256]{2,1,0:T(8,128)(2,1)}, u32[]{:S(2)}, u32[]{:S(2)}) collective-permute-start(bf16[64,16,256]{2,1,0:T(8,128)(2,1)} %get-tuple-element.46), channel_id=1, source_target_pairs={{0,1},{1,2},{2,3},{4,5},{5,6},{6,7},{8,9},{9,10},{10,11},{12,13},{... | collective-permute-start | bytes 1572872 | tf_op jit(solution)/shard_map/ppermute | solution.py:422
  117.7 10.8 %collective-permute-start.3 = (bf16[64,16,256]{2,1,0:T(8,128)(2,1)}, bf16[64,16,256]{2,1,0:T(8,128)(2,1)}, u32[]{:S(2)}, u32[]{:S(2)}) collective-permute-start(bf16[64,16,256]{2,1,0:T(8,128)(2,1)} %get-tuple-element.47), channel_id=1, source_target_pairs={{1,0},{2,1},{3,2},{5,4},{6,5},{7,6},{9,8},{10,9},{11,10},{13,12},{... | collective-permute-start | bytes 1572872 | tf_op jit(solution)/shard_map/ppermute | solution.py:423
  120.4 20.1 %all-to-all-start.4 = ((bf16[4,288,256]{2,1,0:T(8,128)(2,1)}), bf16[4,288,256]{2,1,0:T(8,128)(2,1)S(1)}, u32[]{:S(2)}, u32[]{:S(2)}) async-start(bf16[4,288,256]{2,1,0:T(8,128)(2,1)} %copy-done.14), calls=%async_computation.4 | async-start | bytes 1179648 | tf_op jit(solution)/shard_map/all_to_all | solution.py:475
  131.4 7.6 %copy-start.8 = (f32[1152,256]{1,0:T(8,128)S(1)}, f32[1152,256]{1,0:T(8,128)}, u32[]{:S(2)}) copy-start(f32[1152,256]{1,0:T(8,128)} %copy-done.7) | copy-start | bytes 3538948
  140.5 19.3 %all-to-all-start.5 = ((bf16[4,288,256]{2,1,0:T(8,128)(2,1)}), bf16[4,288,256]{2,1,0:T(8,128)(2,1)S(1)}, u32[]{:S(2)}, u32[]{:S(2)}) async-start(bf16[4,288,256]{2,1,0:T(8,128)(2,1)} %get-tuple-element.68), calls=%async_computation.5 | async-start | bytes 1179648 | tf_op jit(solution)/shard_map/all_to_all | solution.py:475
  159.8 11.3 %all-to-all-start.7 = ((bf16[4,288,256]{2,1,0:T(8,128)(2,1)}), bf16[4,288,256]{2,1,0:T(8,128)(2,1)S(1)}, u32[]{:S(2)}, u32[]{:S(2)}) async-start(bf16[4,288,256]{2,1,0:T(8,128)(2,1)} %get-tuple-element.70), calls=%async_computation.7 | async-start | bytes 1179648 | tf_op jit(solution)/shard_map/all_to_all | solution.py:475
  171.1 12.5 %all-to-all-start.6 = ((bf16[4,288,256]{2,1,0:T(8,128)(2,1)}), bf16[4,288,256]{2,1,0:T(8,128)(2,1)S(1)}, u32[]{:S(2)}, u32[]{:S(2)}) async-start(bf16[4,288,256]{2,1,0:T(8,128)(2,1)} %get-tuple-element.69), calls=%async_computation.6 | async-start | bytes 1179648 | tf_op jit(solution)/shard_map/all_to_all | solution.py:475
  174.9 10.4 %collective-permute-start.7 = (bf16[1152,256]{1,0:T(8,128)(2,1)S(1)}, bf16[1152,256]{1,0:T(8,128)(2,1)S(1)}, u32[]{:S(2)}, u32[]{:S(2)}) collective-permute-start(bf16[1152,256]{1,0:T(8,128)(2,1)S(1)} %bitcast.17), channel_id=1, source_target_pairs={{0,1},{1,0},{2,3},{3,2},{4,5},{5,4},{6,7},{7,6},{8,9},{9,8},{10,11... | collective-permute-start | bytes 1769480 | tf_op jit(solution)/shard_map/ppermute | solution.py:573
  183.6 3.7 %collective-permute-start.6 = (bf16[1152,256]{1,0:T(8,128)(2,1)S(1)}, bf16[1152,256]{1,0:T(8,128)(2,1)S(1)}, u32[]{:S(2)}, u32[]{:S(2)}) collective-permute-start(bf16[1152,256]{1,0:T(8,128)(2,1)S(1)} %bitcast.19), channel_id=1, source_target_pairs={{0,1},{1,0},{2,3},{3,2},{4,5},{5,4},{6,7},{7,6},{8,9},{9,8},{10,11... | collective-permute-start | bytes 1769480 | tf_op jit(solution)/shard_map/ppermute | solution.py:574
  (19 other events, 24.6 us)
where the time goes:
time: 191 us; the launch traced here: 189 us
  Pallas kernels  51.5 us (27%)
  starting transfers between devices  48 us (25%)
  waiting for transfers between devices  46.5 us (24%)
  local copies, waits for them, and re-layouts  30.9 us (16%)
  blocking collectives  11.6 us (6%)
    all_to_all x7, waiting for transfers between devices, exchange(): return lax.all_to_all(parts, axes, 0, 0)  34.1 us
    unnamed x56, local copies, waits for them, and re-layouts  30.9 us
    all_to_all x7, starting transfers between devices, exchange(): return lax.all_to_all(parts, axes, 0, 0)  28.6 us
    all_to_all x1, blocking collectives, exchange(): return lax.all_to_all(parts, axes, 0, 0)  11.6 us
    ppermute x2, starting transfers between devices, row_halo(): up = lax.ppermute(last, axes, [(i, i + 1) for i in range(count - 1)])  9.34 us
    pallas_call x1, Pallas kernels, kernel_grads(): pl.pallas_call(in_grad_kernel, grid=(frames // block,), in_specs=lead + [...  8.9 us
    pallas_call x1, Pallas kernels, kernel_grads(): pl.pallas_call(out_grad_kernel, grid=(frames // block,), in_specs=lead +...  8.63 us
    pallas_call x1, Pallas kernels, outputs_conv(): pl.pallas_call(outputs_kernel, grid=(frames // block,), in_specs=[pl.Bloc...  7.61 us
  transfers between devices with their start and end apart: 15, of which 9 were waited for; matrix products, arithmetic and copies ran while one was open for 0% of the time, Pallas kernels for 14%

commit v1 on v0

--- a/solution.py
+++ b/solution.py
@@ -117,7 +117,7 @@
     return part, taps
 
 
-def scan_kernel(backward, part_ref, up_ref, down_ref, w_ref, decay_ref, after_ref, local_ref, product_ref, end_ref, carry_ref, run_ref):
+def scan_kernel(backward, part_ref, up_ref, down_ref, w_ref, decay_ref, before_ref, local_ref, product_ref, end_ref, carry_ref, run_ref):
     rows, frames, width, p = part_ref.shape
     lines = rows * width
 
@@ -160,14 +160,14 @@
 
     @pl.when(pl.program_id(0) == pl.num_programs(0) - 1)
     def _():
-        high = run.astype(BF16).astype(F32)
-        products = [jnp.broadcast_to(high, (8, p)), jnp.broadcast_to(run - high, (8, p))]
-        message = jnp.concatenate(state + products, axis=0).astype(BF16)
-        for k in range(end_ref.shape[0]):
-            end_ref[k] = message
-
-
-def local_scan(part, up, down, half, taps, decays, block, backward, after):
+        if backward:
+            message = [before_ref[...]] + state + [jnp.broadcast_to(run, (8, p))]
+        else:
+            message = state
+        end_ref[...] = jnp.concatenate(message, axis=0)
+
+
+def local_scan(part, up, down, half, taps, decays, block, backward, before):
     rows, frames, width, p = part.shape
     c = up.shape[-1]
     blocks = frames // block
@@ -176,7 +176,7 @@
     part_spec = pl.BlockSpec((rows, block, width, p), lambda b: (0, at(b), 0, 0))
     frame_spec = pl.BlockSpec((block, p), lambda b: (at(b), 0))
     lines = rows * width
-    count = lax.axis_size("a") * lax.axis_size("x")
+    message = 2 * lines + 8 if backward else lines
     return pl.pallas_call(
         functools.partial(scan_kernel, backward),
         grid=(blocks,),
@@ -186,42 +186,57 @@
             halo_spec,
             pl.BlockSpec(taps.shape, lambda b: (0, 0, 0)),
             frame_spec,
-            ANYWHERE,
+            pl.BlockSpec(before.shape, lambda b: (0, 0)),
         ],
-        out_specs=[
-            part_spec,
-            frame_spec,
-            pl.BlockSpec((count, lines + 16, p), lambda b: (0, 0, 0)),
-        ],
+        out_specs=[part_spec, frame_spec, pl.BlockSpec((message, p), lambda b: (0, 0))],
         out_shape=[
             jax.ShapeDtypeStruct(part.shape, F32),
             jax.ShapeDtypeStruct((frames, p), F32),
-            jax.ShapeDtypeStruct((count, lines + 16, p), BF16),
+            jax.ShapeDtypeStruct((message, p), F32),
         ],
         scratch_shapes=[pltpu.VMEM((lines, p), F32), pltpu.VMEM((8, p), F32)],
         compiler_params=params(),
         cost_estimate=cost(4 * frames * width * 3 * c * p, 12 * 2**20),
         name="scan_back" if backward else "scan_fwd",
-    )(part, up, down, taps, decays, after)
-
-
-def combine(place_ref, ends_ref, total_ref, backward):
-    place = place_ref[0]
+    )(part, up, down, taps, decays, before)
+
+
+def pair_kernel(places_ref, own_ref, got_ref, out_ref):
+    deep, height, _ = out_ref.shape
+    lines = height - 8
+    first = places_ref[1] == 0
+    own_end, got_end = own_ref[0:lines], got_ref[0:lines]
+    own_start, got_start = own_ref[lines : 2 * lines], got_ref[lines : 2 * lines]
+    own_product, got_product = own_ref[2 * lines :], got_ref[2 * lines :]
+    end = jnp.where(
+        first, got_product[0:1] * own_end + got_end, own_product[0:1] * got_end + own_end
+    )
+    start = jnp.where(
+        first, own_product[0:1] * got_start + own_start, got_product[0:1] * own_start + got_start
+    )
+    product = own_product * got_product
+    for k in range(deep):
+        out_ref[k, 0:lines] = jnp.where(k > places_ref[0], end, start)
+        out_ref[k, lines:] = product
+
+
+def combine(places_ref, ends_ref, pair_ref, total_ref, backward):
+    place = places_ref[0]
     count = ends_ref.shape[0]
     lines = total_ref.shape[0]
     total = jnp.zeros(total_ref.shape, F32)
     order = range(count - 1, -1, -1) if backward else range(count)
     for k in order:
-        block = ends_ref[k].astype(F32)
-        product = block[lines : lines + 1] + block[lines + 8 : lines + 9]
-        passed = product * total + block[0:lines]
+        passed = ends_ref[k, lines : lines + 1] * total + ends_ref[k, 0:lines]
         total = jnp.where(k > place if backward else k < place, passed, total)
-    total_ref[...] = total
+    near = pair_ref[lines : 2 * lines] if backward else pair_ref[0:lines]
+    passed = pair_ref[2 * lines : 2 * lines + 1] * total + near
+    total_ref[...] = jnp.where(places_ref[1] == (0 if backward else 1), passed, total)
 
 
 def split_halves(place_ref, sum_ref, sent_ref, kept_ref):
     half = kept_ref.shape[0]
-    side = place_ref[1]
+    side = place_ref[2]
     sent_ref[...] = sum_ref[pl.ds(pl.multiple_of((1 - side) * half, 8), half)].astype(BF16)
     kept_ref[...] = sum_ref[pl.ds(pl.multiple_of(side * half, 8), half)]
 
@@ -234,13 +249,13 @@
     s_ref[rows + 1] = shifted(flat(down_ref[...]), width)
 
 
-def out_grad_kernel(place_ref, ends_ref, local_ref, product_ref, cot_ref, up_ref, down_ref, after_ref, low_ref, first_ref, last_ref, sent_ref, kept_ref, token_ref, s_ref, total_ref, sum_ref):
+def out_grad_kernel(place_ref, ends_ref, pair_ref, local_ref, product_ref, cot_ref, up_ref, down_ref, low_ref, first_ref, last_ref, sent_ref, kept_ref, token_ref, s_ref, total_ref, sum_ref):
     rows, frames, width, p = local_ref.shape
     c = cot_ref.shape[-1]
 
     @pl.when(pl.program_id(0) == 0)
     def _():
-        combine(place_ref, ends_ref, total_ref, False)
+        combine(place_ref, ends_ref, pair_ref, total_ref, False)
         sum_ref[...] = jnp.zeros_like(sum_ref)
         token_ref[...] = jnp.zeros_like(token_ref)
 
@@ -268,13 +283,14 @@
         split_halves(place_ref, sum_ref, sent_ref, kept_ref)
 
 
-def in_grad_kernel(place_ref, ends_ref, local_ref, product_ref, decay_ref, x_ref, up_ref, down_ref, after_ref, sent_ref, kept_ref, token_ref, s_ref, total_ref, sum_ref, flat_ref):
+def in_grad_kernel(place_ref, ends_ref, pair_ref, local_ref, product_ref, decay_ref, x_ref, up_ref, down_ref, *refs):
+    sent_ref, kept_ref, token_ref, s_ref, total_ref, sum_ref, flat_ref = refs[-7:]
     rows, frames, width, p = local_ref.shape
     c = x_ref.shape[-1]
 
     @pl.when(pl.program_id(0) == 0)
     def _():
-        combine(place_ref, ends_ref, total_ref, True)
+        combine(place_ref, ends_ref, pair_ref, total_ref, True)
         sum_ref[...] = jnp.zeros_like(sum_ref)
         token_ref[...] = jnp.zeros_like(token_ref)
 
@@ -299,14 +315,20 @@
         split_halves(place_ref, flat_ref, sent_ref, kept_ref)
 
 
-def kernel_grads(places, ends, local, product, x, up, down, half, decays, block, after):
+def kernel_grads(places, ends, pair, local, product, x, up, down, half, decays, block, after=None):
     rows, frames, width, p = local.shape
     c = x.shape[-1]
     halo_spec = pl.BlockSpec((None, block, width, c), lambda b: (half, b, 0, 0))
     local_spec = pl.BlockSpec((rows, block, width, p), lambda b: (0, b, 0, 0))
     frame_spec = pl.BlockSpec((block, p), lambda b: (b, 0))
     x_spec = pl.BlockSpec((block, rows, width, c), lambda b: (b, 0, 0, 0))
-    lead = [SCALARS, pl.BlockSpec(ends.shape, lambda b: (0, 0, 0)), local_spec, frame_spec]
+    lead = [
+        SCALARS,
+        pl.BlockSpec(ends.shape, lambda b: (0, 0, 0)),
+        pl.BlockSpec(pair.shape, lambda b: (0, 0)),
+        local_spec,
+        frame_spec,
+    ]
     tail = [x_spec, halo_spec, halo_spec]
     scratch = [
         pltpu.VMEM((rows + 2, block * width, 3 * c), BF16),
@@ -327,18 +349,18 @@
         return pl.pallas_call(
             out_grad_kernel,
             grid=(frames // block,),
-            in_specs=lead + tail + [ANYWHERE],
+            in_specs=lead + tail,
             out_specs=[local_spec, line_spec, line_spec] + grad_specs,
             out_shape=[jax.ShapeDtypeStruct(local.shape, BF16), line, line] + grad_shapes,
             scratch_shapes=scratch + [pltpu.VMEM((2 * lines, columns), F32)],
             compiler_params=params(),
             cost_estimate=estimate,
             name="out_grad",
-        )(places, ends, local, product, x, up, down, after)
+        )(places, ends, pair, local, product, x, up, down)
     return pl.pallas_call(
         in_grad_kernel,
         grid=(frames // block,),
-        in_specs=lead + [frame_spec] + tail + [ANYWHERE],
+        in_specs=lead + [frame_spec] + tail + [ANYWHERE] * len(after),
         out_specs=grad_specs,
         out_shape=grad_shapes,
         scratch_shapes=scratch
@@ -346,7 +368,7 @@
         compiler_params=params(),
         cost_estimate=estimate,
         name="in_grad",
-    )(places, ends, local, product, decays, x, up, down, after)
+    )(places, ends, pair, local, product, decays, x, up, down, *after)
 
 
 def outputs_kernel(low_ref, up_ref, down_ref, w_ref, x_ref, skip_ref, after_ref, out_ref, token_ref, s_ref):
@@ -389,7 +411,7 @@
     )(low, up, down, taps, x, skip, after)
 
 
-def edge_rows_kernel(x_ref, cot_ref, first_ref, last_ref, sems):
+def edge_rows_kernel(places_ref, x_ref, cot_ref, first_ref, last_ref, sems):
     rows = x_ref.shape[1]
     copies = []
     for k, ref in enumerate((x_ref, cot_ref)):
@@ -401,19 +423,19 @@
         copy.wait()
 
 
-def edge_rows(x, cot):
+def edge_rows(places, x, cot):
     frames, rows, width, c = x.shape
     line = jax.ShapeDtypeStruct((2, frames, width, c), x.dtype)
     return pl.pallas_call(
         edge_rows_kernel,
-        in_specs=[pl.BlockSpec(memory_space=pltpu.HBM)] * 2,
+        in_specs=[SCALARS, ANYWHERE, ANYWHERE],
         out_specs=[ANYWHERE, ANYWHERE],
         out_shape=[line, line],
         scratch_shapes=[pltpu.SemaphoreType.DMA((2, 2))],
-        compiler_params=pltpu.CompilerParams(vmem_limit_bytes=2**20),
+        compiler_params=pltpu.CompilerParams(vmem_limit_bytes=56 * 2**20),
         cost_estimate=cost(0, 2**22),
         name="edge_rows",
-    )(x, cot)
+    )(places, x, cot)
 
 
 def row_halo(first, last):
@@ -425,86 +447,75 @@
 
 
 CORES = [(0, 1), (1, 0)]
-
-
-def small_call(body, name, out_shapes, operands, after, places=None):
+FAR = 64
+
+
+def small_call(body, name, out_shapes, operands, after, places=None, mib=2):
     extra = [] if places is None else [places]
 
     def kernel(*refs):
-        body(*refs[1 : len(extra) + len(operands) + 1], *refs[len(extra) + len(operands) + 1 : -1])
+        body(*refs[len(after) : -1])
         refs[-1][...] = jnp.zeros_like(refs[-1])
 
     whole = pl.BlockSpec(memory_space=pltpu.VMEM)
     return pl.pallas_call(
         kernel,
-        in_specs=[ANYWHERE] + [SCALARS] * len(extra) + [whole] * len(operands),
+        in_specs=[ANYWHERE] * len(after) + [SCALARS] * len(extra) + [whole] * len(operands),
         out_specs=[whole] * (len(out_shapes) + 1),
         out_shape=[jax.ShapeDtypeStruct(*shape) for shape in out_shapes] + [TOKEN],
-        compiler_params=pltpu.CompilerParams(vmem_limit_bytes=8 * 2**20),
-        cost_estimate=cost(0, 2**21),
+        compiler_params=pltpu.CompilerParams(vmem_limit_bytes=10 * 2**20),
+        cost_estimate=cost(mib * 2**29, 2**21),
         name=name,
-    )(after, *extra, *operands)
-
-
-def add_kernel(kept_ref, got_ref, sent_ref, sum_ref):
-    total = kept_ref[...] + got_ref[...].astype(F32)
-    sum_ref[...] = total
-    sent_ref[...] = total.astype(BF16)
-
-
-def share_kernel(places_ref, kept_ref, parts_ref, out_ref):
-    own = places_ref[2]
-    total = kept_ref[own]
-    for k in range(parts_ref.shape[0]):
-        total = total + jnp.where(k == own, 0.0, parts_ref[k].astype(F32))
-    total = total.astype(BF16)
-    for k in range(out_ref.shape[0]):
-        out_ref[k] = total
-
-
-def total_kernel(scale, parts_ref, out_ref):
-    total = parts_ref[0].astype(F32)
-    for k in range(1, parts_ref.shape[0]):
-        total = total + parts_ref[k].astype(F32)
-    total = (total * scale).astype(BF16)
-    for k in range(out_ref.shape[0]):
-        out_ref[k] = total
-
-
-def exchange(parts, axes):
-    return lax.all_to_all(parts, axes, 0, 0)
-
-
-def pieces(array, count):
-    return array.reshape(count, array.shape[0] // count, array.shape[1])
+    )(*after, *extra, *operands)
+
+
+def quarter(index, ref):
+    size = ref.shape[0] // 4
+    return pl.ds(pl.multiple_of(index * size, 16), size)
+
+
+def add_kernel(places_ref, kept_ref, got_ref, own_ref, *sent_refs):
+    for k, ref in enumerate((own_ref,) + sent_refs):
+        at = quarter(jnp.bitwise_xor(places_ref[3], k), kept_ref)
+        ref[...] = (kept_ref[at] + got_ref[at].astype(F32)).astype(ref.dtype)
+
+
+def tree(terms):
+    while len(terms) > 1:
+        terms = [terms[k] + terms[k + 1] for k in range(0, len(terms), 2)]
+    return terms[0]
+
+
+def sum_kernel(scale, *refs):
+    total = tree([ref[...].astype(F32) for ref in refs[:-1]])
+    if scale is not None:
+        total = total * scale
+    refs[-1][...] = total.astype(BF16)
+
+
+def pack_kernel(*refs):
+    for k, ref in enumerate(refs[:-1]):
+        refs[-1][k] = ref[...]
 
 
 def merge_kernel(places_ref, own_ref, other_ref, out_ref):
-    @pl.when(pl.program_id(0) == 0)
-    def _():
-        out_ref[...] = own_ref[...].astype(F32)
-
-    @pl.when(pl.program_id(0) == 1)
-    def _():
-        out_ref[...] = other_ref[...].astype(F32)
-
-
-def merged(own, other, places):
-    half, c = own.shape
-    part_spec = pl.BlockSpec((half, c), lambda g, places: (0, 0))
-    return pl.pallas_call(
-        merge_kernel,
-        grid_spec=pltpu.PrefetchScalarGridSpec(
-            num_scalar_prefetch=1,
-            grid=(2,),
-            in_specs=[part_spec, part_spec],
-            out_specs=pl.BlockSpec((half, c), lambda g, places: (jnp.bitwise_xor(g, places[1]), 0)),
-        ),
-        out_shape=jax.ShapeDtypeStruct((2 * half, c), F32),
-        compiler_params=params(12),
-        cost_estimate=cost(0, 10 * half * c),
-        name="merge",
-    )(places, own, other)
+    count, lines, _ = own_ref.shape
+    for side, ref in enumerate((own_ref, other_ref)):
+        for k in range(count):
+            index = jnp.bitwise_xor(places_ref[2], side) * count
+            index = index + jnp.bitwise_xor(places_ref[3], k)
+            at = pl.ds(pl.multiple_of(index * lines, 16), lines)
+            out_ref[at] = ref[k].astype(F32)
+
+
+def from_others(sent, axes):
+    count = math.prod(lax.axis_size(name) for name in axes)
+    if not isinstance(sent, list):
+        sent = [sent] * (count - 1)
+    return [
+        lax.ppermute(part, axes, [(i, i ^ k) for i in range(count)])
+        for k, part in enumerate(sent, 1)
+    ]
 
 
 def per_device(inputs, decays, in_kernel, out_kernel, skip, cotangent):
@@ -515,65 +526,84 @@
     grad_scale = 1.0 / math.sqrt(clips * frames * rows * width * devices)
     x = inputs.reshape(frames, rows, width, c)
     cot = cotangent.reshape(frames, rows, width, c)
-    places = jnp.stack(
-        [lax.axis_index(("a", "x")), lax.axis_index("core"), lax.axis_index(("x", "y"))]
-    ).astype(jnp.int32)
-    four = lax.axis_size("x") * lax.axis_size("y")
+    places = jnp.stack([lax.axis_index(name) for name in ("a", "x", "core", ("x", "y"))])
+    places = places.astype(jnp.int32)
     deep = lax.axis_size("a")
-
-    up, down = row_halo(*edge_rows(x, cot))
+    lines = rows * width
+
+    up, down = row_halo(*edge_rows(places, x, cot))
     x_part, x_taps = interior_conv(x, in_kernel, False, block)
     cot_part, cot_taps = interior_conv(cot, out_kernel, True, block)
-    states, running, ends = local_scan(x_part, up, down, 0, x_taps, decays, block, False, decays)
-    ends_all = exchange(ends, ("a", "x"))
-    adjoint, trailing, starts = local_scan(
-        cot_part, up, down, 1, cot_taps, decays, block, True, running
-    )
-    starts_all = exchange(starts, ("a", "x"))
+    states, running, end = local_scan(x_part, up, down, 0, x_taps, decays, block, False, decays)
+    adjoint, trailing, message = local_scan(
+        cot_part, up, down, 1, cot_taps, decays, block, True, end
+    )
+    pair = lax.ppermute(message, "x", [(0, 1), (1, 0)])
+    ends, token = small_call(
+        pair_kernel, "pair", [((deep, lines + 8, p), F32)], [message, pair], [], places
+    )
+    ends = lax.all_to_all(ends, "a", 0, 0)
 
     low, low_first, low_last, sent, kept, token = kernel_grads(
-        places, ends_all, states, running, cot, up, down, 1, None, block, trailing
+        places, ends, pair, states, running, cot, up, down, 1, None, block
     )
     got = lax.ppermute(sent, "core", CORES)
     low_up, low_down = row_halo(low_first, low_last)
-
-    def add(name, kept, got, token):
+    half, q = kept.shape
+    part_shape = (half // 4, q)
+
+    def add(name, kept, got, after):
+        shapes = [(part_shape, F32)] + [(part_shape, BF16)] * 3
+        own, *sent, token = small_call(add_kernel, name, shapes, [kept, got], after, places)
+        return own, from_others(sent, ("x", "y")), token
+
+    def sums(name, scale, terms, after, mib=2):
+        body = functools.partial(sum_kernel, scale)
+        return small_call(body, name, [(part_shape, BF16)], terms, after, None, mib)
+
+    def swapped(part, bit):
+        return lax.ppermute(part, "a", [(i, i ^ bit) for i in range(deep)])
+
+    bits = [2**k for k in range(deep.bit_length() - 1)]
+
+    def middle(name, part, other, after):
+        for bit in bits[1:]:
+            part, token = sums(name, None, [part, other], after)
+            other, after = swapped(part, bit), [token]
+        return part, other, after[0]
+
+    def pack(name, terms, after):
+        packed, token = small_call(pack_kernel, name, [((4,) + part_shape, BF16)], terms, after)
+        return packed, lax.ppermute(packed, "core", CORES), token
+
+    def merge(name, packed, other, after):
         return small_call(
-            add_kernel, name, [(kept.shape, BF16), (kept.shape, F32)], [kept, got], token
+            merge_kernel, name, [((2 * half, q), F32)], [packed, other], after, places
         )
 
-    def share(name, kept, parts, token):
-        shape = (deep,) + parts.shape[1:]
-        kept = pieces(kept, four)
-        return small_call(share_kernel, name, [(shape, BF16)], [kept, parts], token, places)
-
-    def total(name, parts, token):
-        body = functools.partial(total_kernel, grad_scale)
-        return small_call(body, name, [((four,) + parts.shape[1:], BF16)], [parts], token)
-
-    sent, out_kept, out_token = add("out_add", kept, got, token)
-    out_parts = exchange(pieces(sent, four), ("x", "y"))
+    own, others, token = add("out_add", kept, got, [token])
     sent, kept, token = kernel_grads(
-        places, starts_all, adjoint, trailing, x, up, down, 0, decays, block, out_token
+        places, ends, pair, adjoint, trailing, x, up, down, 0, decays, block, [token, low_up, low_down]
     )
     got = lax.ppermute(sent, "core", CORES)
-    out_parts, token = share("out_share", out_kept, out_parts, token)
-    out_parts = exchange(out_parts, ("a",))
-    sent, in_kept, token = add("in_add", kept, got, token)
-    in_parts = exchange(pieces(sent, four), ("x", "y"))
+    out_part, token = sums("out_share", None, [own] + others, [token], mib=FAR)
+    out_other = swapped(out_part, 1)
+    own, others, token = add("in_add", kept, got, [token])
+    out_part, out_other, token = middle("out_mid", out_part, out_other, [token])
     outputs, token = outputs_conv(
         low, low_up, low_down, out_kernel.reshape(3, 3 * p, c), x, skip.reshape(1, c), block, token
     )
-    in_parts, token = share("in_share", in_kept, in_parts, token)
-    in_parts = exchange(in_parts, ("a",))
-    out_parts, token = total("out_total", out_parts, token)
-    out_half = flat(exchange(out_parts, ("x", "y")))
-    in_parts, token = total("in_total", in_parts, token)
-    in_half = flat(exchange(in_parts, ("x", "y")))
-    out_other = lax.ppermute(out_half, "core", CORES)
-    in_other = lax.ppermute(in_half, "core", CORES)
-    out_grad = merged(out_half, out_other, places)
-    in_grad = merged(in_half, in_other, places)
+    in_part, token = sums("in_share", None, [own] + others, [token])
+    in_other = swapped(in_part, 1)
+    out_part, token = sums("out_total", grad_scale, [out_part, out_other], [token])
+    out_others = from_others(out_part, ("x", "y"))
+    in_part, in_other, token = middle("in_mid", in_part, in_other, [token])
+    out_packed, out_other, token = pack("out_pack", [out_part] + out_others, [token])
+    in_part, token = sums("in_total", grad_scale, [in_part, in_other], [token])
+    in_others = from_others(in_part, ("x", "y"))
+    out_grad, token = merge("out_merge", out_packed, out_other, [token])
+    in_packed, in_other, token = pack("in_pack", [in_part] + in_others, [token])
+    in_grad, _ = merge("in_merge", in_packed, in_other, [token])
     return (
         outputs.reshape(inputs.shape),
         in_grad.reshape(in_kernel.shape),

time: 191 us -> 196 us (1.026)
  Pallas kernels: 51.5 us -> 111 us
  local copies, waits for them, and re-layouts: 30.9 us -> 0.04 us
  starting transfers between devices: 48 us -> 33.5 us
  waiting for transfers between devices: 46.5 us -> 38.2 us
    pallas_call x9 -> x14, Pallas kernels: 10.5 us -> 72.6 us  [the longest x1 65.5 us: edge_rows(): pl.pallas_call(edge_rows_kernel, in_specs=[SCALARS, ANYWHERE, ANYWHERE],...]
    all_to_all x7 -> x0, waiting for transfers between devices: 34.1 us -> none  [exchange(): return lax.all_to_all(parts, axes, 0, 0)]
    unnamed x56 -> x14, local copies, waits for them, and re-layouts: 30.9 us -> 0.04 us
    all_to_all x7 -> x0, starting transfers between devices: 28.6 us -> none  [exchange(): return lax.all_to_all(parts, axes, 0, 0)]
    ppermute x2 -> x19, waiting for transfers between devices: 0.01 us -> 23.4 us  [the longest x4 10.8 us: swapped(): return lax.ppermute(part, 'a', [(i, i ^ bit) for i in range(deep)])]
    ppermute x2 -> x19, starting transfers between devices: 3.3 us -> 20.4 us  [the longest x12 10.8 us: from_others(): lax.ppermute(part, axes, [(i, i ^ k) for i in range(count)])]
    ppermute x2, waiting for transfers between devices: 7.17 us -> 12.5 us  [row_halo(): down = lax.ppermute(first, axes, [(i + 1, i) for i in range(count - 1)])]
    ppermute x2, waiting for transfers between devices: 5.22 us -> 0.95 us  [row_halo(): up = lax.ppermute(last, axes, [(i, i + 1) for i in range(count - 1)])]
  transfers between devices with their start and end apart: 15 -> 25, of which waited for: 9 -> 15; matrix products, arithmetic and copies ran while one was open for 0% -> 0% of each run, Pallas kernels for 14% -> 15%
where the time goes in v1:
time: 196 us; the launch traced here: 195 us
  Pallas kernels  111 us (57%)
  waiting for transfers between devices  38.2 us (19%)
  starting transfers between devices  33.5 us (17%)
  blocking collectives  11 us (6%)
    pallas_call x1, Pallas kernels, edge_rows(): pl.pallas_call(edge_rows_kernel, in_specs=[SCALARS, ANYWHERE, ANYWHERE],...  65.5 us
    ppermute x2, waiting for transfers between devices, row_halo(): down = lax.ppermute(first, axes, [(i + 1, i) for i in range(count - 1)])  12.5 us
    all_to_all x1, blocking collectives, per_device(): ends = lax.all_to_all(ends, 'a', 0, 0)  11 us
    ppermute x4, waiting for transfers between devices, swapped(): return lax.ppermute(part, 'a', [(i, i ^ bit) for i in range(deep)])  10.8 us
    ppermute x12, starting transfers between devices, from_others(): lax.ppermute(part, axes, [(i, i ^ k) for i in range(count)])  10.8 us
    ppermute x2, starting transfers between devices, row_halo(): up = lax.ppermute(last, axes, [(i, i + 1) for i in range(count - 1)])  8.95 us
    pallas_call x1, Pallas kernels, kernel_grads(): pl.pallas_call(in_grad_kernel, grid=(frames // block,), in_specs=lead + [...  8.4 us
    ppermute x12, waiting for transfers between devices, from_others(): lax.ppermute(part, axes, [(i, i ^ k) for i in range(count)])  8.24 us
  transfers between devices with their start and end apart: 25, of which 15 were waited for; matrix products, arithmetic and copies ran while one was open for 0% of the time, Pallas kernels for 15%

profile of v1, /device:TPU:1, one launch (start us, length us, event | category | flops | bytes accessed | tf_op | source)
XLA Modules:
  0.0 195.1 jit_solution(13378367195924939687)
XLA Ops:
  1.3 65.5 %edge_rows.1 = (bf16[2,64,16,256]{3,2,1,0:T(8,128)(2,1)}, bf16[2,64,16,256]{3,2,1,0:T(8,128)(2,1)}) custom-call(s32[4]{0:T(128)} %pad_add_fusion.places_ref.refs_0_.place_ref.refs_1_, bf16[64,4,16,256]{3,2,1,0:T(8,128)(2,1)} %bitcast.15, bf16[64,4,16,256]{3,2,1,0:T(8,128)(2,1)} %bitcast.12), custom_call_target="tpu_custom_call" | custom-call | bytes 4194304 | tf_op jit(solution)/shard_map/edge_rows/pallas_call | solution.py:429
  66.8 4.5 %collective-permute-start = (bf16[2,64,16,256]{3,2,1,0:T(8,128)(2,1)}, bf16[2,64,16,256]{3,2,1,0:T(8,128)(2,1)S(1)}, u32[]{:S(2)}, u32[]{:S(2)}) collective-permute-start(bf16[2,64,16,256]{3,2,1,0:T(8,128)(2,1)} %get-tuple-element.55), channel_id=1, source_target_pairs={{0,1},{1,2},{2,3},{4,5},{5,6},{6,7},{8,9},{9,10},{10,11},{12,13},{... | collective-permute-start | bytes 3145736 | tf_op jit(solution)/shard_map/ppermute | solution.py:444
  71.3 1.9 collective-permute-start.1
  73.3 5.1 %interior_in.1.part_ref = f32[4,64,16,256]{3,2,1,0:T(8,128)S(1)} custom-call(bf16[64,4,16,256]{3,2,1,0:T(8,128)(2,1)S(1)} %bitcast.16, bf16[3,768,256]{2,1,0:T(8,128)(2,1)S(1)} %bitcast.19), custom_call_target="tpu_custom_call" | custom-call | flops 4831838208 | bytes 8388608 | tf_op jit(solution)/shard_map/interior_in/pallas_call | solution.py:106
  78.4 5.5 %interior_cot.1 = (f32[4,64,16,256]{3,2,1,0:T(8,128)S(1)}, bf16[3,768,256]{2,1,0:T(8,128)(2,1)S(1)}) custom-call(bf16[64,4,16,256]{3,2,1,0:T(8,128)(2,1)S(1)} %bitcast.13, bf16[3,3,256,256]{3,2,1,0:T(8,128)(2,1)S(1)} %copy-done.5), custom_call_target="tpu_custom_call" | custom-call | flops 4831838208 | bytes 8388608 | tf_op jit(solution)/shard_map/interior_cot/pallas_call | solution.py:91
  83.9 3.8 %collective-permute-done.1.down_ref = bf16[2,64,16,256]{3,2,1,0:T(8,128)(2,1)S(1)} collective-permute-done((bf16[2,64,16,256]{3,2,1,0:T(8,128)(2,1)}, bf16[2,64,16,256]{3,2,1,0:T(8,128)(2,1)S(1)}, u32[]{:S(2)}, u32[]{:S(2)}) %collective-permute-start.1) | collective-permute-done | bytes 1048608 | tf_op jit(solution)/shard_map/ppermute | solution.py:445
  87.6 2.3 %scan_fwd.1 = (f32[4,64,16,256]{3,2,1,0:T(8,128)S(1)}, f32[64,256]{1,0:T(8,128)S(1)}, f32[64,256]{1,0:T(8,128)S(1)}) custom-call(f32[4,64,16,256]{3,2,1,0:T(8,128)S(1)} %interior_in.1.part_ref, bf16[2,64,16,256]{3,2,1,0:T(8,128)(2,1)S(1)} %collective-permute-done.up_ref, bf16[2,64,16,256]{3,2,1,0:T(8,128)(2,1)S(1)} %collective-permute-done.1.down_ref, ...), custom_call_target="tpu_custom_call" | custom-call | flops 805306368 | bytes 12582912 | tf_op jit(solution)/shard_map/scan_fwd/pallas_call | solution.py:180
  89.9 2.6 %scan_back.1 = (f32[4,64,16,256]{3,2,1,0:T(8,128)S(1)}, f32[64,256]{1,0:T(8,128)S(1)}, f32[136,256]{1,0:T(8,128)S(1)}) custom-call(f32[4,64,16,256]{3,2,1,0:T(8,128)S(1)} %get-tuple-element.54.part_ref, bf16[2,64,16,256]{3,2,1,0:T(8,128)(2,1)S(1)} %collective-permute-done.up_ref, bf16[2,64,16,256]{3,2,1,0:T(8,128)(2,1)S(1)} %collective-permute-done.1.down_ref, ...), custom_call_target="tpu_custom_call" | custom-call | flops 805306368 | bytes 12582912 | tf_op jit(solution)/shard_map/scan_back/pallas_call | solution.py:180
  93.7 2.7 %collective-permute-done.2.refs_2_.pair_ref = f32[136,256]{1,0:T(8,128)S(1)} collective-permute-done((f32[136,256]{1,0:T(8,128)S(1)}, f32[136,256]{1,0:T(8,128)S(1)}, u32[]{:S(2)}, u32[]{:S(2)}) %collective-permute-start.2) | collective-permute-done | bytes 139296 | tf_op jit(solution)/shard_map/ppermute | solution.py:541
  97.6 11.0 %all_to_all.5.ends_ref = f32[4,72,256]{2,1,0:T(8,128)S(1)} all-to-all(f32[4,72,256]{2,1,0:T(8,128)S(1)} %get-tuple-element.60), channel_id=1, replica_groups=mesh['a'=4,'x'=2,'y'=2,'core'=2] {'a'}, dimensions={0} | all-to-all | bytes 589824 | tf_op jit(solution)/shard_map/all_to_all | solution.py:545
  108.6 7.9 %out_grad.1 = (bf16[4,64,16,256]{3,2,1,0:T(8,128)(2,1)S(1)}, bf16[64,16,256]{2,1,0:T(8,128)(2,1)S(1)}, bf16[64,16,256]{2,1,0:T(8,128)(2,1)S(1)}, bf16[1152,256]{...) custom-call(s32[4]{0:T(128)S(1)} %copy-done.4, f32[4,72,256]{2,1,0:T(8,128)S(1)} %all_to_all.5.ends_ref, ...), custom_call_target="tpu_custom_call" | custom-call | flops 4831838208 | bytes 10485760 | tf_op jit(solution)/shard_map/out_grad/pallas_call | solution.py:349
  116.5 4.4 %collective-permute-start.3 = (bf16[64,16,256]{2,1,0:T(8,128)(2,1)S(1)}, bf16[64,16,256]{2,1,0:T(8,128)(2,1)S(1)}, u32[]{:S(2)}, u32[]{:S(2)}) collective-permute-start(bf16[64,16,256]{2,1,0:T(8,128)(2,1)S(1)} %get-tuple-element.64), channel_id=1, source_target_pairs={{0,1},{1,2},{2,3},{4,5},{5,6},{6,7},{8,9},{9,10},{10,11},{12,13},{... | collective-permute-start | bytes 1572872 | tf_op jit(solution)/shard_map/ppermute | solution.py:444
  120.9 2.1 %collective-permute-start.4 = (bf16[64,16,256]{2,1,0:T(8,128)(2,1)S(1)}, bf16[64,16,256]{2,1,0:T(8,128)(2,1)S(1)}, u32[]{:S(2)}, u32[]{:S(2)}) collective-permute-start(bf16[64,16,256]{2,1,0:T(8,128)(2,1)S(1)} %get-tuple-element.65), channel_id=1, source_target_pairs={{1,0},{2,1},{3,2},{5,4},{6,5},{7,6},{9,8},{10,9},{11,10},{13,12},{... | collective-permute-start | bytes 1572872 | tf_op jit(solution)/shard_map/ppermute | solution.py:445
  127.4 8.8 %collective-permute-done.4.refs_2_.down_ref = bf16[64,16,256]{2,1,0:T(8,128)(2,1)S(1)} collective-permute-done((bf16[64,16,256]{2,1,0:T(8,128)(2,1)S(1)}, bf16[64,16,256]{2,1,0:T(8,128)(2,1)S(1)}, u32[]{:S(2)}, u32[]{:S(2)}) %collective-permute-start.4) | collective-permute-done | bytes 524320 | tf_op jit(solution)/shard_map/ppermute | solution.py:445
  136.2 8.4 %in_grad.1 = (bf16[1152,256]{1,0:T(8,128)(2,1)S(1)}, f32[1152,256]{1,0:T(8,128)S(1)}, f32[8,128]{1,0:T(8,128)S(1)}) custom-call(s32[4]{0:T(128)S(1)} %copy-done.4, f32[4,72,256]{2,1,0:T(8,128)S(1)} %all_to_all.5.ends_ref, f32[136,256]{1,0:T(8,128)S(1)} %collective-permute-done.2.refs_2_.pair_ref, f32[4,64,16,256]{3,2,1,0:T(8,128)S(1)} %get-tuple-element.66.local_ref, ...), custom_call_target="tpu_custom_call" | custom-call | flops 4831838208 | bytes 10485760 | tf_op jit(solution)/shard_map/in_grad/pallas_call | solution.py:360
  147.3 2.4 %collective-permute-done.10.refs_2_ = bf16[288,256]{1,0:T(8,128)(2,1)S(1)} collective-permute-done((bf16[288,256]{1,0:T(8,128)(2,1)S(1)}, bf16[288,256]{1,0:T(8,128)(2,1)S(1)}, u32[]{:S(2)}, u32[]{:S(2)}) %collective-permute-start.10) | collective-permute-done | bytes 147488 | tf_op jit(solution)/shard_map/ppermute | solution.py:565
  152.9 6.6 %outputs_conv.1 = (bf16[64,4,16,256]{3,2,1,0:T(8,128)(2,1)}, f32[8,128]{1,0:T(8,128)S(1)}) custom-call(bf16[4,64,16,256]{3,2,1,0:T(8,128)(2,1)S(1)} %get-tuple-element.63.low_ref, bf16[64,16,256]{2,1,0:T(8,128)(2,1)S(1)} %collective-permute-done.3.refs_1_.up_ref, bf16[64,16,256]{2,1,0:T(8,128)(2,1)S(1)} %collective-permute-done.4.refs_2_.down_ref, ...), custom_call_target="tpu_custom_call" | custom-call | flops 4831838208 | bytes 8388608 | tf_op jit(solution)/shard_map/outputs_conv/pallas_call | solution.py:393
  163.7 2.0 %collective-permute-done.18.refs_4_ = bf16[288,256]{1,0:T(8,128)(2,1)S(1)} collective-permute-done((bf16[288,256]{1,0:T(8,128)(2,1)S(1)}, bf16[288,256]{1,0:T(8,128)(2,1)S(1)}, u32[]{:S(2)}, u32[]{:S(2)}) %collective-permute-start.18) | collective-permute-done | bytes 147488 | tf_op jit(solution)/shard_map/ppermute | solution.py:516
  167.3 3.9 %collective-permute-start.20 = (bf16[4,288,256]{2,1,0:T(8,128)(2,1)S(1)}, bf16[4,288,256]{2,1,0:T(8,128)(2,1)S(1)}, u32[]{:S(2)}, u32[]{:S(2)}) collective-permute-start(bf16[4,288,256]{2,1,0:T(8,128)(2,1)S(1)} %get-tuple-element.98.refs_2_), channel_id=1, source_target_pairs={{0,1},{1,0},{2,3},{3,2},{4,5},{5,4},{6,7},{7,6},{8,9},{9,8},{10,11... | collective-permute-start | bytes 1769480 | tf_op jit(solution)/shard_map/ppermute | solution.py:577
  172.7 8.1 %collective-permute-done.19.refs_2_ = bf16[288,256]{1,0:T(8,128)(2,1)S(1)} collective-permute-done((bf16[288,256]{1,0:T(8,128)(2,1)S(1)}, bf16[288,256]{1,0:T(8,128)(2,1)S(1)}, u32[]{:S(2)}, u32[]{:S(2)}) %collective-permute-start.19) | collective-permute-done | bytes 147488 | tf_op jit(solution)/shard_map/ppermute | solution.py:565
  180.9 1.8 collective-permute-start.23
  183.6 2.1 %out_merge.1 = (f32[2304,256]{1,0:T(8,128)}, f32[8,128]{1,0:T(8,128)S(1)}) custom-call(f32[8,128]{1,0:T(8,128)S(1)} %get-tuple-element.97.refs_0_, s32[4]{0:T(128)S(1)} %copy-done.4, bf16[4,288,256]{2,1,0:T(8,128)(2,1)S(1)} %get-tuple-element.98.refs_2_, bf16[4,288,256]{2,1,0:T(8,128)(2,1)S(1)} %collective-permute-done.20.refs_3_), custom_call_target="tpu_custom_call" | custom-call | flops 1073741824 | bytes 2097152 | tf_op jit(solution)/shard_map/out_merge/pallas_call | solution.py:461
  186.5 2.7 %collective-permute-done.22.refs_3_ = bf16[288,256]{1,0:T(8,128)(2,1)S(1)} collective-permute-done((bf16[288,256]{1,0:T(8,128)(2,1)S(1)}, bf16[288,256]{1,0:T(8,128)(2,1)S(1)}, u32[]{:S(2)}, u32[]{:S(2)}) %collective-permute-start.22) | collective-permute-done | bytes 147488 | tf_op jit(solution)/shard_map/ppermute | solution.py:516
  193.0 2.1 %in_merge.1 = (f32[2304,256]{1,0:T(8,128)}, f32[8,128]{1,0:T(8,128)}) custom-call(f32[8,128]{1,0:T(8,128)S(1)} %get-tuple-element.101.refs_0_, s32[4]{0:T(128)S(1)} %copy-done.4, bf16[4,288,256]{2,1,0:T(8,128)(2,1)S(1)} %get-tuple-element.102.refs_2_, bf16[4,288,256]{2,1,0:T(8,128)(2,1)S(1)} %collective-permute-done.24.refs_3_), custom_call_target="tpu_custom_call" | custom-call | flops 1073741824 | bytes 2097152 | tf_op jit(solution)/shard_map/in_merge/pallas_call | solution.py:461
  (63 shorter events, 26.1 us)
Async XLA Ops:
  66.8 17.1 %collective-permute-start = (bf16[2,64,16,256]{3,2,1,0:T(8,128)(2,1)}, bf16[2,64,16,256]{3,2,1,0:T(8,128)(2,1)S(1)}, u32[]{:S(2)}, u32[]{:S(2)}) collective-permute-start(bf16[2,64,16,256]{3,2,1,0:T(8,128)(2,1)} %get-tuple-element.55), channel_id=1, source_target_pairs={{0,1},{1,2},{2,3},{4,5},{5,6},{6,7},{8,9},{9,10},{10,11},{12,13},{... | collective-permute-start | bytes 3145736 | tf_op jit(solution)/shard_map/ppermute | solution.py:444
  71.3 16.3 %collective-permute-start.1 = (bf16[2,64,16,256]{3,2,1,0:T(8,128)(2,1)}, bf16[2,64,16,256]{3,2,1,0:T(8,128)(2,1)S(1)}, u32[]{:S(2)}, u32[]{:S(2)}) collective-permute-start(bf16[2,64,16,256]{3,2,1,0:T(8,128)(2,1)} %get-tuple-element.56), channel_id=1, source_target_pairs={{1,0},{2,1},{3,2},{5,4},{6,5},{7,6},{9,8},{10,9},{11,10},{13,12},{... | collective-permute-start | bytes 3145736 | tf_op jit(solution)/shard_map/ppermute | solution.py:445
  92.5 4.0 %collective-permute-start.2 = (f32[136,256]{1,0:T(8,128)S(1)}, f32[136,256]{1,0:T(8,128)S(1)}, u32[]{:S(2)}, u32[]{:S(2)}) collective-permute-start(f32[136,256]{1,0:T(8,128)S(1)} %get-tuple-element.59.refs_1_), channel_id=1, source_target_pairs={{0,4},{4,0},{1,5},{5,1},{2,6},{6,2},{3,7},{7,3},{8,12},{12,8},{9,1... | collective-permute-start | bytes 417800 | tf_op jit(solution)/shard_map/ppermute | solution.py:541
  116.4 6.6 %collective-permute-start.5 = (bf16[1152,256]{1,0:T(8,128)(2,1)S(1)}, bf16[1152,256]{1,0:T(8,128)(2,1)S(1)}, u32[]{:S(2)}, u32[]{:S(2)}) collective-permute-start(bf16[1152,256]{1,0:T(8,128)(2,1)S(1)} %get-tuple-element.70), channel_id=1, source_target_pairs={{0,1},{1,0},{2,3},{3,2},{4,5},{5,4},{6,7},{7,6},{8,9},{9,8},{10,11... | collective-permute-start | bytes 1769480 | tf_op jit(solution)/shard_map/ppermute | solution.py:550
  116.5 10.9 %collective-permute-start.3 = (bf16[64,16,256]{2,1,0:T(8,128)(2,1)S(1)}, bf16[64,16,256]{2,1,0:T(8,128)(2,1)S(1)}, u32[]{:S(2)}, u32[]{:S(2)}) collective-permute-start(bf16[64,16,256]{2,1,0:T(8,128)(2,1)S(1)} %get-tuple-element.64), channel_id=1, source_target_pairs={{0,1},{1,2},{2,3},{4,5},{5,6},{6,7},{8,9},{9,10},{10,11},{12,13},{... | collective-permute-start | bytes 1572872 | tf_op jit(solution)/shard_map/ppermute | solution.py:444
  120.9 15.2 %collective-permute-start.4 = (bf16[64,16,256]{2,1,0:T(8,128)(2,1)S(1)}, bf16[64,16,256]{2,1,0:T(8,128)(2,1)S(1)}, u32[]{:S(2)}, u32[]{:S(2)}) collective-permute-start(bf16[64,16,256]{2,1,0:T(8,128)(2,1)S(1)} %get-tuple-element.65), channel_id=1, source_target_pairs={{1,0},{2,1},{3,2},{5,4},{6,5},{7,6},{9,8},{10,9},{11,10},{13,12},{... | collective-permute-start | bytes 1572872 | tf_op jit(solution)/shard_map/ppermute | solution.py:445
  123.7 20.9 %collective-permute-start.6 = (bf16[288,256]{1,0:T(8,128)(2,1)S(1)}, bf16[288,256]{1,0:T(8,128)(2,1)S(1)}, u32[]{:S(2)}, u32[]{:S(2)}) collective-permute-start(bf16[288,256]{1,0:T(8,128)(2,1)S(1)} %get-tuple-element.74), channel_id=1, source_target_pairs={{0,2},{2,0},{4,6},{6,4},{1,3},{3,1},{5,7},{7,5},{8,10},{10,8},{12,... | collective-permute-start | bytes 442376 | tf_op jit(solution)/shard_map/ppermute | solution.py:516
  124.4 20.3 %collective-permute-start.7 = (bf16[288,256]{1,0:T(8,128)(2,1)S(1)}, bf16[288,256]{1,0:T(8,128)(2,1)S(1)}, u32[]{:S(2)}, u32[]{:S(2)}) collective-permute-start(bf16[288,256]{1,0:T(8,128)(2,1)S(1)} %get-tuple-element.75), channel_id=1, source_target_pairs={{0,4},{2,6},{4,0},{6,2},{1,5},{3,7},{5,1},{7,3},{8,12},{10,14},{12... | collective-permute-start | bytes 442376 | tf_op jit(solution)/shard_map/ppermute | solution.py:516
  125.7 19.0 %collective-permute-start.8 = (bf16[288,256]{1,0:T(8,128)(2,1)S(1)}, bf16[288,256]{1,0:T(8,128)(2,1)S(1)}, u32[]{:S(2)}, u32[]{:S(2)}) collective-permute-start(bf16[288,256]{1,0:T(8,128)(2,1)S(1)} %get-tuple-element.76), channel_id=1, source_target_pairs={{0,6},{2,4},{4,2},{6,0},{1,7},{3,5},{5,3},{7,1},{8,14},{10,12},{12... | collective-permute-start | bytes 442376 | tf_op jit(solution)/shard_map/ppermute | solution.py:516
  144.8 5.0 %collective-permute-start.10 = (bf16[288,256]{1,0:T(8,128)(2,1)S(1)}, bf16[288,256]{1,0:T(8,128)(2,1)S(1)}, u32[]{:S(2)}, u32[]{:S(2)}) collective-permute-start(bf16[288,256]{1,0:T(8,128)(2,1)S(1)} %get-tuple-element.81.refs_1_), channel_id=1, source_target_pairs={{0,8},{8,0},{16,24},{24,16},{1,9},{9,1},{17,25},{25,17},{2,10},{10... | collective-permute-start | bytes 442376 | tf_op jit(solution)/shard_map/ppermute | solution.py:565
  149.8 10.8 %collective-permute-start.14 = (bf16[288,256]{1,0:T(8,128)(2,1)S(1)}, bf16[288,256]{1,0:T(8,128)(2,1)S(1)}, u32[]{:S(2)}, u32[]{:S(2)}) collective-permute-start(bf16[288,256]{1,0:T(8,128)(2,1)S(1)} %get-tuple-element.90.refs_1_), channel_id=1, source_target_pairs={{0,16},{8,24},{16,0},{24,8},{1,17},{9,25},{17,1},{25,9},{2,18},{10... | collective-permute-start | bytes 442376 | tf_op jit(solution)/shard_map/ppermute | solution.py:565
  150.3 9.2 %collective-permute-start.11 = (bf16[288,256]{1,0:T(8,128)(2,1)S(1)}, bf16[288,256]{1,0:T(8,128)(2,1)S(1)}, u32[]{:S(2)}, u32[]{:S(2)}) collective-permute-start(bf16[288,256]{1,0:T(8,128)(2,1)S(1)} %get-tuple-element.86), channel_id=1, source_target_pairs={{0,2},{2,0},{4,6},{6,4},{1,3},{3,1},{5,7},{7,5},{8,10},{10,8},{12,... | collective-permute-start | bytes 442376 | tf_op jit(solution)/shard_map/ppermute | solution.py:516
  150.7 8.8 %collective-permute-start.12 = (bf16[288,256]{1,0:T(8,128)(2,1)S(1)}, bf16[288,256]{1,0:T(8,128)(2,1)S(1)}, u32[]{:S(2)}, u32[]{:S(2)}) collective-permute-start(bf16[288,256]{1,0:T(8,128)(2,1)S(1)} %get-tuple-element.87), channel_id=1, source_target_pairs={{0,4},{2,6},{4,0},{6,2},{1,5},{3,7},{5,1},{7,3},{8,12},{10,14},{12... | collective-permute-start | bytes 442376 | tf_op jit(solution)/shard_map/ppermute | solution.py:516
  151.9 7.6 %collective-permute-start.13 = (bf16[288,256]{1,0:T(8,128)(2,1)S(1)}, bf16[288,256]{1,0:T(8,128)(2,1)S(1)}, u32[]{:S(2)}, u32[]{:S(2)}) collective-permute-start(bf16[288,256]{1,0:T(8,128)(2,1)S(1)} %get-tuple-element.88), channel_id=1, source_target_pairs={{0,6},{2,4},{4,2},{6,0},{1,7},{3,5},{5,3},{7,1},{8,14},{10,12},{12... | collective-permute-start | bytes 442376 | tf_op jit(solution)/shard_map/ppermute | solution.py:516
  159.6 4.1 %collective-permute-start.15 = (bf16[288,256]{1,0:T(8,128)(2,1)S(1)}, bf16[288,256]{1,0:T(8,128)(2,1)S(1)}, u32[]{:S(2)}, u32[]{:S(2)}) collective-permute-start(bf16[288,256]{1,0:T(8,128)(2,1)S(1)} %get-tuple-element.92.refs_1_), channel_id=1, source_target_pairs={{0,8},{8,0},{16,24},{24,16},{1,9},{9,1},{17,25},{25,17},{2,10},{10... | collective-permute-start | bytes 442376 | tf_op jit(solution)/shard_map/ppermute | solution.py:565
  160.7 5.1 %collective-permute-start.18 = (bf16[288,256]{1,0:T(8,128)(2,1)S(1)}, bf16[288,256]{1,0:T(8,128)(2,1)S(1)}, u32[]{:S(2)}, u32[]{:S(2)}) collective-permute-start(bf16[288,256]{1,0:T(8,128)(2,1)S(1)} %get-tuple-element.94.refs_1_), channel_id=1, source_target_pairs={{0,6},{2,4},{4,2},{6,0},{1,7},{3,5},{5,3},{7,1},{8,14},{10,12},{12... | collective-permute-start | bytes 442376 | tf_op jit(solution)/shard_map/ppermute | solution.py:516
  162.1 4.8 %collective-permute-start.17 = (bf16[288,256]{1,0:T(8,128)(2,1)S(1)}, bf16[288,256]{1,0:T(8,128)(2,1)S(1)}, u32[]{:S(2)}, u32[]{:S(2)}) collective-permute-start(bf16[288,256]{1,0:T(8,128)(2,1)S(1)} %get-tuple-element.94.refs_1_), channel_id=1, source_target_pairs={{0,4},{2,6},{4,0},{6,2},{1,5},{3,7},{5,1},{7,3},{8,12},{10,14},{12... | collective-permute-start | bytes 442376 | tf_op jit(solution)/shard_map/ppermute | solution.py:516
  162.4 4.9 %collective-permute-start.16 = (bf16[288,256]{1,0:T(8,128)(2,1)S(1)}, bf16[288,256]{1,0:T(8,128)(2,1)S(1)}, u32[]{:S(2)}, u32[]{:S(2)}) collective-permute-start(bf16[288,256]{1,0:T(8,128)(2,1)S(1)} %get-tuple-element.94.refs_1_), channel_id=1, source_target_pairs={{0,2},{2,0},{4,6},{6,4},{1,3},{3,1},{5,7},{7,5},{8,10},{10,8},{12,... | collective-permute-start | bytes 442376 | tf_op jit(solution)/shard_map/ppermute | solution.py:516
  167.3 16.3 %collective-permute-start.20 = (bf16[4,288,256]{2,1,0:T(8,128)(2,1)S(1)}, bf16[4,288,256]{2,1,0:T(8,128)(2,1)S(1)}, u32[]{:S(2)}, u32[]{:S(2)}) collective-permute-start(bf16[4,288,256]{2,1,0:T(8,128)(2,1)S(1)} %get-tuple-element.98.refs_2_), channel_id=1, source_target_pairs={{0,1},{1,0},{2,3},{3,2},{4,5},{5,4},{6,7},{7,6},{8,9},{9,8},{10,11... | collective-permute-start | bytes 1769480 | tf_op jit(solution)/shard_map/ppermute | solution.py:577
  171.2 9.6 %collective-permute-start.19 = (bf16[288,256]{1,0:T(8,128)(2,1)S(1)}, bf16[288,256]{1,0:T(8,128)(2,1)S(1)}, u32[]{:S(2)}, u32[]{:S(2)}) collective-permute-start(bf16[288,256]{1,0:T(8,128)(2,1)S(1)} %get-tuple-element.96.refs_1_), channel_id=1, source_target_pairs={{0,16},{8,24},{16,0},{24,8},{1,17},{9,25},{17,1},{25,9},{2,18},{10... | collective-permute-start | bytes 442376 | tf_op jit(solution)/shard_map/ppermute | solution.py:565
  180.9 5.6 %collective-permute-start.23 = (bf16[288,256]{1,0:T(8,128)(2,1)S(1)}, bf16[288,256]{1,0:T(8,128)(2,1)S(1)}, u32[]{:S(2)}, u32[]{:S(2)}) collective-permute-start(bf16[288,256]{1,0:T(8,128)(2,1)S(1)} %get-tuple-element.100.refs_1_), channel_id=1, source_target_pairs={{0,6},{2,4},{4,2},{6,0},{1,7},{3,5},{5,3},{7,1},{8,14},{10,12},{12... | collective-permute-start | bytes 442376 | tf_op jit(solution)/shard_map/ppermute | solution.py:516
  182.6 6.6 %collective-permute-start.22 = (bf16[288,256]{1,0:T(8,128)(2,1)S(1)}, bf16[288,256]{1,0:T(8,128)(2,1)S(1)}, u32[]{:S(2)}, u32[]{:S(2)}) collective-permute-start(bf16[288,256]{1,0:T(8,128)(2,1)S(1)} %get-tuple-element.100.refs_1_), channel_id=1, source_target_pairs={{0,4},{2,6},{4,0},{6,2},{1,5},{3,7},{5,1},{7,3},{8,12},{10,14},{12... | collective-permute-start | bytes 442376 | tf_op jit(solution)/shard_map/ppermute | solution.py:516
  182.9 7.6 %collective-permute-start.21 = (bf16[288,256]{1,0:T(8,128)(2,1)S(1)}, bf16[288,256]{1,0:T(8,128)(2,1)S(1)}, u32[]{:S(2)}, u32[]{:S(2)}) collective-permute-start(bf16[288,256]{1,0:T(8,128)(2,1)S(1)} %get-tuple-element.100.refs_1_), channel_id=1, source_target_pairs={{0,2},{2,0},{4,6},{6,4},{1,3},{3,1},{5,7},{7,5},{8,10},{10,8},{12,... | collective-permute-start | bytes 442376 | tf_op jit(solution)/shard_map/ppermute | solution.py:516
  190.5 2.6 %collective-permute-start.24 = (bf16[4,288,256]{2,1,0:T(8,128)(2,1)S(1)}, bf16[4,288,256]{2,1,0:T(8,128)(2,1)S(1)}, u32[]{:S(2)}, u32[]{:S(2)}) collective-permute-start(bf16[4,288,256]{2,1,0:T(8,128)(2,1)S(1)} %get-tuple-element.102.refs_2_), channel_id=1, source_target_pairs={{0,1},{1,0},{2,3},{3,2},{4,5},{5,4},{6,7},{7,6},{8,9},{9,8},{10,11... | collective-permute-start | bytes 1769480 | tf_op jit(solution)/shard_map/ppermute | solution.py:577
  (8 other events, 177.6 us)

commit v2 on v1

--- a/solution.py
+++ b/solution.py
@@ -411,31 +411,29 @@
     )(low, up, down, taps, x, skip, after)
 
 
-def edge_rows_kernel(places_ref, x_ref, cot_ref, first_ref, last_ref, sems):
-    rows = x_ref.shape[1]
-    copies = []
-    for k, ref in enumerate((x_ref, cot_ref)):
-        copies.append(pltpu.make_async_copy(ref.at[:, 0], first_ref.at[k], sems.at[k, 0]))
-        copies.append(pltpu.make_async_copy(ref.at[:, rows - 1], last_ref.at[k], sems.at[k, 1]))
-    for copy in copies:
-        copy.start()
-    for copy in copies:
-        copy.wait()
-
-
-def edge_rows(places, x, cot):
+def edge_rows_kernel(places_ref, *refs):
+    first_ref, last_ref = refs[4:]
+    for k in range(2):
+        first_ref[k] = refs[2 * k][:, 0]
+        last_ref[k] = refs[2 * k + 1][:, 0]
+
+
+def edge_rows(places, x, cot, block):
     frames, rows, width, c = x.shape
     line = jax.ShapeDtypeStruct((2, frames, width, c), x.dtype)
+    line_spec = pl.BlockSpec((2, block, width, c), lambda b: (0, b, 0, 0))
+    first = pl.BlockSpec((block, 1, width, c), lambda b: (b, 0, 0, 0))
+    last = pl.BlockSpec((block, 1, width, c), lambda b: (b, rows - 1, 0, 0))
     return pl.pallas_call(
         edge_rows_kernel,
-        in_specs=[SCALARS, ANYWHERE, ANYWHERE],
-        out_specs=[ANYWHERE, ANYWHERE],
+        grid=(frames // block,),
+        in_specs=[SCALARS, first, last, first, last],
+        out_specs=[line_spec, line_spec],
         out_shape=[line, line],
-        scratch_shapes=[pltpu.SemaphoreType.DMA((2, 2))],
-        compiler_params=pltpu.CompilerParams(vmem_limit_bytes=56 * 2**20),
+        compiler_params=params(56),
         cost_estimate=cost(0, 2**22),
         name="edge_rows",
-    )(places, x, cot)
+    )(places, x, x, cot, cot)
 
 
 def row_halo(first, last):
@@ -531,7 +529,7 @@
     deep = lax.axis_size("a")
     lines = rows * width
 
-    up, down = row_halo(*edge_rows(places, x, cot))
+    up, down = row_halo(*edge_rows(places, x, cot, block))
     x_part, x_taps = interior_conv(x, in_kernel, False, block)
     cot_part, cot_taps = interior_conv(cot, out_kernel, True, block)
     states, running, end = local_scan(x_part, up, down, 0, x_taps, decays, block, False, decays)
@@ -583,10 +581,10 @@
 
     own, others, token = add("out_add", kept, got, [token])
     sent, kept, token = kernel_grads(
-        places, ends, pair, adjoint, trailing, x, up, down, 0, decays, block, [token, low_up, low_down]
+        places, ends, pair, adjoint, trailing, x, up, down, 0, decays, block, [token]
     )
     got = lax.ppermute(sent, "core", CORES)
-    out_part, token = sums("out_share", None, [own] + others, [token], mib=FAR)
+    out_part, token = sums("out_share", None, [own] + others, [token, low_up, low_down], mib=FAR)
     out_other = swapped(out_part, 1)
     own, others, token = add("in_add", kept, got, [token])
     out_part, out_other, token = middle("out_mid", out_part, out_other, [token])

time: 196 us -> 127 us (0.65)
  Pallas kernels: 111 us -> 49.3 us
  waiting for transfers between devices: 38.2 us -> 28 us
  starting transfers between devices: 33.5 us -> 36.4 us
    pallas_call x1, Pallas kernels: 65.5 us -> 4 us  [edge_rows(): pl.pallas_call(edge_rows_kernel, grid=(frames // block,), in_specs=[SCALA...]
    ppermute x2, waiting for transfers between devices: 12.5 us -> 3.93 us  [row_halo(): down = lax.ppermute(first, axes, [(i + 1, i) for i in range(count - 1)])]
  transfers between devices with their start and end apart: 25 -> 25, of which waited for: 15 -> 13; matrix products, arithmetic and copies ran while one was open for 0% -> 0% of each run, Pallas kernels for 15% -> 23%
where the time goes in v2:
time: 127 us; the launch traced here: 126 us
  Pallas kernels  49.3 us (39%)
  starting transfers between devices  36.4 us (29%)
  waiting for transfers between devices  28 us (22%)
  blocking collectives  11 us (9%)
    ppermute x12, starting transfers between devices, from_others(): lax.ppermute(part, axes, [(i, i ^ k) for i in range(count)])  12.3 us
    all_to_all x1, blocking collectives, per_device(): ends = lax.all_to_all(ends, 'a', 0, 0)  11 us
    ppermute x4, waiting for transfers between devices, swapped(): return lax.ppermute(part, 'a', [(i, i ^ bit) for i in range(deep)])  10.1 us
    ppermute x2, starting transfers between devices, row_halo(): up = lax.ppermute(last, axes, [(i, i + 1) for i in range(count - 1)])  8.98 us
    ppermute x12, waiting for transfers between devices, from_others(): lax.ppermute(part, axes, [(i, i ^ k) for i in range(count)])  8.88 us
    pallas_call x1, Pallas kernels, kernel_grads(): pl.pallas_call(in_grad_kernel, grid=(frames // block,), in_specs=lead + [...  8.36 us
    pallas_call x1, Pallas kernels, kernel_grads(): pl.pallas_call(out_grad_kernel, grid=(frames // block,), in_specs=lead +...  7.78 us
    pallas_call x13, Pallas kernels, small_call(): pl.pallas_call(kernel, in_specs=[ANYWHERE] * len(after) + [SCALARS] * len...  7.13 us
  transfers between devices with their start and end apart: 25, of which 13 were waited for; matrix products, arithmetic and copies ran while one was open for 0% of the time, Pallas kernels for 23%

profile of v2, /device:TPU:1, one launch (start us, length us, event | category | flops | bytes accessed | tf_op | source)
XLA Modules:
  0.0 126.2 jit_solution(11666006449172058222)
XLA Ops:
  1.3 4.0 %edge_rows.1 = (bf16[2,64,16,256]{3,2,1,0:T(8,128)(2,1)}, bf16[2,64,16,256]{3,2,1,0:T(8,128)(2,1)}) custom-call(s32[4]{0:T(128)} %pad_add_fusion.places_ref.refs_0_.place_ref.refs_1_, bf16[64,4,16,256]{3,2,1,0:T(8,128)(2,1)} %bitcast.16, bf16[64,4,16,256]{3,2,1,0:T(8,128)(2,1)} %bitcast.17, bf16[64,4,16,256]{3,2,1,0:T(8,128)(2,1)} %bitcast.12, ...), custom_call_target="tpu_custom_call" | custom-call | bytes 4194304 | tf_op jit(solution)/shard_map/edge_rows/pallas_call | solution.py:427
  5.3 4.5 %collective-permute-start = (bf16[2,64,16,256]{3,2,1,0:T(8,128)(2,1)}, bf16[2,64,16,256]{3,2,1,0:T(8,128)(2,1)S(1)}, u32[]{:S(2)}, u32[]{:S(2)}) collective-permute-start(bf16[2,64,16,256]{3,2,1,0:T(8,128)(2,1)} %get-tuple-element.55), channel_id=1, source_target_pairs={{0,1},{1,2},{2,3},{4,5},{5,6},{6,7},{8,9},{9,10},{10,11},{12,13},{... | collective-permute-start | bytes 3145736 | tf_op jit(solution)/shard_map/ppermute | solution.py:442
  11.8 5.1 %interior_in.1.part_ref = f32[4,64,16,256]{3,2,1,0:T(8,128)S(1)} custom-call(bf16[64,4,16,256]{3,2,1,0:T(8,128)(2,1)S(1)} %bitcast.18, bf16[3,768,256]{2,1,0:T(8,128)(2,1)S(1)} %bitcast.21), custom_call_target="tpu_custom_call" | custom-call | flops 4831838208 | bytes 8388608 | tf_op jit(solution)/shard_map/interior_in/pallas_call | solution.py:106
  16.9 5.6 %interior_cot.1 = (f32[4,64,16,256]{3,2,1,0:T(8,128)S(1)}, bf16[3,768,256]{2,1,0:T(8,128)(2,1)S(1)}) custom-call(bf16[64,4,16,256]{3,2,1,0:T(8,128)(2,1)S(1)} %bitcast.14, bf16[3,3,256,256]{3,2,1,0:T(8,128)(2,1)S(1)} %copy-done.5), custom_call_target="tpu_custom_call" | custom-call | flops 4831838208 | bytes 8388608 | tf_op jit(solution)/shard_map/interior_cot/pallas_call | solution.py:91
  22.5 3.7 %collective-permute-done.1.down_ref = bf16[2,64,16,256]{3,2,1,0:T(8,128)(2,1)S(1)} collective-permute-done((bf16[2,64,16,256]{3,2,1,0:T(8,128)(2,1)}, bf16[2,64,16,256]{3,2,1,0:T(8,128)(2,1)S(1)}, u32[]{:S(2)}, u32[]{:S(2)}) %collective-permute-start.1) | collective-permute-done | bytes 1048608 | tf_op jit(solution)/shard_map/ppermute | solution.py:443
  26.2 2.2 %scan_fwd.1 = (f32[4,64,16,256]{3,2,1,0:T(8,128)S(1)}, f32[64,256]{1,0:T(8,128)S(1)}, f32[64,256]{1,0:T(8,128)S(1)}) custom-call(f32[4,64,16,256]{3,2,1,0:T(8,128)S(1)} %interior_in.1.part_ref, bf16[2,64,16,256]{3,2,1,0:T(8,128)(2,1)S(1)} %collective-permute-done.up_ref, bf16[2,64,16,256]{3,2,1,0:T(8,128)(2,1)S(1)} %collective-permute-done.1.down_ref, ...), custom_call_target="tpu_custom_call" | custom-call | flops 805306368 | bytes 12582912 | tf_op jit(solution)/shard_map/scan_fwd/pallas_call | solution.py:180
  28.4 2.5 %scan_back.1 = (f32[4,64,16,256]{3,2,1,0:T(8,128)S(1)}, f32[64,256]{1,0:T(8,128)S(1)}, f32[136,256]{1,0:T(8,128)S(1)}) custom-call(f32[4,64,16,256]{3,2,1,0:T(8,128)S(1)} %get-tuple-element.54.part_ref, bf16[2,64,16,256]{3,2,1,0:T(8,128)(2,1)S(1)} %collective-permute-done.up_ref, bf16[2,64,16,256]{3,2,1,0:T(8,128)(2,1)S(1)} %collective-permute-done.1.down_ref, ...), custom_call_target="tpu_custom_call" | custom-call | flops 805306368 | bytes 12582912 | tf_op jit(solution)/shard_map/scan_back/pallas_call | solution.py:180
  32.2 2.7 %collective-permute-done.2.refs_2_.pair_ref = f32[136,256]{1,0:T(8,128)S(1)} collective-permute-done((f32[136,256]{1,0:T(8,128)S(1)}, f32[136,256]{1,0:T(8,128)S(1)}, u32[]{:S(2)}, u32[]{:S(2)}) %collective-permute-start.2) | collective-permute-done | bytes 139296 | tf_op jit(solution)/shard_map/ppermute | solution.py:539
  36.1 11.0 %all_to_all.5.ends_ref = f32[4,72,256]{2,1,0:T(8,128)S(1)} all-to-all(f32[4,72,256]{2,1,0:T(8,128)S(1)} %get-tuple-element.60), channel_id=1, replica_groups=mesh['a'=4,'x'=2,'y'=2,'core'=2] {'a'}, dimensions={0} | all-to-all | bytes 589824 | tf_op jit(solution)/shard_map/all_to_all | solution.py:543
  47.0 7.8 %out_grad.1 = (bf16[4,64,16,256]{3,2,1,0:T(8,128)(2,1)S(1)}, bf16[64,16,256]{2,1,0:T(8,128)(2,1)S(1)}, bf16[64,16,256]{2,1,0:T(8,128)(2,1)S(1)}, bf16[1152,256]{...) custom-call(s32[4]{0:T(128)S(1)} %copy-done.4, f32[4,72,256]{2,1,0:T(8,128)S(1)} %all_to_all.5.ends_ref, ...), custom_call_target="tpu_custom_call" | custom-call | flops 4831838208 | bytes 10485760 | tf_op jit(solution)/shard_map/out_grad/pallas_call | solution.py:349
  54.9 4.5 %collective-permute-start.3 = (bf16[64,16,256]{2,1,0:T(8,128)(2,1)S(1)}, bf16[64,16,256]{2,1,0:T(8,128)(2,1)S(1)}, u32[]{:S(2)}, u32[]{:S(2)}) collective-permute-start(bf16[64,16,256]{2,1,0:T(8,128)(2,1)S(1)} %get-tuple-element.64), channel_id=1, source_target_pairs={{0,1},{1,2},{2,3},{4,5},{5,6},{6,7},{8,9},{9,10},{10,11},{12,13},{... | collective-permute-start | bytes 1572872 | tf_op jit(solution)/shard_map/ppermute | solution.py:442
  59.4 2.1 %collective-permute-start.4 = (bf16[64,16,256]{2,1,0:T(8,128)(2,1)S(1)}, bf16[64,16,256]{2,1,0:T(8,128)(2,1)S(1)}, u32[]{:S(2)}, u32[]{:S(2)}) collective-permute-start(bf16[64,16,256]{2,1,0:T(8,128)(2,1)S(1)} %get-tuple-element.65), channel_id=1, source_target_pairs={{1,0},{2,1},{3,2},{5,4},{6,5},{7,6},{9,8},{10,9},{11,10},{13,12},{... | collective-permute-start | bytes 1572872 | tf_op jit(solution)/shard_map/ppermute | solution.py:443
  64.9 8.4 %in_grad.1 = (bf16[1152,256]{1,0:T(8,128)(2,1)S(1)}, f32[1152,256]{1,0:T(8,128)S(1)}, f32[8,128]{1,0:T(8,128)S(1)}) custom-call(s32[4]{0:T(128)S(1)} %copy-done.4, f32[4,72,256]{2,1,0:T(8,128)S(1)} %all_to_all.5.ends_ref, f32[136,256]{1,0:T(8,128)S(1)} %collective-permute-done.2.refs_2_.pair_ref, f32[4,64,16,256]{3,2,1,0:T(8,128)S(1)} %get-tuple-element.66.local_ref, ...), custom_call_target="tpu_custom_call" | custom-call | flops 4831838208 | bytes 10485760 | tf_op jit(solution)/shard_map/in_grad/pallas_call | solution.py:360
  76.7 2.1 %collective-permute-done.10.refs_2_ = bf16[288,256]{1,0:T(8,128)(2,1)S(1)} collective-permute-done((bf16[288,256]{1,0:T(8,128)(2,1)S(1)}, bf16[288,256]{1,0:T(8,128)(2,1)S(1)}, u32[]{:S(2)}, u32[]{:S(2)}) %collective-permute-start.10) | collective-permute-done | bytes 147488 | tf_op jit(solution)/shard_map/ppermute | solution.py:563
  79.2 2.8 %collective-permute-start.11 = (bf16[288,256]{1,0:T(8,128)(2,1)S(1)}, bf16[288,256]{1,0:T(8,128)(2,1)S(1)}, u32[]{:S(2)}, u32[]{:S(2)}) collective-permute-start(bf16[288,256]{1,0:T(8,128)(2,1)S(1)} %get-tuple-element.86), channel_id=1, source_target_pairs={{0,2},{2,0},{4,6},{6,4},{1,3},{3,1},{5,7},{7,5},{8,10},{10,8},{12,... | collective-permute-start | bytes 442376 | tf_op jit(solution)/shard_map/ppermute | solution.py:514
  83.3 6.6 %outputs_conv.1 = (bf16[64,4,16,256]{3,2,1,0:T(8,128)(2,1)}, f32[8,128]{1,0:T(8,128)S(1)}) custom-call(bf16[4,64,16,256]{3,2,1,0:T(8,128)(2,1)S(1)} %get-tuple-element.63.low_ref, bf16[64,16,256]{2,1,0:T(8,128)(2,1)S(1)} %collective-permute-done.3.refs_1_.up_ref, bf16[64,16,256]{2,1,0:T(8,128)(2,1)S(1)} %collective-permute-done.4.refs_2_.down_ref, ...), custom_call_target="tpu_custom_call" | custom-call | flops 4831838208 | bytes 8388608 | tf_op jit(solution)/shard_map/outputs_conv/pallas_call | solution.py:393
  91.1 2.4 %collective-permute-start.18 = (bf16[288,256]{1,0:T(8,128)(2,1)S(1)}, bf16[288,256]{1,0:T(8,128)(2,1)S(1)}, u32[]{:S(2)}, u32[]{:S(2)}) collective-permute-start(bf16[288,256]{1,0:T(8,128)(2,1)S(1)} %get-tuple-element.94.refs_1_), channel_id=1, source_target_pairs={{0,6},{2,4},{4,2},{6,0},{1,7},{3,5},{5,3},{7,1},{8,14},{10,12},{12... | collective-permute-start | bytes 442376 | tf_op jit(solution)/shard_map/ppermute | solution.py:514
  94.1 1.9 %collective-permute-done.18.refs_4_ = bf16[288,256]{1,0:T(8,128)(2,1)S(1)} collective-permute-done((bf16[288,256]{1,0:T(8,128)(2,1)S(1)}, bf16[288,256]{1,0:T(8,128)(2,1)S(1)}, u32[]{:S(2)}, u32[]{:S(2)}) %collective-permute-start.18) | collective-permute-done | bytes 147488 | tf_op jit(solution)/shard_map/ppermute | solution.py:514
  96.0 2.2 %collective-permute-done.17.refs_3_ = bf16[288,256]{1,0:T(8,128)(2,1)S(1)} collective-permute-done((bf16[288,256]{1,0:T(8,128)(2,1)S(1)}, bf16[288,256]{1,0:T(8,128)(2,1)S(1)}, u32[]{:S(2)}, u32[]{:S(2)}) %collective-permute-start.17) | collective-permute-done | bytes 147488 | tf_op jit(solution)/shard_map/ppermute | solution.py:514
  98.3 4.0 %collective-permute-start.20 = (bf16[4,288,256]{2,1,0:T(8,128)(2,1)S(1)}, bf16[4,288,256]{2,1,0:T(8,128)(2,1)S(1)}, u32[]{:S(2)}, u32[]{:S(2)}) collective-permute-start(bf16[4,288,256]{2,1,0:T(8,128)(2,1)S(1)} %get-tuple-element.98.refs_2_), channel_id=1, source_target_pairs={{0,1},{1,0},{2,3},{3,2},{4,5},{5,4},{6,7},{7,6},{8,9},{9,8},{10,11... | collective-permute-start | bytes 1769480 | tf_op jit(solution)/shard_map/ppermute | solution.py:575
  104.0 7.9 %collective-permute-done.19.refs_2_ = bf16[288,256]{1,0:T(8,128)(2,1)S(1)} collective-permute-done((bf16[288,256]{1,0:T(8,128)(2,1)S(1)}, bf16[288,256]{1,0:T(8,128)(2,1)S(1)}, u32[]{:S(2)}, u32[]{:S(2)}) %collective-permute-start.19) | collective-permute-done | bytes 147488 | tf_op jit(solution)/shard_map/ppermute | solution.py:563
  114.7 2.1 %out_merge.1 = (f32[2304,256]{1,0:T(8,128)}, f32[8,128]{1,0:T(8,128)S(1)}) custom-call(f32[8,128]{1,0:T(8,128)S(1)} %get-tuple-element.97.refs_0_, s32[4]{0:T(128)S(1)} %copy-done.4, bf16[4,288,256]{2,1,0:T(8,128)(2,1)S(1)} %get-tuple-element.98.refs_2_, bf16[4,288,256]{2,1,0:T(8,128)(2,1)S(1)} %collective-permute-done.20.refs_3_), custom_call_target="tpu_custom_call" | custom-call | flops 1073741824 | bytes 2097152 | tf_op jit(solution)/shard_map/out_merge/pallas_call | solution.py:459
  117.6 2.7 %collective-permute-done.22.refs_3_ = bf16[288,256]{1,0:T(8,128)(2,1)S(1)} collective-permute-done((bf16[288,256]{1,0:T(8,128)(2,1)S(1)}, bf16[288,256]{1,0:T(8,128)(2,1)S(1)}, u32[]{:S(2)}, u32[]{:S(2)}) %collective-permute-start.22) | collective-permute-done | bytes 147488 | tf_op jit(solution)/shard_map/ppermute | solution.py:514
  124.1 2.1 %in_merge.1 = (f32[2304,256]{1,0:T(8,128)}, f32[8,128]{1,0:T(8,128)}) custom-call(f32[8,128]{1,0:T(8,128)S(1)} %get-tuple-element.101.refs_0_, s32[4]{0:T(128)S(1)} %copy-done.4, bf16[4,288,256]{2,1,0:T(8,128)(2,1)S(1)} %get-tuple-element.102.refs_2_, bf16[4,288,256]{2,1,0:T(8,128)(2,1)S(1)} %collective-permute-done.24.refs_3_), custom_call_target="tpu_custom_call" | custom-call | flops 1073741824 | bytes 2097152 | tf_op jit(solution)/shard_map/in_merge/pallas_call | solution.py:459
  (63 shorter events, 24.5 us)
Async XLA Ops:
  5.3 17.2 %collective-permute-start = (bf16[2,64,16,256]{3,2,1,0:T(8,128)(2,1)}, bf16[2,64,16,256]{3,2,1,0:T(8,128)(2,1)S(1)}, u32[]{:S(2)}, u32[]{:S(2)}) collective-permute-start(bf16[2,64,16,256]{3,2,1,0:T(8,128)(2,1)} %get-tuple-element.55), channel_id=1, source_target_pairs={{0,1},{1,2},{2,3},{4,5},{5,6},{6,7},{8,9},{9,10},{10,11},{12,13},{... | collective-permute-start | bytes 3145736 | tf_op jit(solution)/shard_map/ppermute | solution.py:442
  9.8 16.3 %collective-permute-start.1 = (bf16[2,64,16,256]{3,2,1,0:T(8,128)(2,1)}, bf16[2,64,16,256]{3,2,1,0:T(8,128)(2,1)S(1)}, u32[]{:S(2)}, u32[]{:S(2)}) collective-permute-start(bf16[2,64,16,256]{3,2,1,0:T(8,128)(2,1)} %get-tuple-element.56), channel_id=1, source_target_pairs={{1,0},{2,1},{3,2},{5,4},{6,5},{7,6},{9,8},{10,9},{11,10},{13,12},{... | collective-permute-start | bytes 3145736 | tf_op jit(solution)/shard_map/ppermute | solution.py:443
  30.9 4.0 %collective-permute-start.2 = (f32[136,256]{1,0:T(8,128)S(1)}, f32[136,256]{1,0:T(8,128)S(1)}, u32[]{:S(2)}, u32[]{:S(2)}) collective-permute-start(f32[136,256]{1,0:T(8,128)S(1)} %get-tuple-element.59.refs_1_), channel_id=1, source_target_pairs={{0,4},{4,0},{1,5},{5,1},{2,6},{6,2},{3,7},{7,3},{8,12},{12,8},{9,1... | collective-permute-start | bytes 417800 | tf_op jit(solution)/shard_map/ppermute | solution.py:539
  54.8 6.7 %collective-permute-start.5 = (bf16[1152,256]{1,0:T(8,128)(2,1)S(1)}, bf16[1152,256]{1,0:T(8,128)(2,1)S(1)}, u32[]{:S(2)}, u32[]{:S(2)}) collective-permute-start(bf16[1152,256]{1,0:T(8,128)(2,1)S(1)} %get-tuple-element.70), channel_id=1, source_target_pairs={{0,1},{1,0},{2,3},{3,2},{4,5},{5,4},{6,7},{7,6},{8,9},{9,8},{10,11... | collective-permute-start | bytes 1769480 | tf_op jit(solution)/shard_map/ppermute | solution.py:548
  54.9 18.4 %collective-permute-start.3 = (bf16[64,16,256]{2,1,0:T(8,128)(2,1)S(1)}, bf16[64,16,256]{2,1,0:T(8,128)(2,1)S(1)}, u32[]{:S(2)}, u32[]{:S(2)}) collective-permute-start(bf16[64,16,256]{2,1,0:T(8,128)(2,1)S(1)} %get-tuple-element.64), channel_id=1, source_target_pairs={{0,1},{1,2},{2,3},{4,5},{5,6},{6,7},{8,9},{9,10},{10,11},{12,13},{... | collective-permute-start | bytes 1572872 | tf_op jit(solution)/shard_map/ppermute | solution.py:442
  59.4 15.2 %collective-permute-start.4 = (bf16[64,16,256]{2,1,0:T(8,128)(2,1)S(1)}, bf16[64,16,256]{2,1,0:T(8,128)(2,1)S(1)}, u32[]{:S(2)}, u32[]{:S(2)}) collective-permute-start(bf16[64,16,256]{2,1,0:T(8,128)(2,1)S(1)} %get-tuple-element.65), channel_id=1, source_target_pairs={{1,0},{2,1},{3,2},{5,4},{6,5},{7,6},{9,8},{10,9},{11,10},{13,12},{... | collective-permute-start | bytes 1572872 | tf_op jit(solution)/shard_map/ppermute | solution.py:443
  62.2 12.4 %collective-permute-start.6 = (bf16[288,256]{1,0:T(8,128)(2,1)S(1)}, bf16[288,256]{1,0:T(8,128)(2,1)S(1)}, u32[]{:S(2)}, u32[]{:S(2)}) collective-permute-start(bf16[288,256]{1,0:T(8,128)(2,1)S(1)} %get-tuple-element.74), channel_id=1, source_target_pairs={{0,2},{2,0},{4,6},{6,4},{1,3},{3,1},{5,7},{7,5},{8,10},{10,8},{12,... | collective-permute-start | bytes 442376 | tf_op jit(solution)/shard_map/ppermute | solution.py:514
  62.9 11.8 %collective-permute-start.7 = (bf16[288,256]{1,0:T(8,128)(2,1)S(1)}, bf16[288,256]{1,0:T(8,128)(2,1)S(1)}, u32[]{:S(2)}, u32[]{:S(2)}) collective-permute-start(bf16[288,256]{1,0:T(8,128)(2,1)S(1)} %get-tuple-element.75), channel_id=1, source_target_pairs={{0,4},{2,6},{4,0},{6,2},{1,5},{3,7},{5,1},{7,3},{8,12},{10,14},{12... | collective-permute-start | bytes 442376 | tf_op jit(solution)/shard_map/ppermute | solution.py:514
  64.1 10.5 %collective-permute-start.8 = (bf16[288,256]{1,0:T(8,128)(2,1)S(1)}, bf16[288,256]{1,0:T(8,128)(2,1)S(1)}, u32[]{:S(2)}, u32[]{:S(2)}) collective-permute-start(bf16[288,256]{1,0:T(8,128)(2,1)S(1)} %get-tuple-element.76), channel_id=1, source_target_pairs={{0,6},{2,4},{4,2},{6,0},{1,7},{3,5},{5,3},{7,1},{8,14},{10,12},{12... | collective-permute-start | bytes 442376 | tf_op jit(solution)/shard_map/ppermute | solution.py:514
  73.3 2.7 %collective-permute-start.9 = (bf16[1152,256]{1,0:T(8,128)(2,1)S(1)}, bf16[1152,256]{1,0:T(8,128)(2,1)S(1)}, u32[]{:S(2)}, u32[]{:S(2)}) collective-permute-start(bf16[1152,256]{1,0:T(8,128)(2,1)S(1)} %get-tuple-element.79), channel_id=1, source_target_pairs={{0,1},{1,0},{2,3},{3,2},{4,5},{5,4},{6,7},{7,6},{8,9},{9,8},{10,11... | collective-permute-start | bytes 1769480 | tf_op jit(solution)/shard_map/ppermute | solution.py:586
  74.7 4.1 %collective-permute-start.10 = (bf16[288,256]{1,0:T(8,128)(2,1)S(1)}, bf16[288,256]{1,0:T(8,128)(2,1)S(1)}, u32[]{:S(2)}, u32[]{:S(2)}) collective-permute-start(bf16[288,256]{1,0:T(8,128)(2,1)S(1)} %get-tuple-element.81.refs_1_), channel_id=1, source_target_pairs={{0,8},{8,0},{16,24},{24,16},{1,9},{9,1},{17,25},{25,17},{2,10},{10... | collective-permute-start | bytes 442376 | tf_op jit(solution)/shard_map/ppermute | solution.py:563
  78.8 12.2 %collective-permute-start.14 = (bf16[288,256]{1,0:T(8,128)(2,1)S(1)}, bf16[288,256]{1,0:T(8,128)(2,1)S(1)}, u32[]{:S(2)}, u32[]{:S(2)}) collective-permute-start(bf16[288,256]{1,0:T(8,128)(2,1)S(1)} %get-tuple-element.90.refs_1_), channel_id=1, source_target_pairs={{0,16},{8,24},{16,0},{24,8},{1,17},{9,25},{17,1},{25,9},{2,18},{10... | collective-permute-start | bytes 442376 | tf_op jit(solution)/shard_map/ppermute | solution.py:563
  79.2 10.7 %collective-permute-start.11 = (bf16[288,256]{1,0:T(8,128)(2,1)S(1)}, bf16[288,256]{1,0:T(8,128)(2,1)S(1)}, u32[]{:S(2)}, u32[]{:S(2)}) collective-permute-start(bf16[288,256]{1,0:T(8,128)(2,1)S(1)} %get-tuple-element.86), channel_id=1, source_target_pairs={{0,2},{2,0},{4,6},{6,4},{1,3},{3,1},{5,7},{7,5},{8,10},{10,8},{12,... | collective-permute-start | bytes 442376 | tf_op jit(solution)/shard_map/ppermute | solution.py:514
  82.1 7.8 %collective-permute-start.12 = (bf16[288,256]{1,0:T(8,128)(2,1)S(1)}, bf16[288,256]{1,0:T(8,128)(2,1)S(1)}, u32[]{:S(2)}, u32[]{:S(2)}) collective-permute-start(bf16[288,256]{1,0:T(8,128)(2,1)S(1)} %get-tuple-element.87), channel_id=1, source_target_pairs={{0,4},{2,6},{4,0},{6,2},{1,5},{3,7},{5,1},{7,3},{8,12},{10,14},{12... | collective-permute-start | bytes 442376 | tf_op jit(solution)/shard_map/ppermute | solution.py:514
  83.3 6.6 %collective-permute-start.13 = (bf16[288,256]{1,0:T(8,128)(2,1)S(1)}, bf16[288,256]{1,0:T(8,128)(2,1)S(1)}, u32[]{:S(2)}, u32[]{:S(2)}) collective-permute-start(bf16[288,256]{1,0:T(8,128)(2,1)S(1)} %get-tuple-element.88), channel_id=1, source_target_pairs={{0,6},{2,4},{4,2},{6,0},{1,7},{3,5},{5,3},{7,1},{8,14},{10,12},{12... | collective-permute-start | bytes 442376 | tf_op jit(solution)/shard_map/ppermute | solution.py:514
  90.0 4.1 %collective-permute-start.15 = (bf16[288,256]{1,0:T(8,128)(2,1)S(1)}, bf16[288,256]{1,0:T(8,128)(2,1)S(1)}, u32[]{:S(2)}, u32[]{:S(2)}) collective-permute-start(bf16[288,256]{1,0:T(8,128)(2,1)S(1)} %get-tuple-element.92.refs_1_), channel_id=1, source_target_pairs={{0,8},{8,0},{16,24},{24,16},{1,9},{9,1},{17,25},{25,17},{2,10},{10... | collective-permute-start | bytes 442376 | tf_op jit(solution)/shard_map/ppermute | solution.py:563
  91.1 5.0 %collective-permute-start.18 = (bf16[288,256]{1,0:T(8,128)(2,1)S(1)}, bf16[288,256]{1,0:T(8,128)(2,1)S(1)}, u32[]{:S(2)}, u32[]{:S(2)}) collective-permute-start(bf16[288,256]{1,0:T(8,128)(2,1)S(1)} %get-tuple-element.94.refs_1_), channel_id=1, source_target_pairs={{0,6},{2,4},{4,2},{6,0},{1,7},{3,5},{5,3},{7,1},{8,14},{10,12},{12... | collective-permute-start | bytes 442376 | tf_op jit(solution)/shard_map/ppermute | solution.py:514
  93.5 4.7 %collective-permute-start.17 = (bf16[288,256]{1,0:T(8,128)(2,1)S(1)}, bf16[288,256]{1,0:T(8,128)(2,1)S(1)}, u32[]{:S(2)}, u32[]{:S(2)}) collective-permute-start(bf16[288,256]{1,0:T(8,128)(2,1)S(1)} %get-tuple-element.94.refs_1_), channel_id=1, source_target_pairs={{0,4},{2,6},{4,0},{6,2},{1,5},{3,7},{5,1},{7,3},{8,12},{10,14},{12... | collective-permute-start | bytes 442376 | tf_op jit(solution)/shard_map/ppermute | solution.py:514
  93.8 4.5 %collective-permute-start.16 = (bf16[288,256]{1,0:T(8,128)(2,1)S(1)}, bf16[288,256]{1,0:T(8,128)(2,1)S(1)}, u32[]{:S(2)}, u32[]{:S(2)}) collective-permute-start(bf16[288,256]{1,0:T(8,128)(2,1)S(1)} %get-tuple-element.94.refs_1_), channel_id=1, source_target_pairs={{0,2},{2,0},{4,6},{6,4},{1,3},{3,1},{5,7},{7,5},{8,10},{10,8},{12,... | collective-permute-start | bytes 442376 | tf_op jit(solution)/shard_map/ppermute | solution.py:514
  98.3 16.4 %collective-permute-start.20 = (bf16[4,288,256]{2,1,0:T(8,128)(2,1)S(1)}, bf16[4,288,256]{2,1,0:T(8,128)(2,1)S(1)}, u32[]{:S(2)}, u32[]{:S(2)}) collective-permute-start(bf16[4,288,256]{2,1,0:T(8,128)(2,1)S(1)} %get-tuple-element.98.refs_2_), channel_id=1, source_target_pairs={{0,1},{1,0},{2,3},{3,2},{4,5},{5,4},{6,7},{7,6},{8,9},{9,8},{10,11... | collective-permute-start | bytes 1769480 | tf_op jit(solution)/shard_map/ppermute | solution.py:575
  102.3 9.6 %collective-permute-start.19 = (bf16[288,256]{1,0:T(8,128)(2,1)S(1)}, bf16[288,256]{1,0:T(8,128)(2,1)S(1)}, u32[]{:S(2)}, u32[]{:S(2)}) collective-permute-start(bf16[288,256]{1,0:T(8,128)(2,1)S(1)} %get-tuple-element.96.refs_1_), channel_id=1, source_target_pairs={{0,16},{8,24},{16,0},{24,8},{1,17},{9,25},{17,1},{25,9},{2,18},{10... | collective-permute-start | bytes 442376 | tf_op jit(solution)/shard_map/ppermute | solution.py:563
  112.0 5.6 %collective-permute-start.23 = (bf16[288,256]{1,0:T(8,128)(2,1)S(1)}, bf16[288,256]{1,0:T(8,128)(2,1)S(1)}, u32[]{:S(2)}, u32[]{:S(2)}) collective-permute-start(bf16[288,256]{1,0:T(8,128)(2,1)S(1)} %get-tuple-element.100.refs_1_), channel_id=1, source_target_pairs={{0,6},{2,4},{4,2},{6,0},{1,7},{3,5},{5,3},{7,1},{8,14},{10,12},{12... | collective-permute-start | bytes 442376 | tf_op jit(solution)/shard_map/ppermute | solution.py:514
  113.7 6.7 %collective-permute-start.22 = (bf16[288,256]{1,0:T(8,128)(2,1)S(1)}, bf16[288,256]{1,0:T(8,128)(2,1)S(1)}, u32[]{:S(2)}, u32[]{:S(2)}) collective-permute-start(bf16[288,256]{1,0:T(8,128)(2,1)S(1)} %get-tuple-element.100.refs_1_), channel_id=1, source_target_pairs={{0,4},{2,6},{4,0},{6,2},{1,5},{3,7},{5,1},{7,3},{8,12},{10,14},{12... | collective-permute-start | bytes 442376 | tf_op jit(solution)/shard_map/ppermute | solution.py:514
  113.9 7.6 %collective-permute-start.21 = (bf16[288,256]{1,0:T(8,128)(2,1)S(1)}, bf16[288,256]{1,0:T(8,128)(2,1)S(1)}, u32[]{:S(2)}, u32[]{:S(2)}) collective-permute-start(bf16[288,256]{1,0:T(8,128)(2,1)S(1)} %get-tuple-element.100.refs_1_), channel_id=1, source_target_pairs={{0,2},{2,0},{4,6},{6,4},{1,3},{3,1},{5,7},{7,5},{8,10},{10,8},{12,... | collective-permute-start | bytes 442376 | tf_op jit(solution)/shard_map/ppermute | solution.py:514
  (8 other events, 56.1 us)

commit v3 on v2

--- a/solution.py
+++ b/solution.py
@@ -412,28 +412,27 @@
 
 
 def edge_rows_kernel(places_ref, *refs):
-    first_ref, last_ref = refs[4:]
+    first_ref, last_ref = refs[2:]
     for k in range(2):
-        first_ref[k] = refs[2 * k][:, 0]
-        last_ref[k] = refs[2 * k + 1][:, 0]
+        first_ref[k] = refs[k][:, 0]
+        last_ref[k] = refs[k][:, refs[k].shape[1] - 1]
 
 
 def edge_rows(places, x, cot, block):
     frames, rows, width, c = x.shape
     line = jax.ShapeDtypeStruct((2, frames, width, c), x.dtype)
     line_spec = pl.BlockSpec((2, block, width, c), lambda b: (0, b, 0, 0))
-    first = pl.BlockSpec((block, 1, width, c), lambda b: (b, 0, 0, 0))
-    last = pl.BlockSpec((block, 1, width, c), lambda b: (b, rows - 1, 0, 0))
+    x_spec = pl.BlockSpec((block, rows, width, c), lambda b: (b, 0, 0, 0))
     return pl.pallas_call(
         edge_rows_kernel,
         grid=(frames // block,),
-        in_specs=[SCALARS, first, last, first, last],
+        in_specs=[SCALARS, x_spec, x_spec],
         out_specs=[line_spec, line_spec],
         out_shape=[line, line],
         compiler_params=params(56),
         cost_estimate=cost(0, 2**22),
         name="edge_rows",
-    )(places, x, x, cot, cot)
+    )(places, x, cot)
 
 
 def row_halo(first, last):
@@ -570,8 +569,9 @@
             other, after = swapped(part, bit), [token]
         return part, other, after[0]
 
-    def pack(name, terms, after):
-        packed, token = small_call(pack_kernel, name, [((4,) + part_shape, BF16)], terms, after)
+    def pack(name, terms, after, mib=2):
+        shape = (4,) + part_shape
+        packed, token = small_call(pack_kernel, name, [(shape, BF16)], terms, after, None, mib)
         return packed, lax.ppermute(packed, "core", CORES), token
 
     def merge(name, packed, other, after):
@@ -587,18 +587,18 @@
     out_part, token = sums("out_share", None, [own] + others, [token, low_up, low_down], mib=FAR)
     out_other = swapped(out_part, 1)
     own, others, token = add("in_add", kept, got, [token])
-    out_part, out_other, token = middle("out_mid", out_part, out_other, [token])
     outputs, token = outputs_conv(
         low, low_up, low_down, out_kernel.reshape(3, 3 * p, c), x, skip.reshape(1, c), block, token
     )
+    out_part, out_other, token = middle("out_mid", out_part, out_other, [token])
     in_part, token = sums("in_share", None, [own] + others, [token])
     in_other = swapped(in_part, 1)
-    out_part, token = sums("out_total", grad_scale, [out_part, out_other], [token])
+    in_part, in_other, token = middle("in_mid", in_part, in_other, [token])
+    out_part, token = sums("out_total", grad_scale, [out_part, out_other], [token], mib=FAR)
     out_others = from_others(out_part, ("x", "y"))
-    in_part, in_other, token = middle("in_mid", in_part, in_other, [token])
-    out_packed, out_other, token = pack("out_pack", [out_part] + out_others, [token])
     in_part, token = sums("in_total", grad_scale, [in_part, in_other], [token])
     in_others = from_others(in_part, ("x", "y"))
+    out_packed, out_other, token = pack("out_pack", [out_part] + out_others, [token], FAR)
     out_grad, token = merge("out_merge", out_packed, out_other, [token])
     in_packed, in_other, token = pack("in_pack", [in_part] + in_others, [token])
     in_grad, _ = merge("in_merge", in_packed, in_other, [token])

time: 127 us -> 125 us (0.984)
  waiting for transfers between devices: 28 us -> 26 us
    ppermute x12, waiting for transfers between devices: 8.88 us -> 5.12 us  [from_others(): lax.ppermute(part, axes, [(i, i ^ k) for i in range(count)])]
    ppermute x2, starting transfers between devices: 4.91 us -> 7.82 us  [pack(): return (packed, lax.ppermute(packed, 'core', CORES), token)]
    ppermute x4, starting transfers between devices: 3.72 us -> 1.97 us  [swapped(): return lax.ppermute(part, 'a', [(i, i ^ bit) for i in range(deep)])]
    ppermute x4, waiting for transfers between devices: 10.1 us -> 11.8 us  [swapped(): return lax.ppermute(part, 'a', [(i, i ^ bit) for i in range(deep)])]
  transfers between devices with their start and end apart: 25 -> 25, of which waited for: 13 -> 11; matrix products, arithmetic and copies ran while one was open for 0% -> 0% of each run, Pallas kernels for 23% -> 23%
where the time goes in v3:
time: 125 us
  Pallas kernels  49.7 us (40%)
  starting transfers between devices  36.3 us (29%)
  waiting for transfers between devices  26 us (21%)
  blocking collectives  11 us (9%)
    ppermute x4, waiting for transfers between devices, swapped(): return lax.ppermute(part, 'a', [(i, i ^ bit) for i in range(deep)])  11.8 us
    ppermute x12, starting transfers between devices, from_others(): lax.ppermute(part, axes, [(i, i ^ k) for i in range(count)])  11.1 us
    all_to_all x1, blocking collectives, per_device(): ends = lax.all_to_all(ends, 'a', 0, 0)  11 us
    ppermute x2, starting transfers between devices, row_halo(): up = lax.ppermute(last, axes, [(i, i + 1) for i in range(count - 1)])  8.96 us
    pallas_call x1, Pallas kernels, kernel_grads(): pl.pallas_call(in_grad_kernel, grid=(frames // block,), in_specs=lead + [...  8.41 us
    pallas_call x1, Pallas kernels, kernel_grads(): pl.pallas_call(out_grad_kernel, grid=(frames // block,), in_specs=lead +...  7.87 us
    ppermute x2, starting transfers between devices, pack(): return (packed, lax.ppermute(packed, 'core', CORES), token)  7.82 us
    pallas_call x13, Pallas kernels, small_call(): pl.pallas_call(kernel, in_specs=[ANYWHERE] * len(after) + [SCALARS] * len...  7.1 us
  transfers between devices with their start and end apart: 25, of which 11 were waited for; matrix products, arithmetic and copies ran while one was open for 0% of the time, Pallas kernels for 23%

profile of v3, /device:TPU:1, one launch (start us, length us, event | category | flops | bytes accessed | tf_op | source)
XLA Modules:
  0.0 124.6 jit_solution(17915792108813698021)
XLA Ops:
  1.3 4.4 %edge_rows.1 = (bf16[2,64,16,256]{3,2,1,0:T(8,128)(2,1)}, bf16[2,64,16,256]{3,2,1,0:T(8,128)(2,1)}) custom-call(s32[4]{0:T(128)} %pad_add_fusion.places_ref.refs_0_.place_ref.refs_1_, bf16[64,4,16,256]{3,2,1,0:T(8,128)(2,1)} %bitcast.15, bf16[64,4,16,256]{3,2,1,0:T(8,128)(2,1)} %bitcast.12), custom_call_target="tpu_custom_call" | custom-call | bytes 4194304 | tf_op jit(solution)/shard_map/edge_rows/pallas_call | solution.py:426
  5.7 4.5 %collective-permute-start = (bf16[2,64,16,256]{3,2,1,0:T(8,128)(2,1)}, bf16[2,64,16,256]{3,2,1,0:T(8,128)(2,1)S(1)}, u32[]{:S(2)}, u32[]{:S(2)}) collective-permute-start(bf16[2,64,16,256]{3,2,1,0:T(8,128)(2,1)} %get-tuple-element.55), channel_id=1, source_target_pairs={{0,1},{1,2},{2,3},{4,5},{5,6},{6,7},{8,9},{9,10},{10,11},{12,13},{... | collective-permute-start | bytes 3145736 | tf_op jit(solution)/shard_map/ppermute | solution.py:441
  10.2 1.9 %collective-permute-start.1 = (bf16[2,64,16,256]{3,2,1,0:T(8,128)(2,1)}, bf16[2,64,16,256]{3,2,1,0:T(8,128)(2,1)S(1)}, u32[]{:S(2)}, u32[]{:S(2)}) collective-permute-start(bf16[2,64,16,256]{3,2,1,0:T(8,128)(2,1)} %get-tuple-element.56), channel_id=1, source_target_pairs={{1,0},{2,1},{3,2},{5,4},{6,5},{7,6},{9,8},{10,9},{11,10},{13,12},{... | collective-permute-start | bytes 3145736 | tf_op jit(solution)/shard_map/ppermute | solution.py:442
  12.2 5.1 %interior_in.1.part_ref = f32[4,64,16,256]{3,2,1,0:T(8,128)S(1)} custom-call(bf16[64,4,16,256]{3,2,1,0:T(8,128)(2,1)S(1)} %bitcast.16, bf16[3,768,256]{2,1,0:T(8,128)(2,1)S(1)} %bitcast.19), custom_call_target="tpu_custom_call" | custom-call | flops 4831838208 | bytes 8388608 | tf_op jit(solution)/shard_map/interior_in/pallas_call | solution.py:106
  17.3 5.5 %interior_cot.1 = (f32[4,64,16,256]{3,2,1,0:T(8,128)S(1)}, bf16[3,768,256]{2,1,0:T(8,128)(2,1)S(1)}) custom-call(bf16[64,4,16,256]{3,2,1,0:T(8,128)(2,1)S(1)} %bitcast.13, bf16[3,3,256,256]{3,2,1,0:T(8,128)(2,1)S(1)} %copy-done.5), custom_call_target="tpu_custom_call" | custom-call | flops 4831838208 | bytes 8388608 | tf_op jit(solution)/shard_map/interior_cot/pallas_call | solution.py:91
  22.8 3.8 %collective-permute-done.1.down_ref = bf16[2,64,16,256]{3,2,1,0:T(8,128)(2,1)S(1)} collective-permute-done((bf16[2,64,16,256]{3,2,1,0:T(8,128)(2,1)}, bf16[2,64,16,256]{3,2,1,0:T(8,128)(2,1)S(1)}, u32[]{:S(2)}, u32[]{:S(2)}) %collective-permute-start.1) | collective-permute-done | bytes 1048608 | tf_op jit(solution)/shard_map/ppermute | solution.py:442
  26.5 2.3 %scan_fwd.1 = (f32[4,64,16,256]{3,2,1,0:T(8,128)S(1)}, f32[64,256]{1,0:T(8,128)S(1)}, f32[64,256]{1,0:T(8,128)S(1)}) custom-call(f32[4,64,16,256]{3,2,1,0:T(8,128)S(1)} %interior_in.1.part_ref, bf16[2,64,16,256]{3,2,1,0:T(8,128)(2,1)S(1)} %collective-permute-done.up_ref, bf16[2,64,16,256]{3,2,1,0:T(8,128)(2,1)S(1)} %collective-permute-done.1.down_ref, ...), custom_call_target="tpu_custom_call" | custom-call | flops 805306368 | bytes 12582912 | tf_op jit(solution)/shard_map/scan_fwd/pallas_call | solution.py:180
  28.8 2.6 %scan_back.1 = (f32[4,64,16,256]{3,2,1,0:T(8,128)S(1)}, f32[64,256]{1,0:T(8,128)S(1)}, f32[136,256]{1,0:T(8,128)S(1)}) custom-call(f32[4,64,16,256]{3,2,1,0:T(8,128)S(1)} %get-tuple-element.54.part_ref, bf16[2,64,16,256]{3,2,1,0:T(8,128)(2,1)S(1)} %collective-permute-done.up_ref, bf16[2,64,16,256]{3,2,1,0:T(8,128)(2,1)S(1)} %collective-permute-done.1.down_ref, ...), custom_call_target="tpu_custom_call" | custom-call | flops 805306368 | bytes 12582912 | tf_op jit(solution)/shard_map/scan_back/pallas_call | solution.py:180
  32.7 2.7 %collective-permute-done.2.refs_2_.pair_ref = f32[136,256]{1,0:T(8,128)S(1)} collective-permute-done((f32[136,256]{1,0:T(8,128)S(1)}, f32[136,256]{1,0:T(8,128)S(1)}, u32[]{:S(2)}, u32[]{:S(2)}) %collective-permute-start.2) | collective-permute-done | bytes 139296 | tf_op jit(solution)/shard_map/ppermute | solution.py:538
  36.5 11.0 %all_to_all.5.ends_ref = f32[4,72,256]{2,1,0:T(8,128)S(1)} all-to-all(f32[4,72,256]{2,1,0:T(8,128)S(1)} %get-tuple-element.60), channel_id=1, replica_groups=mesh['a'=4,'x'=2,'y'=2,'core'=2] {'a'}, dimensions={0} | all-to-all | bytes 589824 | tf_op jit(solution)/shard_map/all_to_all | solution.py:542
  47.5 7.9 %out_grad.1 = (bf16[4,64,16,256]{3,2,1,0:T(8,128)(2,1)S(1)}, bf16[64,16,256]{2,1,0:T(8,128)(2,1)S(1)}, bf16[64,16,256]{2,1,0:T(8,128)(2,1)S(1)}, bf16[1152,256]{...) custom-call(s32[4]{0:T(128)S(1)} %copy-done.4, f32[4,72,256]{2,1,0:T(8,128)S(1)} %all_to_all.5.ends_ref, ...), custom_call_target="tpu_custom_call" | custom-call | flops 4831838208 | bytes 10485760 | tf_op jit(solution)/shard_map/out_grad/pallas_call | solution.py:349
  55.4 4.4 %collective-permute-start.3 = (bf16[64,16,256]{2,1,0:T(8,128)(2,1)S(1)}, bf16[64,16,256]{2,1,0:T(8,128)(2,1)S(1)}, u32[]{:S(2)}, u32[]{:S(2)}) collective-permute-start(bf16[64,16,256]{2,1,0:T(8,128)(2,1)S(1)} %get-tuple-element.64), channel_id=1, source_target_pairs={{0,1},{1,2},{2,3},{4,5},{5,6},{6,7},{8,9},{9,10},{10,11},{12,13},{... | collective-permute-start | bytes 1572872 | tf_op jit(solution)/shard_map/ppermute | solution.py:441
  59.9 2.1 %collective-permute-start.4 = (bf16[64,16,256]{2,1,0:T(8,128)(2,1)S(1)}, bf16[64,16,256]{2,1,0:T(8,128)(2,1)S(1)}, u32[]{:S(2)}, u32[]{:S(2)}) collective-permute-start(bf16[64,16,256]{2,1,0:T(8,128)(2,1)S(1)} %get-tuple-element.65), channel_id=1, source_target_pairs={{1,0},{2,1},{3,2},{5,4},{6,5},{7,6},{9,8},{10,9},{11,10},{13,12},{... | collective-permute-start | bytes 1572872 | tf_op jit(solution)/shard_map/ppermute | solution.py:442
  65.4 8.4 %in_grad.1 = (bf16[1152,256]{1,0:T(8,128)(2,1)S(1)}, f32[1152,256]{1,0:T(8,128)S(1)}, f32[8,128]{1,0:T(8,128)S(1)}) custom-call(s32[4]{0:T(128)S(1)} %copy-done.4, f32[4,72,256]{2,1,0:T(8,128)S(1)} %all_to_all.5.ends_ref, f32[136,256]{1,0:T(8,128)S(1)} %collective-permute-done.2.refs_2_.pair_ref, f32[4,64,16,256]{3,2,1,0:T(8,128)S(1)} %get-tuple-element.66.local_ref, ...), custom_call_target="tpu_custom_call" | custom-call | flops 4831838208 | bytes 10485760 | tf_op jit(solution)/shard_map/in_grad/pallas_call | solution.py:360
  77.2 1.7 %collective-permute-start.11 = (bf16[288,256]{1,0:T(8,128)(2,1)S(1)}, bf16[288,256]{1,0:T(8,128)(2,1)S(1)}, u32[]{:S(2)}, u32[]{:S(2)}) collective-permute-start(bf16[288,256]{1,0:T(8,128)(2,1)S(1)} %get-tuple-element.86), channel_id=1, source_target_pairs={{0,2},{2,0},{4,6},{6,4},{1,3},{3,1},{5,7},{7,5},{8,10},{10,8},{12,... | collective-permute-start | bytes 442376 | tf_op jit(solution)/shard_map/ppermute | solution.py:513
  80.2 6.6 %outputs_conv.1 = (bf16[64,4,16,256]{3,2,1,0:T(8,128)(2,1)}, f32[8,128]{1,0:T(8,128)S(1)}) custom-call(bf16[4,64,16,256]{3,2,1,0:T(8,128)(2,1)S(1)} %get-tuple-element.63.low_ref, bf16[64,16,256]{2,1,0:T(8,128)(2,1)S(1)} %collective-permute-done.3.refs_1_.up_ref, bf16[64,16,256]{2,1,0:T(8,128)(2,1)S(1)} %collective-permute-done.4.refs_2_.down_ref, ...), custom_call_target="tpu_custom_call" | custom-call | flops 4831838208 | bytes 8388608 | tf_op jit(solution)/shard_map/outputs_conv/pallas_call | solution.py:393
  88.3 3.5 %collective-permute-done.14.refs_2_ = bf16[288,256]{1,0:T(8,128)(2,1)S(1)} collective-permute-done((bf16[288,256]{1,0:T(8,128)(2,1)S(1)}, bf16[288,256]{1,0:T(8,128)(2,1)S(1)}, u32[]{:S(2)}, u32[]{:S(2)}) %collective-permute-start.14) | collective-permute-done | bytes 147488 | tf_op jit(solution)/shard_map/ppermute | solution.py:562
  92.0 2.0 %collective-permute-done.15.refs_2_ = bf16[288,256]{1,0:T(8,128)(2,1)S(1)} collective-permute-done((bf16[288,256]{1,0:T(8,128)(2,1)S(1)}, bf16[288,256]{1,0:T(8,128)(2,1)S(1)}, u32[]{:S(2)}, u32[]{:S(2)}) %collective-permute-start.15) | collective-permute-done | bytes 147488 | tf_op jit(solution)/shard_map/ppermute | solution.py:562
  94.1 2.1 %collective-permute-start.19 = (bf16[288,256]{1,0:T(8,128)(2,1)S(1)}, bf16[288,256]{1,0:T(8,128)(2,1)S(1)}, u32[]{:S(2)}, u32[]{:S(2)}) collective-permute-start(bf16[288,256]{1,0:T(8,128)(2,1)S(1)} %get-tuple-element.96.refs_1_), channel_id=1, source_target_pairs={{0,6},{2,4},{4,2},{6,0},{1,7},{3,5},{5,3},{7,1},{8,14},{10,12},{12... | collective-permute-start | bytes 442376 | tf_op jit(solution)/shard_map/ppermute | solution.py:513
  96.8 6.2 %collective-permute-done.16.refs_2_ = bf16[288,256]{1,0:T(8,128)(2,1)S(1)} collective-permute-done((bf16[288,256]{1,0:T(8,128)(2,1)S(1)}, bf16[288,256]{1,0:T(8,128)(2,1)S(1)}, u32[]{:S(2)}, u32[]{:S(2)}) %collective-permute-start.16) | collective-permute-done | bytes 147488 | tf_op jit(solution)/shard_map/ppermute | solution.py:562
  103.1 7.3 %collective-permute-start.20 = (bf16[4,288,256]{2,1,0:T(8,128)(2,1)S(1)}, bf16[4,288,256]{2,1,0:T(8,128)(2,1)S(1)}, u32[]{:S(2)}, u32[]{:S(2)}) collective-permute-start(bf16[4,288,256]{2,1,0:T(8,128)(2,1)S(1)} %get-tuple-element.98.refs_2_), channel_id=1, source_target_pairs={{0,1},{1,0},{2,3},{3,2},{4,5},{5,4},{6,7},{7,6},{8,9},{9,8},{10,11... | collective-permute-start | bytes 1769480 | tf_op jit(solution)/shard_map/ppermute | solution.py:575
  113.1 2.1 %out_merge.1 = (f32[2304,256]{1,0:T(8,128)}, f32[8,128]{1,0:T(8,128)S(1)}) custom-call(f32[8,128]{1,0:T(8,128)S(1)} %get-tuple-element.97.refs_0_, s32[4]{0:T(128)S(1)} %copy-done.4, bf16[4,288,256]{2,1,0:T(8,128)(2,1)S(1)} %get-tuple-element.98.refs_2_, bf16[4,288,256]{2,1,0:T(8,128)(2,1)S(1)} %collective-permute-done.20.refs_3_), custom_call_target="tpu_custom_call" | custom-call | flops 1073741824 | bytes 2097152 | tf_op jit(solution)/shard_map/out_merge/pallas_call | solution.py:458
  116.7 2.7 %collective-permute-done.22.refs_3_ = bf16[288,256]{1,0:T(8,128)(2,1)S(1)} collective-permute-done((bf16[288,256]{1,0:T(8,128)(2,1)S(1)}, bf16[288,256]{1,0:T(8,128)(2,1)S(1)}, u32[]{:S(2)}, u32[]{:S(2)}) %collective-permute-start.22) | collective-permute-done | bytes 147488 | tf_op jit(solution)/shard_map/ppermute | solution.py:513
  122.5 2.1 %in_merge.1 = (f32[2304,256]{1,0:T(8,128)}, f32[8,128]{1,0:T(8,128)}) custom-call(f32[8,128]{1,0:T(8,128)S(1)} %get-tuple-element.101.refs_0_, s32[4]{0:T(128)S(1)} %copy-done.4, bf16[4,288,256]{2,1,0:T(8,128)(2,1)S(1)} %get-tuple-element.102.refs_2_, bf16[4,288,256]{2,1,0:T(8,128)(2,1)S(1)} %collective-permute-done.24.refs_3_), custom_call_target="tpu_custom_call" | custom-call | flops 1073741824 | bytes 2097152 | tf_op jit(solution)/shard_map/in_merge/pallas_call | solution.py:458
  (63 shorter events, 20.9 us)
Async XLA Ops:
  5.7 17.1 %collective-permute-start = (bf16[2,64,16,256]{3,2,1,0:T(8,128)(2,1)}, bf16[2,64,16,256]{3,2,1,0:T(8,128)(2,1)S(1)}, u32[]{:S(2)}, u32[]{:S(2)}) collective-permute-start(bf16[2,64,16,256]{3,2,1,0:T(8,128)(2,1)} %get-tuple-element.55), channel_id=1, source_target_pairs={{0,1},{1,2},{2,3},{4,5},{5,6},{6,7},{8,9},{9,10},{10,11},{12,13},{... | collective-permute-start | bytes 3145736 | tf_op jit(solution)/shard_map/ppermute | solution.py:441
  10.2 16.3 %collective-permute-start.1 = (bf16[2,64,16,256]{3,2,1,0:T(8,128)(2,1)}, bf16[2,64,16,256]{3,2,1,0:T(8,128)(2,1)S(1)}, u32[]{:S(2)}, u32[]{:S(2)}) collective-permute-start(bf16[2,64,16,256]{3,2,1,0:T(8,128)(2,1)} %get-tuple-element.56), channel_id=1, source_target_pairs={{1,0},{2,1},{3,2},{5,4},{6,5},{7,6},{9,8},{10,9},{11,10},{13,12},{... | collective-permute-start | bytes 3145736 | tf_op jit(solution)/shard_map/ppermute | solution.py:442
  31.4 4.0 %collective-permute-start.2 = (f32[136,256]{1,0:T(8,128)S(1)}, f32[136,256]{1,0:T(8,128)S(1)}, u32[]{:S(2)}, u32[]{:S(2)}) collective-permute-start(f32[136,256]{1,0:T(8,128)S(1)} %get-tuple-element.59.refs_1_), channel_id=1, source_target_pairs={{0,4},{4,0},{1,5},{5,1},{2,6},{6,2},{3,7},{7,3},{8,12},{12,8},{9,1... | collective-permute-start | bytes 417800 | tf_op jit(solution)/shard_map/ppermute | solution.py:538
  55.3 6.6 %collective-permute-start.5 = (bf16[1152,256]{1,0:T(8,128)(2,1)S(1)}, bf16[1152,256]{1,0:T(8,128)(2,1)S(1)}, u32[]{:S(2)}, u32[]{:S(2)}) collective-permute-start(bf16[1152,256]{1,0:T(8,128)(2,1)S(1)} %get-tuple-element.70), channel_id=1, source_target_pairs={{0,1},{1,0},{2,3},{3,2},{4,5},{5,4},{6,7},{7,6},{8,9},{9,8},{10,11... | collective-permute-start | bytes 1769480 | tf_op jit(solution)/shard_map/ppermute | solution.py:547
  55.4 18.4 %collective-permute-start.3 = (bf16[64,16,256]{2,1,0:T(8,128)(2,1)S(1)}, bf16[64,16,256]{2,1,0:T(8,128)(2,1)S(1)}, u32[]{:S(2)}, u32[]{:S(2)}) collective-permute-start(bf16[64,16,256]{2,1,0:T(8,128)(2,1)S(1)} %get-tuple-element.64), channel_id=1, source_target_pairs={{0,1},{1,2},{2,3},{4,5},{5,6},{6,7},{8,9},{9,10},{10,11},{12,13},{... | collective-permute-start | bytes 1572872 | tf_op jit(solution)/shard_map/ppermute | solution.py:441
  59.9 15.2 %collective-permute-start.4 = (bf16[64,16,256]{2,1,0:T(8,128)(2,1)S(1)}, bf16[64,16,256]{2,1,0:T(8,128)(2,1)S(1)}, u32[]{:S(2)}, u32[]{:S(2)}) collective-permute-start(bf16[64,16,256]{2,1,0:T(8,128)(2,1)S(1)} %get-tuple-element.65), channel_id=1, source_target_pairs={{1,0},{2,1},{3,2},{5,4},{6,5},{7,6},{9,8},{10,9},{11,10},{13,12},{... | collective-permute-start | bytes 1572872 | tf_op jit(solution)/shard_map/ppermute | solution.py:442
  62.6 12.4 %collective-permute-start.6 = (bf16[288,256]{1,0:T(8,128)(2,1)S(1)}, bf16[288,256]{1,0:T(8,128)(2,1)S(1)}, u32[]{:S(2)}, u32[]{:S(2)}) collective-permute-start(bf16[288,256]{1,0:T(8,128)(2,1)S(1)} %get-tuple-element.74), channel_id=1, source_target_pairs={{0,2},{2,0},{4,6},{6,4},{1,3},{3,1},{5,7},{7,5},{8,10},{10,8},{12,... | collective-permute-start | bytes 442376 | tf_op jit(solution)/shard_map/ppermute | solution.py:513
  63.3 11.8 %collective-permute-start.7 = (bf16[288,256]{1,0:T(8,128)(2,1)S(1)}, bf16[288,256]{1,0:T(8,128)(2,1)S(1)}, u32[]{:S(2)}, u32[]{:S(2)}) collective-permute-start(bf16[288,256]{1,0:T(8,128)(2,1)S(1)} %get-tuple-element.75), channel_id=1, source_target_pairs={{0,4},{2,6},{4,0},{6,2},{1,5},{3,7},{5,1},{7,3},{8,12},{10,14},{12... | collective-permute-start | bytes 442376 | tf_op jit(solution)/shard_map/ppermute | solution.py:513
  64.5 10.6 %collective-permute-start.8 = (bf16[288,256]{1,0:T(8,128)(2,1)S(1)}, bf16[288,256]{1,0:T(8,128)(2,1)S(1)}, u32[]{:S(2)}, u32[]{:S(2)}) collective-permute-start(bf16[288,256]{1,0:T(8,128)(2,1)S(1)} %get-tuple-element.76), channel_id=1, source_target_pairs={{0,6},{2,4},{4,2},{6,0},{1,7},{3,5},{5,3},{7,1},{8,14},{10,12},{12... | collective-permute-start | bytes 442376 | tf_op jit(solution)/shard_map/ppermute | solution.py:513
  73.8 2.7 %collective-permute-start.9 = (bf16[1152,256]{1,0:T(8,128)(2,1)S(1)}, bf16[1152,256]{1,0:T(8,128)(2,1)S(1)}, u32[]{:S(2)}, u32[]{:S(2)}) collective-permute-start(bf16[1152,256]{1,0:T(8,128)(2,1)S(1)} %get-tuple-element.79), channel_id=1, source_target_pairs={{0,1},{1,0},{2,3},{3,2},{4,5},{5,4},{6,7},{7,6},{8,9},{9,8},{10,11... | collective-permute-start | bytes 1769480 | tf_op jit(solution)/shard_map/ppermute | solution.py:586
  75.2 11.6 %collective-permute-start.10 = (bf16[288,256]{1,0:T(8,128)(2,1)S(1)}, bf16[288,256]{1,0:T(8,128)(2,1)S(1)}, u32[]{:S(2)}, u32[]{:S(2)}) collective-permute-start(bf16[288,256]{1,0:T(8,128)(2,1)S(1)} %get-tuple-element.83.refs_1_), channel_id=1, source_target_pairs={{0,8},{8,0},{16,24},{24,16},{1,9},{9,1},{17,25},{25,17},{2,10},{10... | collective-permute-start | bytes 442376 | tf_op jit(solution)/shard_map/ppermute | solution.py:562
  77.2 9.6 %collective-permute-start.11 = (bf16[288,256]{1,0:T(8,128)(2,1)S(1)}, bf16[288,256]{1,0:T(8,128)(2,1)S(1)}, u32[]{:S(2)}, u32[]{:S(2)}) collective-permute-start(bf16[288,256]{1,0:T(8,128)(2,1)S(1)} %get-tuple-element.86), channel_id=1, source_target_pairs={{0,2},{2,0},{4,6},{6,4},{1,3},{3,1},{5,7},{7,5},{8,10},{10,8},{12,... | collective-permute-start | bytes 442376 | tf_op jit(solution)/shard_map/ppermute | solution.py:513
  78.9 7.9 %collective-permute-start.12 = (bf16[288,256]{1,0:T(8,128)(2,1)S(1)}, bf16[288,256]{1,0:T(8,128)(2,1)S(1)}, u32[]{:S(2)}, u32[]{:S(2)}) collective-permute-start(bf16[288,256]{1,0:T(8,128)(2,1)S(1)} %get-tuple-element.87), channel_id=1, source_target_pairs={{0,4},{2,6},{4,0},{6,2},{1,5},{3,7},{5,1},{7,3},{8,12},{10,14},{12... | collective-permute-start | bytes 442376 | tf_op jit(solution)/shard_map/ppermute | solution.py:513
  80.1 6.8 %collective-permute-start.13 = (bf16[288,256]{1,0:T(8,128)(2,1)S(1)}, bf16[288,256]{1,0:T(8,128)(2,1)S(1)}, u32[]{:S(2)}, u32[]{:S(2)}) collective-permute-start(bf16[288,256]{1,0:T(8,128)(2,1)S(1)} %get-tuple-element.88), channel_id=1, source_target_pairs={{0,6},{2,4},{4,2},{6,0},{1,7},{3,5},{5,3},{7,1},{8,14},{10,12},{12... | collective-permute-start | bytes 442376 | tf_op jit(solution)/shard_map/ppermute | solution.py:513
  87.0 4.9 %collective-permute-start.14 = (bf16[288,256]{1,0:T(8,128)(2,1)S(1)}, bf16[288,256]{1,0:T(8,128)(2,1)S(1)}, u32[]{:S(2)}, u32[]{:S(2)}) collective-permute-start(bf16[288,256]{1,0:T(8,128)(2,1)S(1)} %get-tuple-element.90.refs_1_), channel_id=1, source_target_pairs={{0,8},{8,0},{16,24},{24,16},{1,9},{9,1},{17,25},{25,17},{2,10},{10... | collective-permute-start | bytes 442376 | tf_op jit(solution)/shard_map/ppermute | solution.py:562
  87.5 6.6 %collective-permute-start.15 = (bf16[288,256]{1,0:T(8,128)(2,1)S(1)}, bf16[288,256]{1,0:T(8,128)(2,1)S(1)}, u32[]{:S(2)}, u32[]{:S(2)}) collective-permute-start(bf16[288,256]{1,0:T(8,128)(2,1)S(1)} %get-tuple-element.92.refs_1_), channel_id=1, source_target_pairs={{0,16},{8,24},{16,0},{24,8},{1,17},{9,25},{17,1},{25,9},{2,18},{10... | collective-permute-start | bytes 442376 | tf_op jit(solution)/shard_map/ppermute | solution.py:562
  91.9 11.1 %collective-permute-start.16 = (bf16[288,256]{1,0:T(8,128)(2,1)S(1)}, bf16[288,256]{1,0:T(8,128)(2,1)S(1)}, u32[]{:S(2)}, u32[]{:S(2)}) collective-permute-start(bf16[288,256]{1,0:T(8,128)(2,1)S(1)} %get-tuple-element.94.refs_1_), channel_id=1, source_target_pairs={{0,16},{8,24},{16,0},{24,8},{1,17},{9,25},{17,1},{25,9},{2,18},{10... | collective-permute-start | bytes 442376 | tf_op jit(solution)/shard_map/ppermute | solution.py:562
  94.1 9.0 %collective-permute-start.19 = (bf16[288,256]{1,0:T(8,128)(2,1)S(1)}, bf16[288,256]{1,0:T(8,128)(2,1)S(1)}, u32[]{:S(2)}, u32[]{:S(2)}) collective-permute-start(bf16[288,256]{1,0:T(8,128)(2,1)S(1)} %get-tuple-element.96.refs_1_), channel_id=1, source_target_pairs={{0,6},{2,4},{4,2},{6,0},{1,7},{3,5},{5,3},{7,1},{8,14},{10,12},{12... | collective-permute-start | bytes 442376 | tf_op jit(solution)/shard_map/ppermute | solution.py:513
  96.2 6.9 %collective-permute-start.18 = (bf16[288,256]{1,0:T(8,128)(2,1)S(1)}, bf16[288,256]{1,0:T(8,128)(2,1)S(1)}, u32[]{:S(2)}, u32[]{:S(2)}) collective-permute-start(bf16[288,256]{1,0:T(8,128)(2,1)S(1)} %get-tuple-element.96.refs_1_), channel_id=1, source_target_pairs={{0,4},{2,6},{4,0},{6,2},{1,5},{3,7},{5,1},{7,3},{8,12},{10,14},{12... | collective-permute-start | bytes 442376 | tf_op jit(solution)/shard_map/ppermute | solution.py:513
  96.4 6.6 %collective-permute-start.17 = (bf16[288,256]{1,0:T(8,128)(2,1)S(1)}, bf16[288,256]{1,0:T(8,128)(2,1)S(1)}, u32[]{:S(2)}, u32[]{:S(2)}) collective-permute-start(bf16[288,256]{1,0:T(8,128)(2,1)S(1)} %get-tuple-element.96.refs_1_), channel_id=1, source_target_pairs={{0,2},{2,0},{4,6},{6,4},{1,3},{3,1},{5,7},{7,5},{8,10},{10,8},{12,... | collective-permute-start | bytes 442376 | tf_op jit(solution)/shard_map/ppermute | solution.py:513
  103.1 9.9 %collective-permute-start.20 = (bf16[4,288,256]{2,1,0:T(8,128)(2,1)S(1)}, bf16[4,288,256]{2,1,0:T(8,128)(2,1)S(1)}, u32[]{:S(2)}, u32[]{:S(2)}) collective-permute-start(bf16[4,288,256]{2,1,0:T(8,128)(2,1)S(1)} %get-tuple-element.98.refs_2_), channel_id=1, source_target_pairs={{0,1},{1,0},{2,3},{3,2},{4,5},{5,4},{6,7},{7,6},{8,9},{9,8},{10,11... | collective-permute-start | bytes 1769480 | tf_op jit(solution)/shard_map/ppermute | solution.py:575
  110.4 6.3 %collective-permute-start.23 = (bf16[288,256]{1,0:T(8,128)(2,1)S(1)}, bf16[288,256]{1,0:T(8,128)(2,1)S(1)}, u32[]{:S(2)}, u32[]{:S(2)}) collective-permute-start(bf16[288,256]{1,0:T(8,128)(2,1)S(1)} %get-tuple-element.100.refs_1_), channel_id=1, source_target_pairs={{0,6},{2,4},{4,2},{6,0},{1,7},{3,5},{5,3},{7,1},{8,14},{10,12},{12... | collective-permute-start | bytes 442376 | tf_op jit(solution)/shard_map/ppermute | solution.py:513
  112.1 7.4 %collective-permute-start.22 = (bf16[288,256]{1,0:T(8,128)(2,1)S(1)}, bf16[288,256]{1,0:T(8,128)(2,1)S(1)}, u32[]{:S(2)}, u32[]{:S(2)}) collective-permute-start(bf16[288,256]{1,0:T(8,128)(2,1)S(1)} %get-tuple-element.100.refs_1_), channel_id=1, source_target_pairs={{0,4},{2,6},{4,0},{6,2},{1,5},{3,7},{5,1},{7,3},{8,12},{10,14},{12... | collective-permute-start | bytes 442376 | tf_op jit(solution)/shard_map/ppermute | solution.py:513
  112.3 7.9 %collective-permute-start.21 = (bf16[288,256]{1,0:T(8,128)(2,1)S(1)}, bf16[288,256]{1,0:T(8,128)(2,1)S(1)}, u32[]{:S(2)}, u32[]{:S(2)}) collective-permute-start(bf16[288,256]{1,0:T(8,128)(2,1)S(1)} %get-tuple-element.100.refs_1_), channel_id=1, source_target_pairs={{0,2},{2,0},{4,6},{6,4},{1,3},{3,1},{5,7},{7,5},{8,10},{10,8},{12,... | collective-permute-start | bytes 442376 | tf_op jit(solution)/shard_map/ppermute | solution.py:513
  (8 other events, 54.9 us)

commit v4 on v2

--- a/solution.py
+++ b/solution.py
@@ -564,20 +564,20 @@
 
     bits = [2**k for k in range(deep.bit_length() - 1)]
 
-    def middle(name, part, other, after):
+    def middle(name, part, other, after, mib=2):
         for bit in bits[1:]:
-            part, token = sums(name, None, [part, other], after)
+            part, token = sums(name, None, [part, other], after, mib)
             other, after = swapped(part, bit), [token]
         return part, other, after[0]
 
-    def pack(name, terms, after):
-        packed, token = small_call(pack_kernel, name, [((4,) + part_shape, BF16)], terms, after)
+    def pack(name, terms, after, mib=2):
+        shape = (4,) + part_shape
+        packed, token = small_call(pack_kernel, name, [(shape, BF16)], terms, after, None, mib)
         return packed, lax.ppermute(packed, "core", CORES), token
 
-    def merge(name, packed, other, after):
-        return small_call(
-            merge_kernel, name, [((2 * half, q), F32)], [packed, other], after, places
-        )
+    def merge(name, packed, other, after, mib=2):
+        shapes = [((2 * half, q), F32)]
+        return small_call(merge_kernel, name, shapes, [packed, other], after, places, mib)
 
     own, others, token = add("out_add", kept, got, [token])
     sent, kept, token = kernel_grads(
@@ -587,19 +587,19 @@
     out_part, token = sums("out_share", None, [own] + others, [token, low_up, low_down], mib=FAR)
     out_other = swapped(out_part, 1)
     own, others, token = add("in_add", kept, got, [token])
-    out_part, out_other, token = middle("out_mid", out_part, out_other, [token])
+    out_part, out_other, token = middle("out_mid", out_part, out_other, [token], FAR)
+    in_part, token = sums("in_share", None, [own] + others, [token])
+    in_other = swapped(in_part, 1)
+    out_part, token = sums("out_total", grad_scale, [out_part, out_other], [token], mib=FAR)
+    out_others = from_others(out_part, ("x", "y"))
+    in_part, in_other, token = middle("in_mid", in_part, in_other, [token])
     outputs, token = outputs_conv(
         low, low_up, low_down, out_kernel.reshape(3, 3 * p, c), x, skip.reshape(1, c), block, token
     )
-    in_part, token = sums("in_share", None, [own] + others, [token])
-    in_other = swapped(in_part, 1)
-    out_part, token = sums("out_total", grad_scale, [out_part, out_other], [token])
-    out_others = from_others(out_part, ("x", "y"))
-    in_part, in_other, token = middle("in_mid", in_part, in_other, [token])
-    out_packed, out_other, token = pack("out_pack", [out_part] + out_others, [token])
     in_part, token = sums("in_total", grad_scale, [in_part, in_other], [token])
     in_others = from_others(in_part, ("x", "y"))
-    out_grad, token = merge("out_merge", out_packed, out_other, [token])
+    out_packed, out_other, token = pack("out_pack", [out_part] + out_others, [token])
+    out_grad, token = merge("out_merge", out_packed, out_other, [token], FAR)
     in_packed, in_other, token = pack("in_pack", [in_part] + in_others, [token])
     in_grad, _ = merge("in_merge", in_packed, in_other, [token])
     return (

time: 127 us -> 117 us (0.921)
  waiting for transfers between devices: 28 us -> 20.9 us
  starting transfers between devices: 36.4 us -> 33.9 us
    ppermute x4, waiting for transfers between devices: 10.1 us -> 0.59 us  [swapped(): return lax.ppermute(part, 'a', [(i, i ^ bit) for i in range(deep)])]
    ppermute x4, starting transfers between devices: 3.72 us -> 1.07 us  [swapped(): return lax.ppermute(part, 'a', [(i, i ^ bit) for i in range(deep)])]
    ppermute x12, waiting for transfers between devices: 8.88 us -> 11.3 us  [from_others(): lax.ppermute(part, axes, [(i, i ^ k) for i in range(count)])]
    ppermute x12, starting transfers between devices: 12.3 us -> 14.6 us  [from_others(): lax.ppermute(part, axes, [(i, i ^ k) for i in range(count)])]
    ppermute x2, starting transfers between devices: 4.91 us -> 2.78 us  [pack(): return (packed, lax.ppermute(packed, 'core', CORES), token)]
  transfers between devices with their start and end apart: 25 -> 25, of which waited for: 13 -> 13; matrix products, arithmetic and copies ran while one was open for 0% -> 0% of each run, Pallas kernels for 23% -> 25%
where the time goes in v4:
time: 117 us
  Pallas kernels  49.3 us (42%)
  starting transfers between devices  33.9 us (29%)
  waiting for transfers between devices  20.9 us (18%)
  blocking collectives  11 us (9%)
    ppermute x12, starting transfers between devices, from_others(): lax.ppermute(part, axes, [(i, i ^ k) for i in range(count)])  14.6 us
    ppermute x12, waiting for transfers between devices, from_others(): lax.ppermute(part, axes, [(i, i ^ k) for i in range(count)])  11.3 us
    all_to_all x1, blocking collectives, per_device(): ends = lax.all_to_all(ends, 'a', 0, 0)  11 us
    ppermute x2, starting transfers between devices, row_halo(): up = lax.ppermute(last, axes, [(i, i + 1) for i in range(count - 1)])  8.98 us
    pallas_call x1, Pallas kernels, kernel_grads(): pl.pallas_call(in_grad_kernel, grid=(frames // block,), in_specs=lead + [...  8.36 us
    pallas_call x1, Pallas kernels, kernel_grads(): pl.pallas_call(out_grad_kernel, grid=(frames // block,), in_specs=lead +...  7.78 us
    pallas_call x13, Pallas kernels, small_call(): pl.pallas_call(kernel, in_specs=[ANYWHERE] * len(after) + [SCALARS] * len...  7.13 us
    pallas_call x1, Pallas kernels, outputs_conv(): pl.pallas_call(outputs_kernel, grid=(frames // block,), in_specs=[pl.Bloc...  6.61 us
  transfers between devices with their start and end apart: 25, of which 13 were waited for; matrix products, arithmetic and copies ran while one was open for 0% of the time, Pallas kernels for 25%

profile of v4, /device:TPU:1, one launch (start us, length us, event | category | flops | bytes accessed | tf_op | source)
XLA Modules:
  0.0 116.7 jit_solution(14329913979572583335)
XLA Ops:
  1.3 4.0 %edge_rows.1 = (bf16[2,64,16,256]{3,2,1,0:T(8,128)(2,1)}, bf16[2,64,16,256]{3,2,1,0:T(8,128)(2,1)}) custom-call(s32[4]{0:T(128)} %pad_add_fusion.places_ref.refs_0_.place_ref.refs_1_, bf16[64,4,16,256]{3,2,1,0:T(8,128)(2,1)} %bitcast.16, bf16[64,4,16,256]{3,2,1,0:T(8,128)(2,1)} %bitcast.17, bf16[64,4,16,256]{3,2,1,0:T(8,128)(2,1)} %bitcast.12, ...), custom_call_target="tpu_custom_call" | custom-call | bytes 4194304 | tf_op jit(solution)/shard_map/edge_rows/pallas_call | solution.py:427
  5.3 4.5 %collective-permute-start = (bf16[2,64,16,256]{3,2,1,0:T(8,128)(2,1)}, bf16[2,64,16,256]{3,2,1,0:T(8,128)(2,1)S(1)}, u32[]{:S(2)}, u32[]{:S(2)}) collective-permute-start(bf16[2,64,16,256]{3,2,1,0:T(8,128)(2,1)} %get-tuple-element.55), channel_id=1, source_target_pairs={{0,1},{1,2},{2,3},{4,5},{5,6},{6,7},{8,9},{9,10},{10,11},{12,13},{... | collective-permute-start | bytes 3145736 | tf_op jit(solution)/shard_map/ppermute | solution.py:442
  9.8 1.9 %collective-permute-start.1 = (bf16[2,64,16,256]{3,2,1,0:T(8,128)(2,1)}, bf16[2,64,16,256]{3,2,1,0:T(8,128)(2,1)S(1)}, u32[]{:S(2)}, u32[]{:S(2)}) collective-permute-start(bf16[2,64,16,256]{3,2,1,0:T(8,128)(2,1)} %get-tuple-element.56), channel_id=1, source_target_pairs={{1,0},{2,1},{3,2},{5,4},{6,5},{7,6},{9,8},{10,9},{11,10},{13,12},{... | collective-permute-start | bytes 3145736 | tf_op jit(solution)/shard_map/ppermute | solution.py:443
  11.8 5.1 %interior_in.1.part_ref = f32[4,64,16,256]{3,2,1,0:T(8,128)S(1)} custom-call(bf16[64,4,16,256]{3,2,1,0:T(8,128)(2,1)S(1)} %bitcast.18, bf16[3,768,256]{2,1,0:T(8,128)(2,1)S(1)} %bitcast.21), custom_call_target="tpu_custom_call" | custom-call | flops 4831838208 | bytes 8388608 | tf_op jit(solution)/shard_map/interior_in/pallas_call | solution.py:106
  16.9 5.6 %interior_cot.1 = (f32[4,64,16,256]{3,2,1,0:T(8,128)S(1)}, bf16[3,768,256]{2,1,0:T(8,128)(2,1)S(1)}) custom-call(bf16[64,4,16,256]{3,2,1,0:T(8,128)(2,1)S(1)} %bitcast.14, bf16[3,3,256,256]{3,2,1,0:T(8,128)(2,1)S(1)} %copy-done.5), custom_call_target="tpu_custom_call" | custom-call | flops 4831838208 | bytes 8388608 | tf_op jit(solution)/shard_map/interior_cot/pallas_call | solution.py:91
  22.5 3.7 %collective-permute-done.1.down_ref = bf16[2,64,16,256]{3,2,1,0:T(8,128)(2,1)S(1)} collective-permute-done((bf16[2,64,16,256]{3,2,1,0:T(8,128)(2,1)}, bf16[2,64,16,256]{3,2,1,0:T(8,128)(2,1)S(1)}, u32[]{:S(2)}, u32[]{:S(2)}) %collective-permute-start.1) | collective-permute-done | bytes 1048608 | tf_op jit(solution)/shard_map/ppermute | solution.py:443
  26.2 2.2 %scan_fwd.1 = (f32[4,64,16,256]{3,2,1,0:T(8,128)S(1)}, f32[64,256]{1,0:T(8,128)S(1)}, f32[64,256]{1,0:T(8,128)S(1)}) custom-call(f32[4,64,16,256]{3,2,1,0:T(8,128)S(1)} %interior_in.1.part_ref, bf16[2,64,16,256]{3,2,1,0:T(8,128)(2,1)S(1)} %collective-permute-done.up_ref, bf16[2,64,16,256]{3,2,1,0:T(8,128)(2,1)S(1)} %collective-permute-done.1.down_ref, ...), custom_call_target="tpu_custom_call" | custom-call | flops 805306368 | bytes 12582912 | tf_op jit(solution)/shard_map/scan_fwd/pallas_call | solution.py:180
  28.4 2.5 %scan_back.1 = (f32[4,64,16,256]{3,2,1,0:T(8,128)S(1)}, f32[64,256]{1,0:T(8,128)S(1)}, f32[136,256]{1,0:T(8,128)S(1)}) custom-call(f32[4,64,16,256]{3,2,1,0:T(8,128)S(1)} %get-tuple-element.54.part_ref, bf16[2,64,16,256]{3,2,1,0:T(8,128)(2,1)S(1)} %collective-permute-done.up_ref, bf16[2,64,16,256]{3,2,1,0:T(8,128)(2,1)S(1)} %collective-permute-done.1.down_ref, ...), custom_call_target="tpu_custom_call" | custom-call | flops 805306368 | bytes 12582912 | tf_op jit(solution)/shard_map/scan_back/pallas_call | solution.py:180
  32.2 2.7 %collective-permute-done.2.refs_2_.pair_ref = f32[136,256]{1,0:T(8,128)S(1)} collective-permute-done((f32[136,256]{1,0:T(8,128)S(1)}, f32[136,256]{1,0:T(8,128)S(1)}, u32[]{:S(2)}, u32[]{:S(2)}) %collective-permute-start.2) | collective-permute-done | bytes 139296 | tf_op jit(solution)/shard_map/ppermute | solution.py:539
  36.1 11.0 %all_to_all.5.ends_ref = f32[4,72,256]{2,1,0:T(8,128)S(1)} all-to-all(f32[4,72,256]{2,1,0:T(8,128)S(1)} %get-tuple-element.60), channel_id=1, replica_groups=mesh['a'=4,'x'=2,'y'=2,'core'=2] {'a'}, dimensions={0} | all-to-all | bytes 589824 | tf_op jit(solution)/shard_map/all_to_all | solution.py:543
  47.0 7.8 %out_grad.1 = (bf16[4,64,16,256]{3,2,1,0:T(8,128)(2,1)S(1)}, bf16[64,16,256]{2,1,0:T(8,128)(2,1)S(1)}, bf16[64,16,256]{2,1,0:T(8,128)(2,1)S(1)}, bf16[1152,256]{...) custom-call(s32[4]{0:T(128)S(1)} %copy-done.4, f32[4,72,256]{2,1,0:T(8,128)S(1)} %all_to_all.5.ends_ref, ...), custom_call_target="tpu_custom_call" | custom-call | flops 4831838208 | bytes 10485760 | tf_op jit(solution)/shard_map/out_grad/pallas_call | solution.py:349
  54.9 4.5 %collective-permute-start.3 = (bf16[64,16,256]{2,1,0:T(8,128)(2,1)S(1)}, bf16[64,16,256]{2,1,0:T(8,128)(2,1)S(1)}, u32[]{:S(2)}, u32[]{:S(2)}) collective-permute-start(bf16[64,16,256]{2,1,0:T(8,128)(2,1)S(1)} %get-tuple-element.64), channel_id=1, source_target_pairs={{0,1},{1,2},{2,3},{4,5},{5,6},{6,7},{8,9},{9,10},{10,11},{12,13},{... | collective-permute-start | bytes 1572872 | tf_op jit(solution)/shard_map/ppermute | solution.py:442
  59.4 2.1 %collective-permute-start.4 = (bf16[64,16,256]{2,1,0:T(8,128)(2,1)S(1)}, bf16[64,16,256]{2,1,0:T(8,128)(2,1)S(1)}, u32[]{:S(2)}, u32[]{:S(2)}) collective-permute-start(bf16[64,16,256]{2,1,0:T(8,128)(2,1)S(1)} %get-tuple-element.65), channel_id=1, source_target_pairs={{1,0},{2,1},{3,2},{5,4},{6,5},{7,6},{9,8},{10,9},{11,10},{13,12},{... | collective-permute-start | bytes 1572872 | tf_op jit(solution)/shard_map/ppermute | solution.py:443
  64.9 8.4 %in_grad.1 = (bf16[1152,256]{1,0:T(8,128)(2,1)S(1)}, f32[1152,256]{1,0:T(8,128)S(1)}, f32[8,128]{1,0:T(8,128)S(1)}) custom-call(s32[4]{0:T(128)S(1)} %copy-done.4, f32[4,72,256]{2,1,0:T(8,128)S(1)} %all_to_all.5.ends_ref, f32[136,256]{1,0:T(8,128)S(1)} %collective-permute-done.2.refs_2_.pair_ref, f32[4,64,16,256]{3,2,1,0:T(8,128)S(1)} %get-tuple-element.66.local_ref, ...), custom_call_target="tpu_custom_call" | custom-call | flops 4831838208 | bytes 10485760 | tf_op jit(solution)/shard_map/in_grad/pallas_call | solution.py:360
  81.3 1.9 %collective-permute-done.12.refs_3_ = bf16[288,256]{1,0:T(8,128)(2,1)S(1)} collective-permute-done((bf16[288,256]{1,0:T(8,128)(2,1)S(1)}, bf16[288,256]{1,0:T(8,128)(2,1)S(1)}, u32[]{:S(2)}, u32[]{:S(2)}) %collective-permute-start.12) | collective-permute-done | bytes 147488 | tf_op jit(solution)/shard_map/ppermute | solution.py:514
  83.1 3.2 %collective-permute-done.13.refs_4_ = bf16[288,256]{1,0:T(8,128)(2,1)S(1)} collective-permute-done((bf16[288,256]{1,0:T(8,128)(2,1)S(1)}, bf16[288,256]{1,0:T(8,128)(2,1)S(1)}, u32[]{:S(2)}, u32[]{:S(2)}) %collective-permute-start.13) | collective-permute-done | bytes 147488 | tf_op jit(solution)/shard_map/ppermute | solution.py:514
  86.7 5.7 %collective-permute-start.19 = (bf16[288,256]{1,0:T(8,128)(2,1)S(1)}, bf16[288,256]{1,0:T(8,128)(2,1)S(1)}, u32[]{:S(2)}, u32[]{:S(2)}) collective-permute-start(bf16[288,256]{1,0:T(8,128)(2,1)S(1)} %get-tuple-element.96.refs_1_), channel_id=1, source_target_pairs={{0,6},{2,4},{4,2},{6,0},{1,7},{3,5},{5,3},{7,1},{8,14},{10,12},{12... | collective-permute-start | bytes 442376 | tf_op jit(solution)/shard_map/ppermute | solution.py:514
  92.9 6.6 %outputs_conv.1 = (bf16[64,4,16,256]{3,2,1,0:T(8,128)(2,1)}, f32[8,128]{1,0:T(8,128)S(1)}) custom-call(bf16[4,64,16,256]{3,2,1,0:T(8,128)(2,1)S(1)} %get-tuple-element.63.low_ref, bf16[64,16,256]{2,1,0:T(8,128)(2,1)S(1)} %collective-permute-done.3.refs_1_.up_ref, bf16[64,16,256]{2,1,0:T(8,128)(2,1)S(1)} %collective-permute-done.4.refs_2_.down_ref, ...), custom_call_target="tpu_custom_call" | custom-call | flops 4831838208 | bytes 8388608 | tf_op jit(solution)/shard_map/outputs_conv/pallas_call | solution.py:393
  100.1 1.9 %collective-permute-start.20 = (bf16[4,288,256]{2,1,0:T(8,128)(2,1)S(1)}, bf16[4,288,256]{2,1,0:T(8,128)(2,1)S(1)}, u32[]{:S(2)}, u32[]{:S(2)}) collective-permute-start(bf16[4,288,256]{2,1,0:T(8,128)(2,1)S(1)} %get-tuple-element.98.refs_2_), channel_id=1, source_target_pairs={{0,1},{1,0},{2,3},{3,2},{4,5},{5,4},{6,7},{7,6},{8,9},{9,8},{10,11... | collective-permute-start | bytes 1769480 | tf_op jit(solution)/shard_map/ppermute | solution.py:576
  102.1 2.6 %collective-permute-start.23 = (bf16[288,256]{1,0:T(8,128)(2,1)S(1)}, bf16[288,256]{1,0:T(8,128)(2,1)S(1)}, u32[]{:S(2)}, u32[]{:S(2)}) collective-permute-start(bf16[288,256]{1,0:T(8,128)(2,1)S(1)} %get-tuple-element.100.refs_1_), channel_id=1, source_target_pairs={{0,6},{2,4},{4,2},{6,0},{1,7},{3,5},{5,3},{7,1},{8,14},{10,12},{12... | collective-permute-start | bytes 442376 | tf_op jit(solution)/shard_map/ppermute | solution.py:514
  104.9 2.1 %out_merge.1 = (f32[2304,256]{1,0:T(8,128)}, f32[8,128]{1,0:T(8,128)S(1)}) custom-call(f32[8,128]{1,0:T(8,128)S(1)} %get-tuple-element.97.refs_0_, s32[4]{0:T(128)S(1)} %copy-done.4, bf16[4,288,256]{2,1,0:T(8,128)(2,1)S(1)} %get-tuple-element.98.refs_2_, bf16[4,288,256]{2,1,0:T(8,128)(2,1)S(1)} %collective-permute-done.20.refs_3_), custom_call_target="tpu_custom_call" | custom-call | flops 34359738368 | bytes 2097152 | tf_op jit(solution)/shard_map/out_merge/pallas_call | solution.py:459
  107.0 1.7 %collective-permute-done.23.refs_4_ = bf16[288,256]{1,0:T(8,128)(2,1)S(1)} collective-permute-done((bf16[288,256]{1,0:T(8,128)(2,1)S(1)}, bf16[288,256]{1,0:T(8,128)(2,1)S(1)}, u32[]{:S(2)}, u32[]{:S(2)}) %collective-permute-start.23) | collective-permute-done | bytes 147488 | tf_op jit(solution)/shard_map/ppermute | solution.py:514
  108.7 3.3 %collective-permute-done.22.refs_3_ = bf16[288,256]{1,0:T(8,128)(2,1)S(1)} collective-permute-done((bf16[288,256]{1,0:T(8,128)(2,1)S(1)}, bf16[288,256]{1,0:T(8,128)(2,1)S(1)}, u32[]{:S(2)}, u32[]{:S(2)}) %collective-permute-start.22) | collective-permute-done | bytes 147488 | tf_op jit(solution)/shard_map/ppermute | solution.py:514
  114.6 2.1 %in_merge.1 = (f32[2304,256]{1,0:T(8,128)}, f32[8,128]{1,0:T(8,128)}) custom-call(f32[8,128]{1,0:T(8,128)S(1)} %get-tuple-element.101.refs_0_, s32[4]{0:T(128)S(1)} %copy-done.4, bf16[4,288,256]{2,1,0:T(8,128)(2,1)S(1)} %get-tuple-element.102.refs_2_, bf16[4,288,256]{2,1,0:T(8,128)(2,1)S(1)} %collective-permute-done.24.refs_3_), custom_call_target="tpu_custom_call" | custom-call | flops 1073741824 | bytes 2097152 | tf_op jit(solution)/shard_map/in_merge/pallas_call | solution.py:459
  (63 shorter events, 18.8 us)
Async XLA Ops:
  5.3 17.2 %collective-permute-start = (bf16[2,64,16,256]{3,2,1,0:T(8,128)(2,1)}, bf16[2,64,16,256]{3,2,1,0:T(8,128)(2,1)S(1)}, u32[]{:S(2)}, u32[]{:S(2)}) collective-permute-start(bf16[2,64,16,256]{3,2,1,0:T(8,128)(2,1)} %get-tuple-element.55), channel_id=1, source_target_pairs={{0,1},{1,2},{2,3},{4,5},{5,6},{6,7},{8,9},{9,10},{10,11},{12,13},{... | collective-permute-start | bytes 3145736 | tf_op jit(solution)/shard_map/ppermute | solution.py:442
  9.8 16.3 %collective-permute-start.1 = (bf16[2,64,16,256]{3,2,1,0:T(8,128)(2,1)}, bf16[2,64,16,256]{3,2,1,0:T(8,128)(2,1)S(1)}, u32[]{:S(2)}, u32[]{:S(2)}) collective-permute-start(bf16[2,64,16,256]{3,2,1,0:T(8,128)(2,1)} %get-tuple-element.56), channel_id=1, source_target_pairs={{1,0},{2,1},{3,2},{5,4},{6,5},{7,6},{9,8},{10,9},{11,10},{13,12},{... | collective-permute-start | bytes 3145736 | tf_op jit(solution)/shard_map/ppermute | solution.py:443
  30.9 4.0 %collective-permute-start.2 = (f32[136,256]{1,0:T(8,128)S(1)}, f32[136,256]{1,0:T(8,128)S(1)}, u32[]{:S(2)}, u32[]{:S(2)}) collective-permute-start(f32[136,256]{1,0:T(8,128)S(1)} %get-tuple-element.59.refs_1_), channel_id=1, source_target_pairs={{0,4},{4,0},{1,5},{5,1},{2,6},{6,2},{3,7},{7,3},{8,12},{12,8},{9,1... | collective-permute-start | bytes 417800 | tf_op jit(solution)/shard_map/ppermute | solution.py:539
  54.8 6.7 %collective-permute-start.5 = (bf16[1152,256]{1,0:T(8,128)(2,1)S(1)}, bf16[1152,256]{1,0:T(8,128)(2,1)S(1)}, u32[]{:S(2)}, u32[]{:S(2)}) collective-permute-start(bf16[1152,256]{1,0:T(8,128)(2,1)S(1)} %get-tuple-element.70), channel_id=1, source_target_pairs={{0,1},{1,0},{2,3},{3,2},{4,5},{5,4},{6,7},{7,6},{8,9},{9,8},{10,11... | collective-permute-start | bytes 1769480 | tf_op jit(solution)/shard_map/ppermute | solution.py:548
  54.9 18.4 %collective-permute-start.3 = (bf16[64,16,256]{2,1,0:T(8,128)(2,1)S(1)}, bf16[64,16,256]{2,1,0:T(8,128)(2,1)S(1)}, u32[]{:S(2)}, u32[]{:S(2)}) collective-permute-start(bf16[64,16,256]{2,1,0:T(8,128)(2,1)S(1)} %get-tuple-element.64), channel_id=1, source_target_pairs={{0,1},{1,2},{2,3},{4,5},{5,6},{6,7},{8,9},{9,10},{10,11},{12,13},{... | collective-permute-start | bytes 1572872 | tf_op jit(solution)/shard_map/ppermute | solution.py:442
  59.4 15.2 %collective-permute-start.4 = (bf16[64,16,256]{2,1,0:T(8,128)(2,1)S(1)}, bf16[64,16,256]{2,1,0:T(8,128)(2,1)S(1)}, u32[]{:S(2)}, u32[]{:S(2)}) collective-permute-start(bf16[64,16,256]{2,1,0:T(8,128)(2,1)S(1)} %get-tuple-element.65), channel_id=1, source_target_pairs={{1,0},{2,1},{3,2},{5,4},{6,5},{7,6},{9,8},{10,9},{11,10},{13,12},{... | collective-permute-start | bytes 1572872 | tf_op jit(solution)/shard_map/ppermute | solution.py:443
  62.2 12.4 %collective-permute-start.6 = (bf16[288,256]{1,0:T(8,128)(2,1)S(1)}, bf16[288,256]{1,0:T(8,128)(2,1)S(1)}, u32[]{:S(2)}, u32[]{:S(2)}) collective-permute-start(bf16[288,256]{1,0:T(8,128)(2,1)S(1)} %get-tuple-element.74), channel_id=1, source_target_pairs={{0,2},{2,0},{4,6},{6,4},{1,3},{3,1},{5,7},{7,5},{8,10},{10,8},{12,... | collective-permute-start | bytes 442376 | tf_op jit(solution)/shard_map/ppermute | solution.py:514
  62.9 11.8 %collective-permute-start.7 = (bf16[288,256]{1,0:T(8,128)(2,1)S(1)}, bf16[288,256]{1,0:T(8,128)(2,1)S(1)}, u32[]{:S(2)}, u32[]{:S(2)}) collective-permute-start(bf16[288,256]{1,0:T(8,128)(2,1)S(1)} %get-tuple-element.75), channel_id=1, source_target_pairs={{0,4},{2,6},{4,0},{6,2},{1,5},{3,7},{5,1},{7,3},{8,12},{10,14},{12... | collective-permute-start | bytes 442376 | tf_op jit(solution)/shard_map/ppermute | solution.py:514
  64.1 10.5 %collective-permute-start.8 = (bf16[288,256]{1,0:T(8,128)(2,1)S(1)}, bf16[288,256]{1,0:T(8,128)(2,1)S(1)}, u32[]{:S(2)}, u32[]{:S(2)}) collective-permute-start(bf16[288,256]{1,0:T(8,128)(2,1)S(1)} %get-tuple-element.76), channel_id=1, source_target_pairs={{0,6},{2,4},{4,2},{6,0},{1,7},{3,5},{5,3},{7,1},{8,14},{10,12},{12... | collective-permute-start | bytes 442376 | tf_op jit(solution)/shard_map/ppermute | solution.py:514
  73.3 2.7 %collective-permute-start.9 = (bf16[1152,256]{1,0:T(8,128)(2,1)S(1)}, bf16[1152,256]{1,0:T(8,128)(2,1)S(1)}, u32[]{:S(2)}, u32[]{:S(2)}) collective-permute-start(bf16[1152,256]{1,0:T(8,128)(2,1)S(1)} %get-tuple-element.79), channel_id=1, source_target_pairs={{0,1},{1,0},{2,3},{3,2},{4,5},{5,4},{6,7},{7,6},{8,9},{9,8},{10,11... | collective-permute-start | bytes 1769480 | tf_op jit(solution)/shard_map/ppermute | solution.py:586
  74.7 5.0 %collective-permute-start.10 = (bf16[288,256]{1,0:T(8,128)(2,1)S(1)}, bf16[288,256]{1,0:T(8,128)(2,1)S(1)}, u32[]{:S(2)}, u32[]{:S(2)}) collective-permute-start(bf16[288,256]{1,0:T(8,128)(2,1)S(1)} %get-tuple-element.81.refs_1_), channel_id=1, source_target_pairs={{0,8},{8,0},{16,24},{24,16},{1,9},{9,1},{17,25},{25,17},{2,10},{10... | collective-permute-start | bytes 442376 | tf_op jit(solution)/shard_map/ppermute | solution.py:563
  76.7 4.6 %collective-permute-start.11 = (bf16[288,256]{1,0:T(8,128)(2,1)S(1)}, bf16[288,256]{1,0:T(8,128)(2,1)S(1)}, u32[]{:S(2)}, u32[]{:S(2)}) collective-permute-start(bf16[288,256]{1,0:T(8,128)(2,1)S(1)} %get-tuple-element.84), channel_id=1, source_target_pairs={{0,2},{2,0},{4,6},{6,4},{1,3},{3,1},{5,7},{7,5},{8,10},{10,8},{12,... | collective-permute-start | bytes 442376 | tf_op jit(solution)/shard_map/ppermute | solution.py:514
  78.4 4.7 %collective-permute-start.12 = (bf16[288,256]{1,0:T(8,128)(2,1)S(1)}, bf16[288,256]{1,0:T(8,128)(2,1)S(1)}, u32[]{:S(2)}, u32[]{:S(2)}) collective-permute-start(bf16[288,256]{1,0:T(8,128)(2,1)S(1)} %get-tuple-element.85), channel_id=1, source_target_pairs={{0,4},{2,6},{4,0},{6,2},{1,5},{3,7},{5,1},{7,3},{8,12},{10,14},{12... | collective-permute-start | bytes 442376 | tf_op jit(solution)/shard_map/ppermute | solution.py:514
  79.6 6.8 %collective-permute-start.13 = (bf16[288,256]{1,0:T(8,128)(2,1)S(1)}, bf16[288,256]{1,0:T(8,128)(2,1)S(1)}, u32[]{:S(2)}, u32[]{:S(2)}) collective-permute-start(bf16[288,256]{1,0:T(8,128)(2,1)S(1)} %get-tuple-element.86), channel_id=1, source_target_pairs={{0,6},{2,4},{4,2},{6,0},{1,7},{3,5},{5,3},{7,1},{8,14},{10,12},{12... | collective-permute-start | bytes 442376 | tf_op jit(solution)/shard_map/ppermute | solution.py:514
  79.7 7.0 %collective-permute-start.14 = (bf16[288,256]{1,0:T(8,128)(2,1)S(1)}, bf16[288,256]{1,0:T(8,128)(2,1)S(1)}, u32[]{:S(2)}, u32[]{:S(2)}) collective-permute-start(bf16[288,256]{1,0:T(8,128)(2,1)S(1)} %get-tuple-element.88.refs_1_), channel_id=1, source_target_pairs={{0,16},{8,24},{16,0},{24,8},{1,17},{9,25},{17,1},{25,9},{2,18},{10... | collective-permute-start | bytes 442376 | tf_op jit(solution)/shard_map/ppermute | solution.py:563
  86.5 6.3 %collective-permute-start.15 = (bf16[288,256]{1,0:T(8,128)(2,1)S(1)}, bf16[288,256]{1,0:T(8,128)(2,1)S(1)}, u32[]{:S(2)}, u32[]{:S(2)}) collective-permute-start(bf16[288,256]{1,0:T(8,128)(2,1)S(1)} %get-tuple-element.90.refs_1_), channel_id=1, source_target_pairs={{0,8},{8,0},{16,24},{24,16},{1,9},{9,1},{17,25},{25,17},{2,10},{10... | collective-permute-start | bytes 442376 | tf_op jit(solution)/shard_map/ppermute | solution.py:563
  86.7 13.3 %collective-permute-start.19 = (bf16[288,256]{1,0:T(8,128)(2,1)S(1)}, bf16[288,256]{1,0:T(8,128)(2,1)S(1)}, u32[]{:S(2)}, u32[]{:S(2)}) collective-permute-start(bf16[288,256]{1,0:T(8,128)(2,1)S(1)} %get-tuple-element.96.refs_1_), channel_id=1, source_target_pairs={{0,6},{2,4},{4,2},{6,0},{1,7},{3,5},{5,3},{7,1},{8,14},{10,12},{12... | collective-permute-start | bytes 442376 | tf_op jit(solution)/shard_map/ppermute | solution.py:514
  92.4 7.6 %collective-permute-start.18 = (bf16[288,256]{1,0:T(8,128)(2,1)S(1)}, bf16[288,256]{1,0:T(8,128)(2,1)S(1)}, u32[]{:S(2)}, u32[]{:S(2)}) collective-permute-start(bf16[288,256]{1,0:T(8,128)(2,1)S(1)} %get-tuple-element.96.refs_1_), channel_id=1, source_target_pairs={{0,4},{2,6},{4,0},{6,2},{1,5},{3,7},{5,1},{7,3},{8,12},{10,14},{12... | collective-permute-start | bytes 442376 | tf_op jit(solution)/shard_map/ppermute | solution.py:514
  92.7 7.4 %collective-permute-start.17 = (bf16[288,256]{1,0:T(8,128)(2,1)S(1)}, bf16[288,256]{1,0:T(8,128)(2,1)S(1)}, u32[]{:S(2)}, u32[]{:S(2)}) collective-permute-start(bf16[288,256]{1,0:T(8,128)(2,1)S(1)} %get-tuple-element.96.refs_1_), channel_id=1, source_target_pairs={{0,2},{2,0},{4,6},{6,4},{1,3},{3,1},{5,7},{7,5},{8,10},{10,8},{12,... | collective-permute-start | bytes 442376 | tf_op jit(solution)/shard_map/ppermute | solution.py:514
  92.8 7.2 %collective-permute-start.16 = (bf16[288,256]{1,0:T(8,128)(2,1)S(1)}, bf16[288,256]{1,0:T(8,128)(2,1)S(1)}, u32[]{:S(2)}, u32[]{:S(2)}) collective-permute-start(bf16[288,256]{1,0:T(8,128)(2,1)S(1)} %get-tuple-element.94.refs_1_), channel_id=1, source_target_pairs={{0,16},{8,24},{16,0},{24,8},{1,17},{9,25},{17,1},{25,9},{2,18},{10... | collective-permute-start | bytes 442376 | tf_op jit(solution)/shard_map/ppermute | solution.py:563
  100.1 4.8 %collective-permute-start.20 = (bf16[4,288,256]{2,1,0:T(8,128)(2,1)S(1)}, bf16[4,288,256]{2,1,0:T(8,128)(2,1)S(1)}, u32[]{:S(2)}, u32[]{:S(2)}) collective-permute-start(bf16[4,288,256]{2,1,0:T(8,128)(2,1)S(1)} %get-tuple-element.98.refs_2_), channel_id=1, source_target_pairs={{0,1},{1,0},{2,3},{3,2},{4,5},{5,4},{6,7},{7,6},{8,9},{9,8},{10,11... | collective-permute-start | bytes 1769480 | tf_op jit(solution)/shard_map/ppermute | solution.py:576
  102.1 6.7 %collective-permute-start.23 = (bf16[288,256]{1,0:T(8,128)(2,1)S(1)}, bf16[288,256]{1,0:T(8,128)(2,1)S(1)}, u32[]{:S(2)}, u32[]{:S(2)}) collective-permute-start(bf16[288,256]{1,0:T(8,128)(2,1)S(1)} %get-tuple-element.100.refs_1_), channel_id=1, source_target_pairs={{0,6},{2,4},{4,2},{6,0},{1,7},{3,5},{5,3},{7,1},{8,14},{10,12},{12... | collective-permute-start | bytes 442376 | tf_op jit(solution)/shard_map/ppermute | solution.py:514
  104.6 7.4 %collective-permute-start.22 = (bf16[288,256]{1,0:T(8,128)(2,1)S(1)}, bf16[288,256]{1,0:T(8,128)(2,1)S(1)}, u32[]{:S(2)}, u32[]{:S(2)}) collective-permute-start(bf16[288,256]{1,0:T(8,128)(2,1)S(1)} %get-tuple-element.100.refs_1_), channel_id=1, source_target_pairs={{0,4},{2,6},{4,0},{6,2},{1,5},{3,7},{5,1},{7,3},{8,12},{10,14},{12... | collective-permute-start | bytes 442376 | tf_op jit(solution)/shard_map/ppermute | solution.py:514
  104.9 7.2 %collective-permute-start.21 = (bf16[288,256]{1,0:T(8,128)(2,1)S(1)}, bf16[288,256]{1,0:T(8,128)(2,1)S(1)}, u32[]{:S(2)}, u32[]{:S(2)}) collective-permute-start(bf16[288,256]{1,0:T(8,128)(2,1)S(1)} %get-tuple-element.100.refs_1_), channel_id=1, source_target_pairs={{0,2},{2,0},{4,6},{6,4},{1,3},{3,1},{5,7},{7,5},{8,10},{10,8},{12,... | collective-permute-start | bytes 442376 | tf_op jit(solution)/shard_map/ppermute | solution.py:514
  (8 other events, 55.6 us)

commit v5 on v4

--- a/solution.py
+++ b/solution.py
@@ -18,7 +18,7 @@
 TOKEN_SPEC = pl.BlockSpec((8, 128), lambda *b: (0, 0))
 
 
-def params(mib=20):
+def params(mib=30):
     return pltpu.CompilerParams(
         dimension_semantics=("arbitrary",), vmem_limit_bytes=mib * 1024 * 1024
     )
@@ -519,7 +519,7 @@
 def per_device(inputs, decays, in_kernel, out_kernel, skip, cotangent):
     clips, frames, rows, width, c = inputs.shape
     p = in_kernel.shape[3]
-    block = 16
+    block = 32
     devices = math.prod(lax.axis_size(name) for name in ("a", "x", "y", "core"))
     grad_scale = 1.0 / math.sqrt(clips * frames * rows * width * devices)
     x = inputs.reshape(frames, rows, width, c)

time: 117 us -> 114 us (0.974)
  Pallas kernels: 49.3 us -> 45.7 us
    pallas_call x1, Pallas kernels: 4 us -> 2.76 us  [edge_rows(): pl.pallas_call(edge_rows_kernel, grid=(frames // block,), in_specs=[SCALA...]
where the time goes in v5:
time: 114 us; the launch traced here: 113 us
  Pallas kernels  45.7 us (40%)
  starting transfers between devices  33.9 us (30%)
  waiting for transfers between devices  21.1 us (19%)
  blocking collectives  11 us (10%)
    ppermute x12, starting transfers between devices, from_others(): lax.ppermute(part, axes, [(i, i ^ k) for i in range(count)])  14 us
    all_to_all x1, blocking collectives, per_device(): ends = lax.all_to_all(ends, 'a', 0, 0)  11 us
    ppermute x12, waiting for transfers between devices, from_others(): lax.ppermute(part, axes, [(i, i ^ k) for i in range(count)])  10.6 us
    ppermute x2, starting transfers between devices, row_halo(): up = lax.ppermute(last, axes, [(i, i + 1) for i in range(count - 1)])  8.96 us
    pallas_call x1, Pallas kernels, kernel_grads(): pl.pallas_call(in_grad_kernel, grid=(frames // block,), in_specs=lead + [...  7.83 us
    pallas_call x1, Pallas kernels, kernel_grads(): pl.pallas_call(out_grad_kernel, grid=(frames // block,), in_specs=lead +...  7.27 us
    pallas_call x13, Pallas kernels, small_call(): pl.pallas_call(kernel, in_specs=[ANYWHERE] * len(after) + [SCALARS] * len...  7.09 us
    pallas_call x1, Pallas kernels, outputs_conv(): pl.pallas_call(outputs_kernel, grid=(frames // block,), in_specs=[pl.Bloc...  6.63 us
  transfers between devices with their start and end apart: 25, of which 13 were waited for; matrix products, arithmetic and copies ran while one was open for 0% of the time, Pallas kernels for 25%

profile of v5, /device:TPU:1, one launch (start us, length us, event | category | flops | bytes accessed | tf_op | source)
XLA Modules:
  0.0 113.3 jit_solution(124850737340627255)
XLA Ops:
  1.3 2.8 %edge_rows.1 = (bf16[2,64,16,256]{3,2,1,0:T(8,128)(2,1)}, bf16[2,64,16,256]{3,2,1,0:T(8,128)(2,1)}) custom-call(s32[4]{0:T(128)} %pad_add_fusion.places_ref.refs_0_.place_ref.refs_1_, bf16[64,4,16,256]{3,2,1,0:T(8,128)(2,1)} %bitcast.16, bf16[64,4,16,256]{3,2,1,0:T(8,128)(2,1)} %bitcast.17, bf16[64,4,16,256]{3,2,1,0:T(8,128)(2,1)} %bitcast.12, ...), custom_call_target="tpu_custom_call" | custom-call | bytes 4194304 | tf_op jit(solution)/shard_map/edge_rows/pallas_call | solution.py:427
  4.0 4.5 %collective-permute-start = (bf16[2,64,16,256]{3,2,1,0:T(8,128)(2,1)}, bf16[2,64,16,256]{3,2,1,0:T(8,128)(2,1)S(1)}, u32[]{:S(2)}, u32[]{:S(2)}) collective-permute-start(bf16[2,64,16,256]{3,2,1,0:T(8,128)(2,1)} %get-tuple-element.55), channel_id=1, source_target_pairs={{0,1},{1,2},{2,3},{4,5},{5,6},{6,7},{8,9},{9,10},{10,11},{12,13},{... | collective-permute-start | bytes 3145736 | tf_op jit(solution)/shard_map/ppermute | solution.py:442
  8.6 1.9 %collective-permute-start.1 = (bf16[2,64,16,256]{3,2,1,0:T(8,128)(2,1)}, bf16[2,64,16,256]{3,2,1,0:T(8,128)(2,1)S(1)}, u32[]{:S(2)}, u32[]{:S(2)}) collective-permute-start(bf16[2,64,16,256]{3,2,1,0:T(8,128)(2,1)} %get-tuple-element.56), channel_id=1, source_target_pairs={{1,0},{2,1},{3,2},{5,4},{6,5},{7,6},{9,8},{10,9},{11,10},{13,12},{... | collective-permute-start | bytes 3145736 | tf_op jit(solution)/shard_map/ppermute | solution.py:443
  10.5 4.8 %interior_in.1.part_ref = f32[4,64,16,256]{3,2,1,0:T(8,128)S(1)} custom-call(bf16[64,4,16,256]{3,2,1,0:T(8,128)(2,1)S(1)} %bitcast.18, bf16[3,768,256]{2,1,0:T(8,128)(2,1)S(1)} %bitcast.21), custom_call_target="tpu_custom_call" | custom-call | flops 4831838208 | bytes 8388608 | tf_op jit(solution)/shard_map/interior_in/pallas_call | solution.py:106
  15.4 5.2 %interior_cot.1 = (f32[4,64,16,256]{3,2,1,0:T(8,128)S(1)}, bf16[3,768,256]{2,1,0:T(8,128)(2,1)S(1)}) custom-call(bf16[64,4,16,256]{3,2,1,0:T(8,128)(2,1)S(1)} %bitcast.14, bf16[3,3,256,256]{3,2,1,0:T(8,128)(2,1)S(1)} %copy-done.5), custom_call_target="tpu_custom_call" | custom-call | flops 4831838208 | bytes 8388608 | tf_op jit(solution)/shard_map/interior_cot/pallas_call | solution.py:91
  20.6 4.3 %collective-permute-done.1.down_ref = bf16[2,64,16,256]{3,2,1,0:T(8,128)(2,1)S(1)} collective-permute-done((bf16[2,64,16,256]{3,2,1,0:T(8,128)(2,1)}, bf16[2,64,16,256]{3,2,1,0:T(8,128)(2,1)S(1)}, u32[]{:S(2)}, u32[]{:S(2)}) %collective-permute-start.1) | collective-permute-done | bytes 1048608 | tf_op jit(solution)/shard_map/ppermute | solution.py:443
  24.9 2.0 %scan_fwd.1 = (f32[4,64,16,256]{3,2,1,0:T(8,128)S(1)}, f32[64,256]{1,0:T(8,128)S(1)}, f32[64,256]{1,0:T(8,128)S(1)}) custom-call(f32[4,64,16,256]{3,2,1,0:T(8,128)S(1)} %interior_in.1.part_ref, bf16[2,64,16,256]{3,2,1,0:T(8,128)(2,1)S(1)} %collective-permute-done.up_ref, bf16[2,64,16,256]{3,2,1,0:T(8,128)(2,1)S(1)} %collective-permute-done.1.down_ref, ...), custom_call_target="tpu_custom_call" | custom-call | flops 805306368 | bytes 12582912 | tf_op jit(solution)/shard_map/scan_fwd/pallas_call | solution.py:180
  27.0 2.2 %scan_back.1 = (f32[4,64,16,256]{3,2,1,0:T(8,128)S(1)}, f32[64,256]{1,0:T(8,128)S(1)}, f32[136,256]{1,0:T(8,128)S(1)}) custom-call(f32[4,64,16,256]{3,2,1,0:T(8,128)S(1)} %get-tuple-element.54.part_ref, bf16[2,64,16,256]{3,2,1,0:T(8,128)(2,1)S(1)} %collective-permute-done.up_ref, bf16[2,64,16,256]{3,2,1,0:T(8,128)(2,1)S(1)} %collective-permute-done.1.down_ref, ...), custom_call_target="tpu_custom_call" | custom-call | flops 805306368 | bytes 12582912 | tf_op jit(solution)/shard_map/scan_back/pallas_call | solution.py:180
  30.4 2.7 %collective-permute-done.2.refs_2_.pair_ref = f32[136,256]{1,0:T(8,128)S(1)} collective-permute-done((f32[136,256]{1,0:T(8,128)S(1)}, f32[136,256]{1,0:T(8,128)S(1)}, u32[]{:S(2)}, u32[]{:S(2)}) %collective-permute-start.2) | collective-permute-done | bytes 139296 | tf_op jit(solution)/shard_map/ppermute | solution.py:539
  34.3 11.0 %all_to_all.5.ends_ref = f32[4,72,256]{2,1,0:T(8,128)S(1)} all-to-all(f32[4,72,256]{2,1,0:T(8,128)S(1)} %get-tuple-element.60), channel_id=1, replica_groups=mesh['a'=4,'x'=2,'y'=2,'core'=2] {'a'}, dimensions={0} | all-to-all | bytes 589824 | tf_op jit(solution)/shard_map/all_to_all | solution.py:543
  45.3 7.3 %out_grad.1 = (bf16[4,64,16,256]{3,2,1,0:T(8,128)(2,1)S(1)}, bf16[64,16,256]{2,1,0:T(8,128)(2,1)S(1)}, bf16[64,16,256]{2,1,0:T(8,128)(2,1)S(1)}, bf16[1152,256]{...) custom-call(s32[4]{0:T(128)S(1)} %copy-done.4, f32[4,72,256]{2,1,0:T(8,128)S(1)} %all_to_all.5.ends_ref, ...), custom_call_target="tpu_custom_call" | custom-call | flops 4831838208 | bytes 10485760 | tf_op jit(solution)/shard_map/out_grad/pallas_call | solution.py:349
  52.6 4.4 %collective-permute-start.3 = (bf16[64,16,256]{2,1,0:T(8,128)(2,1)S(1)}, bf16[64,16,256]{2,1,0:T(8,128)(2,1)S(1)}, u32[]{:S(2)}, u32[]{:S(2)}) collective-permute-start(bf16[64,16,256]{2,1,0:T(8,128)(2,1)S(1)} %get-tuple-element.64), channel_id=1, source_target_pairs={{0,1},{1,2},{2,3},{4,5},{5,6},{6,7},{8,9},{9,10},{10,11},{12,13},{... | collective-permute-start | bytes 1572872 | tf_op jit(solution)/shard_map/ppermute | solution.py:442
  57.1 2.1 %collective-permute-start.4 = (bf16[64,16,256]{2,1,0:T(8,128)(2,1)S(1)}, bf16[64,16,256]{2,1,0:T(8,128)(2,1)S(1)}, u32[]{:S(2)}, u32[]{:S(2)}) collective-permute-start(bf16[64,16,256]{2,1,0:T(8,128)(2,1)S(1)} %get-tuple-element.65), channel_id=1, source_target_pairs={{1,0},{2,1},{3,2},{5,4},{6,5},{7,6},{9,8},{10,9},{11,10},{13,12},{... | collective-permute-start | bytes 1572872 | tf_op jit(solution)/shard_map/ppermute | solution.py:443
  62.6 7.8 %in_grad.1 = (bf16[1152,256]{1,0:T(8,128)(2,1)S(1)}, f32[1152,256]{1,0:T(8,128)S(1)}, f32[8,128]{1,0:T(8,128)S(1)}) custom-call(s32[4]{0:T(128)S(1)} %copy-done.4, f32[4,72,256]{2,1,0:T(8,128)S(1)} %all_to_all.5.ends_ref, f32[136,256]{1,0:T(8,128)S(1)} %collective-permute-done.2.refs_2_.pair_ref, f32[4,64,16,256]{3,2,1,0:T(8,128)S(1)} %get-tuple-element.66.local_ref, ...), custom_call_target="tpu_custom_call" | custom-call | flops 4831838208 | bytes 10485760 | tf_op jit(solution)/shard_map/in_grad/pallas_call | solution.py:360
  73.8 1.7 %collective-permute-start.11 = (bf16[288,256]{1,0:T(8,128)(2,1)S(1)}, bf16[288,256]{1,0:T(8,128)(2,1)S(1)}, u32[]{:S(2)}, u32[]{:S(2)}) collective-permute-start(bf16[288,256]{1,0:T(8,128)(2,1)S(1)} %get-tuple-element.84), channel_id=1, source_target_pairs={{0,2},{2,0},{4,6},{6,4},{1,3},{3,1},{5,7},{7,5},{8,10},{10,8},{12,... | collective-permute-start | bytes 442376 | tf_op jit(solution)/shard_map/ppermute | solution.py:514
  78.4 1.8 %collective-permute-done.12.refs_3_ = bf16[288,256]{1,0:T(8,128)(2,1)S(1)} collective-permute-done((bf16[288,256]{1,0:T(8,128)(2,1)S(1)}, bf16[288,256]{1,0:T(8,128)(2,1)S(1)}, u32[]{:S(2)}, u32[]{:S(2)}) %collective-permute-start.12) | collective-permute-done | bytes 147488 | tf_op jit(solution)/shard_map/ppermute | solution.py:514
  80.2 2.6 %collective-permute-done.13.refs_4_ = bf16[288,256]{1,0:T(8,128)(2,1)S(1)} collective-permute-done((bf16[288,256]{1,0:T(8,128)(2,1)S(1)}, bf16[288,256]{1,0:T(8,128)(2,1)S(1)}, u32[]{:S(2)}, u32[]{:S(2)}) %collective-permute-start.13) | collective-permute-done | bytes 147488 | tf_op jit(solution)/shard_map/ppermute | solution.py:514
  83.7 5.2 %collective-permute-start.19 = (bf16[288,256]{1,0:T(8,128)(2,1)S(1)}, bf16[288,256]{1,0:T(8,128)(2,1)S(1)}, u32[]{:S(2)}, u32[]{:S(2)}) collective-permute-start(bf16[288,256]{1,0:T(8,128)(2,1)S(1)} %get-tuple-element.96.refs_1_), channel_id=1, source_target_pairs={{0,6},{2,4},{4,2},{6,0},{1,7},{3,5},{5,3},{7,1},{8,14},{10,12},{12... | collective-permute-start | bytes 442376 | tf_op jit(solution)/shard_map/ppermute | solution.py:514
  89.5 6.6 %outputs_conv.1 = (bf16[64,4,16,256]{3,2,1,0:T(8,128)(2,1)}, f32[8,128]{1,0:T(8,128)S(1)}) custom-call(bf16[4,64,16,256]{3,2,1,0:T(8,128)(2,1)S(1)} %get-tuple-element.63.low_ref, bf16[64,16,256]{2,1,0:T(8,128)(2,1)S(1)} %collective-permute-done.3.refs_1_.up_ref, bf16[64,16,256]{2,1,0:T(8,128)(2,1)S(1)} %collective-permute-done.4.refs_2_.down_ref, ...), custom_call_target="tpu_custom_call" | custom-call | flops 4831838208 | bytes 8388608 | tf_op jit(solution)/shard_map/outputs_conv/pallas_call | solution.py:393
  96.2 2.8 %collective-permute-start.20 = (bf16[4,288,256]{2,1,0:T(8,128)(2,1)S(1)}, bf16[4,288,256]{2,1,0:T(8,128)(2,1)S(1)}, u32[]{:S(2)}, u32[]{:S(2)}) collective-permute-start(bf16[4,288,256]{2,1,0:T(8,128)(2,1)S(1)} %get-tuple-element.98.refs_2_), channel_id=1, source_target_pairs={{0,1},{1,0},{2,3},{3,2},{4,5},{5,4},{6,7},{7,6},{8,9},{9,8},{10,11... | collective-permute-start | bytes 1769480 | tf_op jit(solution)/shard_map/ppermute | solution.py:576
  99.1 1.8 %collective-permute-start.23 = (bf16[288,256]{1,0:T(8,128)(2,1)S(1)}, bf16[288,256]{1,0:T(8,128)(2,1)S(1)}, u32[]{:S(2)}, u32[]{:S(2)}) collective-permute-start(bf16[288,256]{1,0:T(8,128)(2,1)S(1)} %get-tuple-element.100.refs_1_), channel_id=1, source_target_pairs={{0,6},{2,4},{4,2},{6,0},{1,7},{3,5},{5,3},{7,1},{8,14},{10,12},{12... | collective-permute-start | bytes 442376 | tf_op jit(solution)/shard_map/ppermute | solution.py:514
  101.8 2.1 %out_merge.1 = (f32[2304,256]{1,0:T(8,128)}, f32[8,128]{1,0:T(8,128)S(1)}) custom-call(f32[8,128]{1,0:T(8,128)S(1)} %get-tuple-element.97.refs_0_, s32[4]{0:T(128)S(1)} %copy-done.4, bf16[4,288,256]{2,1,0:T(8,128)(2,1)S(1)} %get-tuple-element.98.refs_2_, bf16[4,288,256]{2,1,0:T(8,128)(2,1)S(1)} %collective-permute-done.20.refs_3_), custom_call_target="tpu_custom_call" | custom-call | flops 34359738368 | bytes 2097152 | tf_op jit(solution)/shard_map/out_merge/pallas_call | solution.py:459
  105.4 2.9 %collective-permute-done.22.refs_3_ = bf16[288,256]{1,0:T(8,128)(2,1)S(1)} collective-permute-done((bf16[288,256]{1,0:T(8,128)(2,1)S(1)}, bf16[288,256]{1,0:T(8,128)(2,1)S(1)}, u32[]{:S(2)}, u32[]{:S(2)}) %collective-permute-start.22) | collective-permute-done | bytes 147488 | tf_op jit(solution)/shard_map/ppermute | solution.py:514
  111.2 2.1 %in_merge.1 = (f32[2304,256]{1,0:T(8,128)}, f32[8,128]{1,0:T(8,128)}) custom-call(f32[8,128]{1,0:T(8,128)S(1)} %get-tuple-element.101.refs_0_, s32[4]{0:T(128)S(1)} %copy-done.4, bf16[4,288,256]{2,1,0:T(8,128)(2,1)S(1)} %get-tuple-element.102.refs_2_, bf16[4,288,256]{2,1,0:T(8,128)(2,1)S(1)} %collective-permute-done.24.refs_3_), custom_call_target="tpu_custom_call" | custom-call | flops 1073741824 | bytes 2097152 | tf_op jit(solution)/shard_map/in_merge/pallas_call | solution.py:459
  (63 shorter events, 19.6 us)
Async XLA Ops:
  4.0 16.6 %collective-permute-start = (bf16[2,64,16,256]{3,2,1,0:T(8,128)(2,1)}, bf16[2,64,16,256]{3,2,1,0:T(8,128)(2,1)S(1)}, u32[]{:S(2)}, u32[]{:S(2)}) collective-permute-start(bf16[2,64,16,256]{3,2,1,0:T(8,128)(2,1)} %get-tuple-element.55), channel_id=1, source_target_pairs={{0,1},{1,2},{2,3},{4,5},{5,6},{6,7},{8,9},{9,10},{10,11},{12,13},{... | collective-permute-start | bytes 3145736 | tf_op jit(solution)/shard_map/ppermute | solution.py:442
  8.6 16.3 %collective-permute-start.1 = (bf16[2,64,16,256]{3,2,1,0:T(8,128)(2,1)}, bf16[2,64,16,256]{3,2,1,0:T(8,128)(2,1)S(1)}, u32[]{:S(2)}, u32[]{:S(2)}) collective-permute-start(bf16[2,64,16,256]{3,2,1,0:T(8,128)(2,1)} %get-tuple-element.56), channel_id=1, source_target_pairs={{1,0},{2,1},{3,2},{5,4},{6,5},{7,6},{9,8},{10,9},{11,10},{13,12},{... | collective-permute-start | bytes 3145736 | tf_op jit(solution)/shard_map/ppermute | solution.py:443
  29.1 4.0 %collective-permute-start.2 = (f32[136,256]{1,0:T(8,128)S(1)}, f32[136,256]{1,0:T(8,128)S(1)}, u32[]{:S(2)}, u32[]{:S(2)}) collective-permute-start(f32[136,256]{1,0:T(8,128)S(1)} %get-tuple-element.59.refs_1_), channel_id=1, source_target_pairs={{0,4},{4,0},{1,5},{5,1},{2,6},{6,2},{3,7},{7,3},{8,12},{12,8},{9,1... | collective-permute-start | bytes 417800 | tf_op jit(solution)/shard_map/ppermute | solution.py:539
  52.5 6.6 %collective-permute-start.5 = (bf16[1152,256]{1,0:T(8,128)(2,1)S(1)}, bf16[1152,256]{1,0:T(8,128)(2,1)S(1)}, u32[]{:S(2)}, u32[]{:S(2)}) collective-permute-start(bf16[1152,256]{1,0:T(8,128)(2,1)S(1)} %get-tuple-element.70), channel_id=1, source_target_pairs={{0,1},{1,0},{2,3},{3,2},{4,5},{5,4},{6,7},{7,6},{8,9},{9,8},{10,11... | collective-permute-start | bytes 1769480 | tf_op jit(solution)/shard_map/ppermute | solution.py:548
  52.6 17.8 %collective-permute-start.3 = (bf16[64,16,256]{2,1,0:T(8,128)(2,1)S(1)}, bf16[64,16,256]{2,1,0:T(8,128)(2,1)S(1)}, u32[]{:S(2)}, u32[]{:S(2)}) collective-permute-start(bf16[64,16,256]{2,1,0:T(8,128)(2,1)S(1)} %get-tuple-element.64), channel_id=1, source_target_pairs={{0,1},{1,2},{2,3},{4,5},{5,6},{6,7},{8,9},{9,10},{10,11},{12,13},{... | collective-permute-start | bytes 1572872 | tf_op jit(solution)/shard_map/ppermute | solution.py:442
  57.1 15.2 %collective-permute-start.4 = (bf16[64,16,256]{2,1,0:T(8,128)(2,1)S(1)}, bf16[64,16,256]{2,1,0:T(8,128)(2,1)S(1)}, u32[]{:S(2)}, u32[]{:S(2)}) collective-permute-start(bf16[64,16,256]{2,1,0:T(8,128)(2,1)S(1)} %get-tuple-element.65), channel_id=1, source_target_pairs={{1,0},{2,1},{3,2},{5,4},{6,5},{7,6},{9,8},{10,9},{11,10},{13,12},{... | collective-permute-start | bytes 1572872 | tf_op jit(solution)/shard_map/ppermute | solution.py:443
  59.9 12.4 %collective-permute-start.6 = (bf16[288,256]{1,0:T(8,128)(2,1)S(1)}, bf16[288,256]{1,0:T(8,128)(2,1)S(1)}, u32[]{:S(2)}, u32[]{:S(2)}) collective-permute-start(bf16[288,256]{1,0:T(8,128)(2,1)S(1)} %get-tuple-element.74), channel_id=1, source_target_pairs={{0,2},{2,0},{4,6},{6,4},{1,3},{3,1},{5,7},{7,5},{8,10},{10,8},{12,... | collective-permute-start | bytes 442376 | tf_op jit(solution)/shard_map/ppermute | solution.py:514
  60.5 11.8 %collective-permute-start.7 = (bf16[288,256]{1,0:T(8,128)(2,1)S(1)}, bf16[288,256]{1,0:T(8,128)(2,1)S(1)}, u32[]{:S(2)}, u32[]{:S(2)}) collective-permute-start(bf16[288,256]{1,0:T(8,128)(2,1)S(1)} %get-tuple-element.75), channel_id=1, source_target_pairs={{0,4},{2,6},{4,0},{6,2},{1,5},{3,7},{5,1},{7,3},{8,12},{10,14},{12... | collective-permute-start | bytes 442376 | tf_op jit(solution)/shard_map/ppermute | solution.py:514
  61.7 10.6 %collective-permute-start.8 = (bf16[288,256]{1,0:T(8,128)(2,1)S(1)}, bf16[288,256]{1,0:T(8,128)(2,1)S(1)}, u32[]{:S(2)}, u32[]{:S(2)}) collective-permute-start(bf16[288,256]{1,0:T(8,128)(2,1)S(1)} %get-tuple-element.76), channel_id=1, source_target_pairs={{0,6},{2,4},{4,2},{6,0},{1,7},{3,5},{5,3},{7,1},{8,14},{10,12},{12... | collective-permute-start | bytes 442376 | tf_op jit(solution)/shard_map/ppermute | solution.py:514
  70.4 2.7 %collective-permute-start.9 = (bf16[1152,256]{1,0:T(8,128)(2,1)S(1)}, bf16[1152,256]{1,0:T(8,128)(2,1)S(1)}, u32[]{:S(2)}, u32[]{:S(2)}) collective-permute-start(bf16[1152,256]{1,0:T(8,128)(2,1)S(1)} %get-tuple-element.79), channel_id=1, source_target_pairs={{0,1},{1,0},{2,3},{3,2},{4,5},{5,4},{6,7},{7,6},{8,9},{9,8},{10,11... | collective-permute-start | bytes 1769480 | tf_op jit(solution)/shard_map/ppermute | solution.py:586
  72.4 4.4 %collective-permute-start.10 = (bf16[288,256]{1,0:T(8,128)(2,1)S(1)}, bf16[288,256]{1,0:T(8,128)(2,1)S(1)}, u32[]{:S(2)}, u32[]{:S(2)}) collective-permute-start(bf16[288,256]{1,0:T(8,128)(2,1)S(1)} %get-tuple-element.81.refs_1_), channel_id=1, source_target_pairs={{0,8},{8,0},{16,24},{24,16},{1,9},{9,1},{17,25},{25,17},{2,10},{10... | collective-permute-start | bytes 442376 | tf_op jit(solution)/shard_map/ppermute | solution.py:563
  73.8 4.6 %collective-permute-start.11 = (bf16[288,256]{1,0:T(8,128)(2,1)S(1)}, bf16[288,256]{1,0:T(8,128)(2,1)S(1)}, u32[]{:S(2)}, u32[]{:S(2)}) collective-permute-start(bf16[288,256]{1,0:T(8,128)(2,1)S(1)} %get-tuple-element.84), channel_id=1, source_target_pairs={{0,2},{2,0},{4,6},{6,4},{1,3},{3,1},{5,7},{7,5},{8,10},{10,8},{12,... | collective-permute-start | bytes 442376 | tf_op jit(solution)/shard_map/ppermute | solution.py:514
  75.5 4.7 %collective-permute-start.12 = (bf16[288,256]{1,0:T(8,128)(2,1)S(1)}, bf16[288,256]{1,0:T(8,128)(2,1)S(1)}, u32[]{:S(2)}, u32[]{:S(2)}) collective-permute-start(bf16[288,256]{1,0:T(8,128)(2,1)S(1)} %get-tuple-element.85), channel_id=1, source_target_pairs={{0,4},{2,6},{4,0},{6,2},{1,5},{3,7},{5,1},{7,3},{8,12},{10,14},{12... | collective-permute-start | bytes 442376 | tf_op jit(solution)/shard_map/ppermute | solution.py:514
  76.7 6.1 %collective-permute-start.13 = (bf16[288,256]{1,0:T(8,128)(2,1)S(1)}, bf16[288,256]{1,0:T(8,128)(2,1)S(1)}, u32[]{:S(2)}, u32[]{:S(2)}) collective-permute-start(bf16[288,256]{1,0:T(8,128)(2,1)S(1)} %get-tuple-element.86), channel_id=1, source_target_pairs={{0,6},{2,4},{4,2},{6,0},{1,7},{3,5},{5,3},{7,1},{8,14},{10,12},{12... | collective-permute-start | bytes 442376 | tf_op jit(solution)/shard_map/ppermute | solution.py:514
  76.9 6.8 %collective-permute-start.14 = (bf16[288,256]{1,0:T(8,128)(2,1)S(1)}, bf16[288,256]{1,0:T(8,128)(2,1)S(1)}, u32[]{:S(2)}, u32[]{:S(2)}) collective-permute-start(bf16[288,256]{1,0:T(8,128)(2,1)S(1)} %get-tuple-element.88.refs_1_), channel_id=1, source_target_pairs={{0,16},{8,24},{16,0},{24,8},{1,17},{9,25},{17,1},{25,9},{2,18},{10... | collective-permute-start | bytes 442376 | tf_op jit(solution)/shard_map/ppermute | solution.py:563
  82.9 6.5 %collective-permute-start.15 = (bf16[288,256]{1,0:T(8,128)(2,1)S(1)}, bf16[288,256]{1,0:T(8,128)(2,1)S(1)}, u32[]{:S(2)}, u32[]{:S(2)}) collective-permute-start(bf16[288,256]{1,0:T(8,128)(2,1)S(1)} %get-tuple-element.90.refs_1_), channel_id=1, source_target_pairs={{0,8},{8,0},{16,24},{24,16},{1,9},{9,1},{17,25},{25,17},{2,10},{10... | collective-permute-start | bytes 442376 | tf_op jit(solution)/shard_map/ppermute | solution.py:563
  83.7 12.4 %collective-permute-start.19 = (bf16[288,256]{1,0:T(8,128)(2,1)S(1)}, bf16[288,256]{1,0:T(8,128)(2,1)S(1)}, u32[]{:S(2)}, u32[]{:S(2)}) collective-permute-start(bf16[288,256]{1,0:T(8,128)(2,1)S(1)} %get-tuple-element.96.refs_1_), channel_id=1, source_target_pairs={{0,6},{2,4},{4,2},{6,0},{1,7},{3,5},{5,3},{7,1},{8,14},{10,12},{12... | collective-permute-start | bytes 442376 | tf_op jit(solution)/shard_map/ppermute | solution.py:514
  89.0 7.2 %collective-permute-start.18 = (bf16[288,256]{1,0:T(8,128)(2,1)S(1)}, bf16[288,256]{1,0:T(8,128)(2,1)S(1)}, u32[]{:S(2)}, u32[]{:S(2)}) collective-permute-start(bf16[288,256]{1,0:T(8,128)(2,1)S(1)} %get-tuple-element.96.refs_1_), channel_id=1, source_target_pairs={{0,4},{2,6},{4,0},{6,2},{1,5},{3,7},{5,1},{7,3},{8,12},{10,14},{12... | collective-permute-start | bytes 442376 | tf_op jit(solution)/shard_map/ppermute | solution.py:514
  89.3 6.9 %collective-permute-start.17 = (bf16[288,256]{1,0:T(8,128)(2,1)S(1)}, bf16[288,256]{1,0:T(8,128)(2,1)S(1)}, u32[]{:S(2)}, u32[]{:S(2)}) collective-permute-start(bf16[288,256]{1,0:T(8,128)(2,1)S(1)} %get-tuple-element.96.refs_1_), channel_id=1, source_target_pairs={{0,2},{2,0},{4,6},{6,4},{1,3},{3,1},{5,7},{7,5},{8,10},{10,8},{12,... | collective-permute-start | bytes 442376 | tf_op jit(solution)/shard_map/ppermute | solution.py:514
  89.4 6.7 %collective-permute-start.16 = (bf16[288,256]{1,0:T(8,128)(2,1)S(1)}, bf16[288,256]{1,0:T(8,128)(2,1)S(1)}, u32[]{:S(2)}, u32[]{:S(2)}) collective-permute-start(bf16[288,256]{1,0:T(8,128)(2,1)S(1)} %get-tuple-element.94.refs_1_), channel_id=1, source_target_pairs={{0,16},{8,24},{16,0},{24,8},{1,17},{9,25},{17,1},{25,9},{2,18},{10... | collective-permute-start | bytes 442376 | tf_op jit(solution)/shard_map/ppermute | solution.py:563
  96.2 5.5 %collective-permute-start.20 = (bf16[4,288,256]{2,1,0:T(8,128)(2,1)S(1)}, bf16[4,288,256]{2,1,0:T(8,128)(2,1)S(1)}, u32[]{:S(2)}, u32[]{:S(2)}) collective-permute-start(bf16[4,288,256]{2,1,0:T(8,128)(2,1)S(1)} %get-tuple-element.98.refs_2_), channel_id=1, source_target_pairs={{0,1},{1,0},{2,3},{3,2},{4,5},{5,4},{6,7},{7,6},{8,9},{9,8},{10,11... | collective-permute-start | bytes 1769480 | tf_op jit(solution)/shard_map/ppermute | solution.py:576
  99.1 6.3 %collective-permute-start.23 = (bf16[288,256]{1,0:T(8,128)(2,1)S(1)}, bf16[288,256]{1,0:T(8,128)(2,1)S(1)}, u32[]{:S(2)}, u32[]{:S(2)}) collective-permute-start(bf16[288,256]{1,0:T(8,128)(2,1)S(1)} %get-tuple-element.100.refs_1_), channel_id=1, source_target_pairs={{0,6},{2,4},{4,2},{6,0},{1,7},{3,5},{5,3},{7,1},{8,14},{10,12},{12... | collective-permute-start | bytes 442376 | tf_op jit(solution)/shard_map/ppermute | solution.py:514
  100.9 7.4 %collective-permute-start.22 = (bf16[288,256]{1,0:T(8,128)(2,1)S(1)}, bf16[288,256]{1,0:T(8,128)(2,1)S(1)}, u32[]{:S(2)}, u32[]{:S(2)}) collective-permute-start(bf16[288,256]{1,0:T(8,128)(2,1)S(1)} %get-tuple-element.100.refs_1_), channel_id=1, source_target_pairs={{0,4},{2,6},{4,0},{6,2},{1,5},{3,7},{5,1},{7,3},{8,12},{10,14},{12... | collective-permute-start | bytes 442376 | tf_op jit(solution)/shard_map/ppermute | solution.py:514
  101.2 7.8 %collective-permute-start.21 = (bf16[288,256]{1,0:T(8,128)(2,1)S(1)}, bf16[288,256]{1,0:T(8,128)(2,1)S(1)}, u32[]{:S(2)}, u32[]{:S(2)}) collective-permute-start(bf16[288,256]{1,0:T(8,128)(2,1)S(1)} %get-tuple-element.100.refs_1_), channel_id=1, source_target_pairs={{0,2},{2,0},{4,6},{6,4},{1,3},{3,1},{5,7},{7,5},{8,10},{10,8},{12,... | collective-permute-start | bytes 442376 | tf_op jit(solution)/shard_map/ppermute | solution.py:514
  (8 other events, 51.7 us)

commit v6 on v5

--- a/solution.py
+++ b/solution.py
@@ -491,6 +491,11 @@
     refs[-1][...] = total.astype(BF16)
 
 
+def copy_kernel(first_ref, last_ref, first_out_ref, last_out_ref):
+    first_out_ref[...] = first_ref[...]
+    last_out_ref[...] = last_ref[...]
+
+
 def pack_kernel(*refs):
     for k, ref in enumerate(refs[:-1]):
         refs[-1][k] = ref[...]
@@ -529,7 +534,7 @@
     deep = lax.axis_size("a")
     lines = rows * width
 
-    up, down = row_halo(*edge_rows(places, x, cot, block))
+    up, down = row_halo(*edge_rows(places, x, cot, frames))
     x_part, x_taps = interior_conv(x, in_kernel, False, block)
     cot_part, cot_taps = interior_conv(cot, out_kernel, True, block)
     states, running, end = local_scan(x_part, up, down, 0, x_taps, decays, block, False, decays)
@@ -546,7 +551,6 @@
         places, ends, pair, states, running, cot, up, down, 1, None, block
     )
     got = lax.ppermute(sent, "core", CORES)
-    low_up, low_down = row_halo(low_first, low_last)
     half, q = kept.shape
     part_shape = (half // 4, q)
 
@@ -584,13 +588,20 @@
         places, ends, pair, adjoint, trailing, x, up, down, 0, decays, block, [token]
     )
     got = lax.ppermute(sent, "core", CORES)
-    out_part, token = sums("out_share", None, [own] + others, [token, low_up, low_down], mib=FAR)
+    out_part, token = sums("out_share", None, [own] + others, [token], mib=FAR)
     out_other = swapped(out_part, 1)
     own, others, token = add("in_add", kept, got, [token])
     out_part, out_other, token = middle("out_mid", out_part, out_other, [token], FAR)
+    line = (low_first.shape, BF16)
+    low_first, low_last, _ = small_call(
+        copy_kernel, "low_edges", [line, line], [low_first, low_last], [token]
+    )
+    low_up, low_down = row_halo(low_first, low_last)
     in_part, token = sums("in_share", None, [own] + others, [token])
     in_other = swapped(in_part, 1)
-    out_part, token = sums("out_total", grad_scale, [out_part, out_other], [token], mib=FAR)
+    out_part, token = sums(
+        "out_total", grad_scale, [out_part, out_other], [token], mib=FAR
+    )
     out_others = from_others(out_part, ("x", "y"))
     in_part, in_other, token = middle("in_mid", in_part, in_other, [token])
     outputs, token = outputs_conv(

time: 114 us -> 116 us (1.018)
  waiting for transfers between devices: 21.1 us -> 24.1 us
  starting transfers between devices: 33.9 us -> 32.5 us
    ppermute x12, waiting for transfers between devices: 10.6 us -> 5.09 us  [from_others(): lax.ppermute(part, axes, [(i, i ^ k) for i in range(count)])]
    ppermute x2, waiting for transfers between devices: 5.08 us -> 9.61 us  [row_halo(): down = lax.ppermute(first, axes, [(i + 1, i) for i in range(count - 1)])]
    ppermute x4, starting transfers between devices: 1.09 us -> 4.21 us  [swapped(): return lax.ppermute(part, 'a', [(i, i ^ bit) for i in range(deep)])]
    ppermute x2, starting transfers between devices: 3.4 us -> 0.63 us  [pack(): return (packed, lax.ppermute(packed, 'core', CORES), token)]
    ppermute x2, waiting for transfers between devices: 0.23 us -> 3 us  [per_device(): got = lax.ppermute(sent, 'core', CORES)]
    ppermute x12, starting transfers between devices: 14 us -> 12.2 us  [from_others(): lax.ppermute(part, axes, [(i, i ^ k) for i in range(count)])]
    ppermute x4, waiting for transfers between devices: 0.72 us -> 1.99 us  [swapped(): return lax.ppermute(part, 'a', [(i, i ^ bit) for i in range(deep)])]
    pallas_call x13 -> x14, Pallas kernels: 7.09 us -> 7.73 us  [small_call(): pl.pallas_call(kernel, in_specs=[ANYWHERE] * len(after) + [SCALARS] * len...]
  transfers between devices with their start and end apart: 25 -> 25, of which waited for: 13 -> 13; matrix products, arithmetic and copies ran while one was open for 0% -> 0% of each run, Pallas kernels for 25% -> 24%
where the time goes in v6:
time: 116 us
  Pallas kernels  46.7 us (40%)
  starting transfers between devices  32.5 us (28%)
  waiting for transfers between devices  24.1 us (21%)
  blocking collectives  11 us (9%)
    ppermute x12, starting transfers between devices, from_others(): lax.ppermute(part, axes, [(i, i ^ k) for i in range(count)])  12.2 us
    all_to_all x1, blocking collectives, per_device(): ends = lax.all_to_all(ends, 'a', 0, 0)  11 us
    ppermute x2, waiting for transfers between devices, row_halo(): down = lax.ppermute(first, axes, [(i + 1, i) for i in range(count - 1)])  9.61 us
    ppermute x2, starting transfers between devices, row_halo(): up = lax.ppermute(last, axes, [(i, i + 1) for i in range(count - 1)])  9.07 us
    pallas_call x1, Pallas kernels, kernel_grads(): pl.pallas_call(in_grad_kernel, grid=(frames // block,), in_specs=lead + [...  7.83 us
    pallas_call x14, Pallas kernels, small_call(): pl.pallas_call(kernel, in_specs=[ANYWHERE] * len(after) + [SCALARS] * len...  7.73 us
    pallas_call x1, Pallas kernels, kernel_grads(): pl.pallas_call(out_grad_kernel, grid=(frames // block,), in_specs=lead +...  7.27 us
    pallas_call x1, Pallas kernels, outputs_conv(): pl.pallas_call(outputs_kernel, grid=(frames // block,), in_specs=[pl.Bloc...  6.63 us
  transfers between devices with their start and end apart: 25, of which 13 were waited for; matrix products, arithmetic and copies ran while one was open for 0% of the time, Pallas kernels for 24%

profile of v6, /device:TPU:1, one launch (start us, length us, event | category | flops | bytes accessed | tf_op | source)
XLA Modules:
  0.0 115.9 jit_solution(6594255822245640141)
XLA Ops:
  1.2 3.1 %edge_rows.1 = (bf16[2,64,16,256]{3,2,1,0:T(8,128)(2,1)}, bf16[2,64,16,256]{3,2,1,0:T(8,128)(2,1)}) custom-call(s32[4]{0:T(128)} %pad_add_fusion.places_ref.refs_0_.place_ref.refs_1_, bf16[64,4,16,256]{3,2,1,0:T(8,128)(2,1)} %bitcast.16, bf16[64,4,16,256]{3,2,1,0:T(8,128)(2,1)} %bitcast.17, bf16[64,4,16,256]{3,2,1,0:T(8,128)(2,1)} %bitcast.12, ...), custom_call_target="tpu_custom_call" | custom-call | bytes 4194304 | tf_op jit(solution)/shard_map/edge_rows/pallas_call | solution.py:427
  4.3 4.5 %collective-permute-start = (bf16[2,64,16,256]{3,2,1,0:T(8,128)(2,1)}, bf16[2,64,16,256]{3,2,1,0:T(8,128)(2,1)S(1)}, u32[]{:S(2)}, u32[]{:S(2)}) collective-permute-start(bf16[2,64,16,256]{3,2,1,0:T(8,128)(2,1)} %get-tuple-element.57), channel_id=1, source_target_pairs={{0,1},{1,2},{2,3},{4,5},{5,6},{6,7},{8,9},{9,10},{10,11},{12,13},{... | collective-permute-start | bytes 3145736 | tf_op jit(solution)/shard_map/ppermute | solution.py:442
  8.9 1.9 %collective-permute-start.1 = (bf16[2,64,16,256]{3,2,1,0:T(8,128)(2,1)}, bf16[2,64,16,256]{3,2,1,0:T(8,128)(2,1)S(1)}, u32[]{:S(2)}, u32[]{:S(2)}) collective-permute-start(bf16[2,64,16,256]{3,2,1,0:T(8,128)(2,1)} %get-tuple-element.58), channel_id=1, source_target_pairs={{1,0},{2,1},{3,2},{5,4},{6,5},{7,6},{9,8},{10,9},{11,10},{13,12},{... | collective-permute-start | bytes 3145736 | tf_op jit(solution)/shard_map/ppermute | solution.py:443
  10.8 4.8 %interior_in.1.part_ref = f32[4,64,16,256]{3,2,1,0:T(8,128)S(1)} custom-call(bf16[64,4,16,256]{3,2,1,0:T(8,128)(2,1)S(1)} %bitcast.18, bf16[3,768,256]{2,1,0:T(8,128)(2,1)S(1)} %bitcast.21), custom_call_target="tpu_custom_call" | custom-call | flops 4831838208 | bytes 8388608 | tf_op jit(solution)/shard_map/interior_in/pallas_call | solution.py:106
  15.6 5.2 %interior_cot.1 = (f32[4,64,16,256]{3,2,1,0:T(8,128)S(1)}, bf16[3,768,256]{2,1,0:T(8,128)(2,1)S(1)}) custom-call(bf16[64,4,16,256]{3,2,1,0:T(8,128)(2,1)S(1)} %bitcast.14, bf16[3,3,256,256]{3,2,1,0:T(8,128)(2,1)S(1)} %copy-done.5), custom_call_target="tpu_custom_call" | custom-call | flops 4831838208 | bytes 8388608 | tf_op jit(solution)/shard_map/interior_cot/pallas_call | solution.py:91
  20.9 4.3 %collective-permute-done.1.down_ref = bf16[2,64,16,256]{3,2,1,0:T(8,128)(2,1)S(1)} collective-permute-done((bf16[2,64,16,256]{3,2,1,0:T(8,128)(2,1)}, bf16[2,64,16,256]{3,2,1,0:T(8,128)(2,1)S(1)}, u32[]{:S(2)}, u32[]{:S(2)}) %collective-permute-start.1) | collective-permute-done | bytes 1048608 | tf_op jit(solution)/shard_map/ppermute | solution.py:443
  25.2 2.0 %scan_fwd.1 = (f32[4,64,16,256]{3,2,1,0:T(8,128)S(1)}, f32[64,256]{1,0:T(8,128)S(1)}, f32[64,256]{1,0:T(8,128)S(1)}) custom-call(f32[4,64,16,256]{3,2,1,0:T(8,128)S(1)} %interior_in.1.part_ref, bf16[2,64,16,256]{3,2,1,0:T(8,128)(2,1)S(1)} %collective-permute-done.up_ref, bf16[2,64,16,256]{3,2,1,0:T(8,128)(2,1)S(1)} %collective-permute-done.1.down_ref, ...), custom_call_target="tpu_custom_call" | custom-call | flops 805306368 | bytes 12582912 | tf_op jit(solution)/shard_map/scan_fwd/pallas_call | solution.py:180
  27.3 2.2 %scan_back.1 = (f32[4,64,16,256]{3,2,1,0:T(8,128)S(1)}, f32[64,256]{1,0:T(8,128)S(1)}, f32[136,256]{1,0:T(8,128)S(1)}) custom-call(f32[4,64,16,256]{3,2,1,0:T(8,128)S(1)} %get-tuple-element.56.part_ref, bf16[2,64,16,256]{3,2,1,0:T(8,128)(2,1)S(1)} %collective-permute-done.up_ref, bf16[2,64,16,256]{3,2,1,0:T(8,128)(2,1)S(1)} %collective-permute-done.1.down_ref, ...), custom_call_target="tpu_custom_call" | custom-call | flops 805306368 | bytes 12582912 | tf_op jit(solution)/shard_map/scan_back/pallas_call | solution.py:180
  30.7 2.7 %collective-permute-done.2.refs_2_.pair_ref = f32[136,256]{1,0:T(8,128)S(1)} collective-permute-done((f32[136,256]{1,0:T(8,128)S(1)}, f32[136,256]{1,0:T(8,128)S(1)}, u32[]{:S(2)}, u32[]{:S(2)}) %collective-permute-start.2) | collective-permute-done | bytes 139296 | tf_op jit(solution)/shard_map/ppermute | solution.py:544
  34.5 11.0 %all_to_all.5.ends_ref = f32[4,72,256]{2,1,0:T(8,128)S(1)} all-to-all(f32[4,72,256]{2,1,0:T(8,128)S(1)} %get-tuple-element.62), channel_id=1, replica_groups=mesh['a'=4,'x'=2,'y'=2,'core'=2] {'a'}, dimensions={0} | all-to-all | bytes 589824 | tf_op jit(solution)/shard_map/all_to_all | solution.py:548
  45.6 7.3 %out_grad.1 = (bf16[4,64,16,256]{3,2,1,0:T(8,128)(2,1)S(1)}, bf16[64,16,256]{2,1,0:T(8,128)(2,1)S(1)}, bf16[64,16,256]{2,1,0:T(8,128)(2,1)S(1)}, bf16[1152,256]{...) custom-call(s32[4]{0:T(128)S(1)} %copy-done.4, f32[4,72,256]{2,1,0:T(8,128)S(1)} %all_to_all.5.ends_ref, ...), custom_call_target="tpu_custom_call" | custom-call | flops 4831838208 | bytes 10485760 | tf_op jit(solution)/shard_map/out_grad/pallas_call | solution.py:349
  52.9 2.0 %collective-permute-done.3.refs_3_ = bf16[1152,256]{1,0:T(8,128)(2,1)S(1)} collective-permute-done((bf16[1152,256]{1,0:T(8,128)(2,1)S(1)}, bf16[1152,256]{1,0:T(8,128)(2,1)S(1)}, u32[]{:S(2)}, u32[]{:S(2)}) %collective-permute-start.3) | collective-permute-done | bytes 589856 | tf_op jit(solution)/shard_map/ppermute | solution.py:553
  55.6 2.3 %collective-permute-start.4 = (bf16[288,256]{1,0:T(8,128)(2,1)S(1)}, bf16[288,256]{1,0:T(8,128)(2,1)S(1)}, u32[]{:S(2)}, u32[]{:S(2)}) collective-permute-start(bf16[288,256]{1,0:T(8,128)(2,1)S(1)} %get-tuple-element.74), channel_id=1, source_target_pairs={{0,2},{2,0},{4,6},{6,4},{1,3},{3,1},{5,7},{7,5},{8,10},{10,8},{12,... | collective-permute-start | bytes 442376 | tf_op jit(solution)/shard_map/ppermute | solution.py:519
  59.1 7.8 %in_grad.1 = (bf16[1152,256]{1,0:T(8,128)(2,1)S(1)}, f32[1152,256]{1,0:T(8,128)S(1)}, f32[8,128]{1,0:T(8,128)S(1)}) custom-call(s32[4]{0:T(128)S(1)} %copy-done.4, f32[4,72,256]{2,1,0:T(8,128)S(1)} %all_to_all.5.ends_ref, f32[136,256]{1,0:T(8,128)S(1)} %collective-permute-done.2.refs_2_.pair_ref, f32[4,64,16,256]{3,2,1,0:T(8,128)S(1)} %get-tuple-element.66.local_ref, ...), custom_call_target="tpu_custom_call" | custom-call | flops 4831838208 | bytes 10485760 | tf_op jit(solution)/shard_map/in_grad/pallas_call | solution.py:360
  70.3 1.7 %collective-permute-start.11 = (bf16[288,256]{1,0:T(8,128)(2,1)S(1)}, bf16[288,256]{1,0:T(8,128)(2,1)S(1)}, u32[]{:S(2)}, u32[]{:S(2)}) collective-permute-start(bf16[288,256]{1,0:T(8,128)(2,1)S(1)} %get-tuple-element.88), channel_id=1, source_target_pairs={{0,2},{2,0},{4,6},{6,4},{1,3},{3,1},{5,7},{7,5},{8,10},{10,8},{12,... | collective-permute-start | bytes 442376 | tf_op jit(solution)/shard_map/ppermute | solution.py:519
  74.7 4.5 %collective-permute-start.9 = (bf16[64,16,256]{2,1,0:T(8,128)(2,1)S(1)}, bf16[64,16,256]{2,1,0:T(8,128)(2,1)S(1)}, u32[]{:S(2)}, u32[]{:S(2)}) collective-permute-start(bf16[64,16,256]{2,1,0:T(8,128)(2,1)S(1)} %get-tuple-element.85), channel_id=1, source_target_pairs={{0,1},{1,2},{2,3},{4,5},{5,6},{6,7},{8,9},{9,10},{10,11},{12,13},{... | collective-permute-start | bytes 1572872 | tf_op jit(solution)/shard_map/ppermute | solution.py:442
  79.3 2.1 %collective-permute-start.10 = (bf16[64,16,256]{2,1,0:T(8,128)(2,1)S(1)}, bf16[64,16,256]{2,1,0:T(8,128)(2,1)S(1)}, u32[]{:S(2)}, u32[]{:S(2)}) collective-permute-start(bf16[64,16,256]{2,1,0:T(8,128)(2,1)S(1)} %get-tuple-element.86), channel_id=1, source_target_pairs={{1,0},{2,1},{3,2},{5,4},{6,5},{7,6},{9,8},{10,9},{11,10},{13,12},{... | collective-permute-start | bytes 1572872 | tf_op jit(solution)/shard_map/ppermute | solution.py:443
  83.4 2.7 %collective-permute-start.19 = (bf16[288,256]{1,0:T(8,128)(2,1)S(1)}, bf16[288,256]{1,0:T(8,128)(2,1)S(1)}, u32[]{:S(2)}, u32[]{:S(2)}) collective-permute-start(bf16[288,256]{1,0:T(8,128)(2,1)S(1)} %get-tuple-element.100.refs_1_), channel_id=1, source_target_pairs={{0,6},{2,4},{4,2},{6,0},{1,7},{3,5},{5,3},{7,1},{8,14},{10,12},{12... | collective-permute-start | bytes 442376 | tf_op jit(solution)/shard_map/ppermute | solution.py:519
  87.3 2.2 %collective-permute-start.16 = (bf16[288,256]{1,0:T(8,128)(2,1)S(1)}, bf16[288,256]{1,0:T(8,128)(2,1)S(1)}, u32[]{:S(2)}, u32[]{:S(2)}) collective-permute-start(bf16[288,256]{1,0:T(8,128)(2,1)S(1)} %get-tuple-element.98.refs_1_), channel_id=1, source_target_pairs={{0,16},{8,24},{16,0},{24,8},{1,17},{9,25},{17,1},{25,9},{2,18},{10... | collective-permute-start | bytes 442376 | tf_op jit(solution)/shard_map/ppermute | solution.py:567
  89.5 5.3 %collective-permute-done.10.down_ref = bf16[64,16,256]{2,1,0:T(8,128)(2,1)S(1)} collective-permute-done((bf16[64,16,256]{2,1,0:T(8,128)(2,1)S(1)}, bf16[64,16,256]{2,1,0:T(8,128)(2,1)S(1)}, u32[]{:S(2)}, u32[]{:S(2)}) %collective-permute-start.10) | collective-permute-done | bytes 524320 | tf_op jit(solution)/shard_map/ppermute | solution.py:443
  94.8 6.6 %outputs_conv.1 = (bf16[64,4,16,256]{3,2,1,0:T(8,128)(2,1)}, f32[8,128]{1,0:T(8,128)S(1)}) custom-call(bf16[4,64,16,256]{3,2,1,0:T(8,128)(2,1)S(1)} %get-tuple-element.65.low_ref, bf16[64,16,256]{2,1,0:T(8,128)(2,1)S(1)} %collective-permute-done.9.up_ref, bf16[64,16,256]{2,1,0:T(8,128)(2,1)S(1)} %collective-permute-done.10.down_ref, ...), custom_call_target="tpu_custom_call" | custom-call | flops 4831838208 | bytes 8388608 | tf_op jit(solution)/shard_map/outputs_conv/pallas_call | solution.py:393
  104.4 2.1 %out_merge.1 = (f32[2304,256]{1,0:T(8,128)}, f32[8,128]{1,0:T(8,128)S(1)}) custom-call(f32[8,128]{1,0:T(8,128)S(1)} %get-tuple-element.101.refs_0_, s32[4]{0:T(128)S(1)} %copy-done.4, bf16[4,288,256]{2,1,0:T(8,128)(2,1)S(1)} %get-tuple-element.102.refs_2_, bf16[4,288,256]{2,1,0:T(8,128)(2,1)S(1)} %collective-permute-done.20.refs_3_), custom_call_target="tpu_custom_call" | custom-call | flops 34359738368 | bytes 2097152 | tf_op jit(solution)/shard_map/out_merge/pallas_call | solution.py:459
  107.7 2.3 %collective-permute-done.22.refs_3_ = bf16[288,256]{1,0:T(8,128)(2,1)S(1)} collective-permute-done((bf16[288,256]{1,0:T(8,128)(2,1)S(1)}, bf16[288,256]{1,0:T(8,128)(2,1)S(1)}, u32[]{:S(2)}, u32[]{:S(2)}) %collective-permute-start.22) | collective-permute-done | bytes 147488 | tf_op jit(solution)/shard_map/ppermute | solution.py:519
  113.8 2.1 %in_merge.1 = (f32[2304,256]{1,0:T(8,128)}, f32[8,128]{1,0:T(8,128)}) custom-call(f32[8,128]{1,0:T(8,128)S(1)} %get-tuple-element.105.refs_0_, s32[4]{0:T(128)S(1)} %copy-done.4, bf16[4,288,256]{2,1,0:T(8,128)(2,1)S(1)} %get-tuple-element.106.refs_2_, bf16[4,288,256]{2,1,0:T(8,128)(2,1)S(1)} %collective-permute-done.24.refs_3_), custom_call_target="tpu_custom_call" | custom-call | flops 1073741824 | bytes 2097152 | tf_op jit(solution)/shard_map/in_merge/pallas_call | solution.py:459
  (64 shorter events, 22.1 us)
Async XLA Ops:
  4.3 16.6 %collective-permute-start = (bf16[2,64,16,256]{3,2,1,0:T(8,128)(2,1)}, bf16[2,64,16,256]{3,2,1,0:T(8,128)(2,1)S(1)}, u32[]{:S(2)}, u32[]{:S(2)}) collective-permute-start(bf16[2,64,16,256]{3,2,1,0:T(8,128)(2,1)} %get-tuple-element.57), channel_id=1, source_target_pairs={{0,1},{1,2},{2,3},{4,5},{5,6},{6,7},{8,9},{9,10},{10,11},{12,13},{... | collective-permute-start | bytes 3145736 | tf_op jit(solution)/shard_map/ppermute | solution.py:442
  8.9 16.3 %collective-permute-start.1 = (bf16[2,64,16,256]{3,2,1,0:T(8,128)(2,1)}, bf16[2,64,16,256]{3,2,1,0:T(8,128)(2,1)S(1)}, u32[]{:S(2)}, u32[]{:S(2)}) collective-permute-start(bf16[2,64,16,256]{3,2,1,0:T(8,128)(2,1)} %get-tuple-element.58), channel_id=1, source_target_pairs={{1,0},{2,1},{3,2},{5,4},{6,5},{7,6},{9,8},{10,9},{11,10},{13,12},{... | collective-permute-start | bytes 3145736 | tf_op jit(solution)/shard_map/ppermute | solution.py:443
  29.4 4.0 %collective-permute-start.2 = (f32[136,256]{1,0:T(8,128)S(1)}, f32[136,256]{1,0:T(8,128)S(1)}, u32[]{:S(2)}, u32[]{:S(2)}) collective-permute-start(f32[136,256]{1,0:T(8,128)S(1)} %get-tuple-element.61.refs_1_), channel_id=1, source_target_pairs={{0,4},{4,0},{1,5},{5,1},{2,6},{6,2},{3,7},{7,3},{8,12},{12,8},{9,1... | collective-permute-start | bytes 417800 | tf_op jit(solution)/shard_map/ppermute | solution.py:544
  55.6 12.4 %collective-permute-start.4 = (bf16[288,256]{1,0:T(8,128)(2,1)S(1)}, bf16[288,256]{1,0:T(8,128)(2,1)S(1)}, u32[]{:S(2)}, u32[]{:S(2)}) collective-permute-start(bf16[288,256]{1,0:T(8,128)(2,1)S(1)} %get-tuple-element.74), channel_id=1, source_target_pairs={{0,2},{2,0},{4,6},{6,4},{1,3},{3,1},{5,7},{7,5},{8,10},{10,8},{12,... | collective-permute-start | bytes 442376 | tf_op jit(solution)/shard_map/ppermute | solution.py:519
  57.9 10.1 %collective-permute-start.5 = (bf16[288,256]{1,0:T(8,128)(2,1)S(1)}, bf16[288,256]{1,0:T(8,128)(2,1)S(1)}, u32[]{:S(2)}, u32[]{:S(2)}) collective-permute-start(bf16[288,256]{1,0:T(8,128)(2,1)S(1)} %get-tuple-element.75), channel_id=1, source_target_pairs={{0,4},{2,6},{4,0},{6,2},{1,5},{3,7},{5,1},{7,3},{8,12},{10,14},{12... | collective-permute-start | bytes 442376 | tf_op jit(solution)/shard_map/ppermute | solution.py:519
  59.1 8.9 %collective-permute-start.6 = (bf16[288,256]{1,0:T(8,128)(2,1)S(1)}, bf16[288,256]{1,0:T(8,128)(2,1)S(1)}, u32[]{:S(2)}, u32[]{:S(2)}) collective-permute-start(bf16[288,256]{1,0:T(8,128)(2,1)S(1)} %get-tuple-element.76), channel_id=1, source_target_pairs={{0,6},{2,4},{4,2},{6,0},{1,7},{3,5},{5,3},{7,1},{8,14},{10,12},{12... | collective-permute-start | bytes 442376 | tf_op jit(solution)/shard_map/ppermute | solution.py:519
  67.0 2.6 %collective-permute-start.7 = (bf16[1152,256]{1,0:T(8,128)(2,1)S(1)}, bf16[1152,256]{1,0:T(8,128)(2,1)S(1)}, u32[]{:S(2)}, u32[]{:S(2)}) collective-permute-start(bf16[1152,256]{1,0:T(8,128)(2,1)S(1)} %get-tuple-element.79), channel_id=1, source_target_pairs={{0,1},{1,0},{2,3},{3,2},{4,5},{5,4},{6,7},{7,6},{8,9},{9,8},{10,11... | collective-permute-start | bytes 1769480 | tf_op jit(solution)/shard_map/ppermute | solution.py:590
  68.0 5.5 %collective-permute-start.8 = (bf16[288,256]{1,0:T(8,128)(2,1)S(1)}, bf16[288,256]{1,0:T(8,128)(2,1)S(1)}, u32[]{:S(2)}, u32[]{:S(2)}) collective-permute-start(bf16[288,256]{1,0:T(8,128)(2,1)S(1)} %get-tuple-element.81.refs_1_), channel_id=1, source_target_pairs={{0,8},{8,0},{16,24},{24,16},{1,9},{9,1},{17,25},{25,17},{2,10},{10... | collective-permute-start | bytes 442376 | tf_op jit(solution)/shard_map/ppermute | solution.py:567
  70.3 9.0 %collective-permute-start.11 = (bf16[288,256]{1,0:T(8,128)(2,1)S(1)}, bf16[288,256]{1,0:T(8,128)(2,1)S(1)}, u32[]{:S(2)}, u32[]{:S(2)}) collective-permute-start(bf16[288,256]{1,0:T(8,128)(2,1)S(1)} %get-tuple-element.88), channel_id=1, source_target_pairs={{0,2},{2,0},{4,6},{6,4},{1,3},{3,1},{5,7},{7,5},{8,10},{10,8},{12,... | collective-permute-start | bytes 442376 | tf_op jit(solution)/shard_map/ppermute | solution.py:519
  72.0 9.4 %collective-permute-start.12 = (bf16[288,256]{1,0:T(8,128)(2,1)S(1)}, bf16[288,256]{1,0:T(8,128)(2,1)S(1)}, u32[]{:S(2)}, u32[]{:S(2)}) collective-permute-start(bf16[288,256]{1,0:T(8,128)(2,1)S(1)} %get-tuple-element.89), channel_id=1, source_target_pairs={{0,4},{2,6},{4,0},{6,2},{1,5},{3,7},{5,1},{7,3},{8,12},{10,14},{12... | collective-permute-start | bytes 442376 | tf_op jit(solution)/shard_map/ppermute | solution.py:519
  73.2 8.2 %collective-permute-start.13 = (bf16[288,256]{1,0:T(8,128)(2,1)S(1)}, bf16[288,256]{1,0:T(8,128)(2,1)S(1)}, u32[]{:S(2)}, u32[]{:S(2)}) collective-permute-start(bf16[288,256]{1,0:T(8,128)(2,1)S(1)} %get-tuple-element.90), channel_id=1, source_target_pairs={{0,6},{2,4},{4,2},{6,0},{1,7},{3,5},{5,3},{7,1},{8,14},{10,12},{12... | collective-permute-start | bytes 442376 | tf_op jit(solution)/shard_map/ppermute | solution.py:519
  73.6 9.7 %collective-permute-start.14 = (bf16[288,256]{1,0:T(8,128)(2,1)S(1)}, bf16[288,256]{1,0:T(8,128)(2,1)S(1)}, u32[]{:S(2)}, u32[]{:S(2)}) collective-permute-start(bf16[288,256]{1,0:T(8,128)(2,1)S(1)} %get-tuple-element.92.refs_1_), channel_id=1, source_target_pairs={{0,16},{8,24},{16,0},{24,8},{1,17},{9,25},{17,1},{25,9},{2,18},{10... | collective-permute-start | bytes 442376 | tf_op jit(solution)/shard_map/ppermute | solution.py:567
  74.7 12.6 %collective-permute-start.9 = (bf16[64,16,256]{2,1,0:T(8,128)(2,1)S(1)}, bf16[64,16,256]{2,1,0:T(8,128)(2,1)S(1)}, u32[]{:S(2)}, u32[]{:S(2)}) collective-permute-start(bf16[64,16,256]{2,1,0:T(8,128)(2,1)S(1)} %get-tuple-element.85), channel_id=1, source_target_pairs={{0,1},{1,2},{2,3},{4,5},{5,6},{6,7},{8,9},{9,10},{10,11},{12,13},{... | collective-permute-start | bytes 1572872 | tf_op jit(solution)/shard_map/ppermute | solution.py:442
  79.3 15.5 %collective-permute-start.10 = (bf16[64,16,256]{2,1,0:T(8,128)(2,1)S(1)}, bf16[64,16,256]{2,1,0:T(8,128)(2,1)S(1)}, u32[]{:S(2)}, u32[]{:S(2)}) collective-permute-start(bf16[64,16,256]{2,1,0:T(8,128)(2,1)S(1)} %get-tuple-element.86), channel_id=1, source_target_pairs={{1,0},{2,1},{3,2},{5,4},{6,5},{7,6},{9,8},{10,9},{11,10},{13,12},{... | collective-permute-start | bytes 1572872 | tf_op jit(solution)/shard_map/ppermute | solution.py:443
  81.5 5.7 %collective-permute-start.15 = (bf16[288,256]{1,0:T(8,128)(2,1)S(1)}, bf16[288,256]{1,0:T(8,128)(2,1)S(1)}, u32[]{:S(2)}, u32[]{:S(2)}) collective-permute-start(bf16[288,256]{1,0:T(8,128)(2,1)S(1)} %get-tuple-element.94.refs_1_), channel_id=1, source_target_pairs={{0,8},{8,0},{16,24},{24,16},{1,9},{9,1},{17,25},{25,17},{2,10},{10... | collective-permute-start | bytes 442376 | tf_op jit(solution)/shard_map/ppermute | solution.py:567
  83.4 18.1 %collective-permute-start.19 = (bf16[288,256]{1,0:T(8,128)(2,1)S(1)}, bf16[288,256]{1,0:T(8,128)(2,1)S(1)}, u32[]{:S(2)}, u32[]{:S(2)}) collective-permute-start(bf16[288,256]{1,0:T(8,128)(2,1)S(1)} %get-tuple-element.100.refs_1_), channel_id=1, source_target_pairs={{0,6},{2,4},{4,2},{6,0},{1,7},{3,5},{5,3},{7,1},{8,14},{10,12},{12... | collective-permute-start | bytes 442376 | tf_op jit(solution)/shard_map/ppermute | solution.py:519
  86.1 15.5 %collective-permute-start.18 = (bf16[288,256]{1,0:T(8,128)(2,1)S(1)}, bf16[288,256]{1,0:T(8,128)(2,1)S(1)}, u32[]{:S(2)}, u32[]{:S(2)}) collective-permute-start(bf16[288,256]{1,0:T(8,128)(2,1)S(1)} %get-tuple-element.100.refs_1_), channel_id=1, source_target_pairs={{0,4},{2,6},{4,0},{6,2},{1,5},{3,7},{5,1},{7,3},{8,12},{10,14},{12... | collective-permute-start | bytes 442376 | tf_op jit(solution)/shard_map/ppermute | solution.py:519
  87.2 14.3 %collective-permute-start.17 = (bf16[288,256]{1,0:T(8,128)(2,1)S(1)}, bf16[288,256]{1,0:T(8,128)(2,1)S(1)}, u32[]{:S(2)}, u32[]{:S(2)}) collective-permute-start(bf16[288,256]{1,0:T(8,128)(2,1)S(1)} %get-tuple-element.100.refs_1_), channel_id=1, source_target_pairs={{0,2},{2,0},{4,6},{6,4},{1,3},{3,1},{5,7},{7,5},{8,10},{10,8},{12,... | collective-permute-start | bytes 442376 | tf_op jit(solution)/shard_map/ppermute | solution.py:519
  87.3 14.2 %collective-permute-start.16 = (bf16[288,256]{1,0:T(8,128)(2,1)S(1)}, bf16[288,256]{1,0:T(8,128)(2,1)S(1)}, u32[]{:S(2)}, u32[]{:S(2)}) collective-permute-start(bf16[288,256]{1,0:T(8,128)(2,1)S(1)} %get-tuple-element.98.refs_1_), channel_id=1, source_target_pairs={{0,16},{8,24},{16,0},{24,8},{1,17},{9,25},{17,1},{25,9},{2,18},{10... | collective-permute-start | bytes 442376 | tf_op jit(solution)/shard_map/ppermute | solution.py:567
  101.6 2.8 %collective-permute-start.20 = (bf16[4,288,256]{2,1,0:T(8,128)(2,1)S(1)}, bf16[4,288,256]{2,1,0:T(8,128)(2,1)S(1)}, u32[]{:S(2)}, u32[]{:S(2)}) collective-permute-start(bf16[4,288,256]{2,1,0:T(8,128)(2,1)S(1)} %get-tuple-element.102.refs_2_), channel_id=1, source_target_pairs={{0,1},{1,0},{2,3},{3,2},{4,5},{5,4},{6,7},{7,6},{8,9},{9,8},{10,11... | collective-permute-start | bytes 1769480 | tf_op jit(solution)/shard_map/ppermute | solution.py:580
  101.7 6.0 %collective-permute-start.23 = (bf16[288,256]{1,0:T(8,128)(2,1)S(1)}, bf16[288,256]{1,0:T(8,128)(2,1)S(1)}, u32[]{:S(2)}, u32[]{:S(2)}) collective-permute-start(bf16[288,256]{1,0:T(8,128)(2,1)S(1)} %get-tuple-element.104.refs_1_), channel_id=1, source_target_pairs={{0,6},{2,4},{4,2},{6,0},{1,7},{3,5},{5,3},{7,1},{8,14},{10,12},{12... | collective-permute-start | bytes 442376 | tf_op jit(solution)/shard_map/ppermute | solution.py:519
  102.2 7.7 %collective-permute-start.22 = (bf16[288,256]{1,0:T(8,128)(2,1)S(1)}, bf16[288,256]{1,0:T(8,128)(2,1)S(1)}, u32[]{:S(2)}, u32[]{:S(2)}) collective-permute-start(bf16[288,256]{1,0:T(8,128)(2,1)S(1)} %get-tuple-element.104.refs_1_), channel_id=1, source_target_pairs={{0,4},{2,6},{4,0},{6,2},{1,5},{3,7},{5,1},{7,3},{8,12},{10,14},{12... | collective-permute-start | bytes 442376 | tf_op jit(solution)/shard_map/ppermute | solution.py:519
  103.0 8.5 %collective-permute-start.21 = (bf16[288,256]{1,0:T(8,128)(2,1)S(1)}, bf16[288,256]{1,0:T(8,128)(2,1)S(1)}, u32[]{:S(2)}, u32[]{:S(2)}) collective-permute-start(bf16[288,256]{1,0:T(8,128)(2,1)S(1)} %get-tuple-element.104.refs_1_), channel_id=1, source_target_pairs={{0,2},{2,0},{4,6},{6,4},{1,3},{3,1},{5,7},{7,5},{8,10},{10,8},{12,... | collective-permute-start | bytes 442376 | tf_op jit(solution)/shard_map/ppermute | solution.py:519
  111.6 2.2 %collective-permute-start.24 = (bf16[4,288,256]{2,1,0:T(8,128)(2,1)S(1)}, bf16[4,288,256]{2,1,0:T(8,128)(2,1)S(1)}, u32[]{:S(2)}, u32[]{:S(2)}) collective-permute-start(bf16[4,288,256]{2,1,0:T(8,128)(2,1)S(1)} %get-tuple-element.106.refs_2_), channel_id=1, source_target_pairs={{0,1},{1,0},{2,3},{3,2},{4,5},{5,4},{6,7},{7,6},{8,9},{9,8},{10,11... | collective-permute-start | bytes 1769480 | tf_op jit(solution)/shard_map/ppermute | solution.py:580
  (8 other events, 58.0 us)

commit v7 on v6

--- a/solution.py
+++ b/solution.py
@@ -604,14 +604,14 @@
     )
     out_others = from_others(out_part, ("x", "y"))
     in_part, in_other, token = middle("in_mid", in_part, in_other, [token])
-    outputs, token = outputs_conv(
-        low, low_up, low_down, out_kernel.reshape(3, 3 * p, c), x, skip.reshape(1, c), block, token
-    )
     in_part, token = sums("in_total", grad_scale, [in_part, in_other], [token])
     in_others = from_others(in_part, ("x", "y"))
     out_packed, out_other, token = pack("out_pack", [out_part] + out_others, [token])
+    outputs, token = outputs_conv(
+        low, low_up, low_down, out_kernel.reshape(3, 3 * p, c), x, skip.reshape(1, c), block, token
+    )
+    in_packed, in_other, token = pack("in_pack", [in_part] + in_others, [token])
     out_grad, token = merge("out_merge", out_packed, out_other, [token], FAR)
-    in_packed, in_other, token = pack("in_pack", [in_part] + in_others, [token])
     in_grad, _ = merge("in_merge", in_packed, in_other, [token])
     return (
         outputs.reshape(inputs.shape),

time: 116 us -> 118 us (1.017)
  waiting for transfers between devices: 24.1 us -> 27.3 us
  starting transfers between devices: 32.5 us -> 31.2 us
    ppermute x4, waiting for transfers between devices: 1.99 us -> 12.4 us  [swapped(): return lax.ppermute(part, 'a', [(i, i ^ bit) for i in range(deep)])]
    ppermute x2, waiting for transfers between devices: 9.61 us -> 4.29 us  [row_halo(): down = lax.ppermute(first, axes, [(i + 1, i) for i in range(count - 1)])]
    ppermute x2, starting transfers between devices: 0.63 us -> 2.43 us  [pack(): return (packed, lax.ppermute(packed, 'core', CORES), token)]
    ppermute x2, waiting for transfers between devices: 1.63 us -> 0.01 us  [pack(): return (packed, lax.ppermute(packed, 'core', CORES), token)]
    ppermute x4, starting transfers between devices: 4.21 us -> 2.62 us  [swapped(): return lax.ppermute(part, 'a', [(i, i ^ bit) for i in range(deep)])]
    ppermute x12, starting transfers between devices: 12.2 us -> 10.7 us  [from_others(): lax.ppermute(part, axes, [(i, i ^ k) for i in range(count)])]
  transfers between devices with their start and end apart: 25 -> 25, of which waited for: 13 -> 11; matrix products, arithmetic and copies ran while one was open for 0% -> 0% of each run, Pallas kernels for 24% -> 24%
where the time goes in v7:
time: 118 us
  Pallas kernels  46.7 us (40%)
  starting transfers between devices  31.2 us (26%)
  waiting for transfers between devices  27.3 us (23%)
  blocking collectives  11 us (9%)
    ppermute x4, waiting for transfers between devices, swapped(): return lax.ppermute(part, 'a', [(i, i ^ bit) for i in range(deep)])  12.4 us
    all_to_all x1, blocking collectives, per_device(): ends = lax.all_to_all(ends, 'a', 0, 0)  11 us
    ppermute x12, starting transfers between devices, from_others(): lax.ppermute(part, axes, [(i, i ^ k) for i in range(count)])  10.7 us
    ppermute x2, starting transfers between devices, row_halo(): up = lax.ppermute(last, axes, [(i, i + 1) for i in range(count - 1)])  9.07 us
    pallas_call x1, Pallas kernels, kernel_grads(): pl.pallas_call(in_grad_kernel, grid=(frames // block,), in_specs=lead + [...  7.83 us
    pallas_call x14, Pallas kernels, small_call(): pl.pallas_call(kernel, in_specs=[ANYWHERE] * len(after) + [SCALARS] * len...  7.72 us
    pallas_call x1, Pallas kernels, kernel_grads(): pl.pallas_call(out_grad_kernel, grid=(frames // block,), in_specs=lead +...  7.27 us
    pallas_call x1, Pallas kernels, outputs_conv(): pl.pallas_call(outputs_kernel, grid=(frames // block,), in_specs=[pl.Bloc...  6.64 us
  transfers between devices with their start and end apart: 25, of which 11 were waited for; matrix products, arithmetic and copies ran while one was open for 0% of the time, Pallas kernels for 24%

profile of v7, /device:TPU:1, one launch (start us, length us, event | category | flops | bytes accessed | tf_op | source)
XLA Modules:
  0.0 117.8 jit_solution(2871048832438816698)
XLA Ops:
  1.2 3.1 %edge_rows.1 = (bf16[2,64,16,256]{3,2,1,0:T(8,128)(2,1)}, bf16[2,64,16,256]{3,2,1,0:T(8,128)(2,1)}) custom-call(s32[4]{0:T(128)} %pad_add_fusion.places_ref.refs_0_.place_ref.refs_1_, bf16[64,4,16,256]{3,2,1,0:T(8,128)(2,1)} %bitcast.16, bf16[64,4,16,256]{3,2,1,0:T(8,128)(2,1)} %bitcast.17, bf16[64,4,16,256]{3,2,1,0:T(8,128)(2,1)} %bitcast.12, ...), custom_call_target="tpu_custom_call" | custom-call | bytes 4194304 | tf_op jit(solution)/shard_map/edge_rows/pallas_call | solution.py:427
  4.3 4.5 %collective-permute-start = (bf16[2,64,16,256]{3,2,1,0:T(8,128)(2,1)}, bf16[2,64,16,256]{3,2,1,0:T(8,128)(2,1)S(1)}, u32[]{:S(2)}, u32[]{:S(2)}) collective-permute-start(bf16[2,64,16,256]{3,2,1,0:T(8,128)(2,1)} %get-tuple-element.57), channel_id=1, source_target_pairs={{0,1},{1,2},{2,3},{4,5},{5,6},{6,7},{8,9},{9,10},{10,11},{12,13},{... | collective-permute-start | bytes 3145736 | tf_op jit(solution)/shard_map/ppermute | solution.py:442
  8.9 1.9 %collective-permute-start.1 = (bf16[2,64,16,256]{3,2,1,0:T(8,128)(2,1)}, bf16[2,64,16,256]{3,2,1,0:T(8,128)(2,1)S(1)}, u32[]{:S(2)}, u32[]{:S(2)}) collective-permute-start(bf16[2,64,16,256]{3,2,1,0:T(8,128)(2,1)} %get-tuple-element.58), channel_id=1, source_target_pairs={{1,0},{2,1},{3,2},{5,4},{6,5},{7,6},{9,8},{10,9},{11,10},{13,12},{... | collective-permute-start | bytes 3145736 | tf_op jit(solution)/shard_map/ppermute | solution.py:443
  10.8 4.8 %interior_in.1.part_ref = f32[4,64,16,256]{3,2,1,0:T(8,128)S(1)} custom-call(bf16[64,4,16,256]{3,2,1,0:T(8,128)(2,1)S(1)} %bitcast.18, bf16[3,768,256]{2,1,0:T(8,128)(2,1)S(1)} %bitcast.21), custom_call_target="tpu_custom_call" | custom-call | flops 4831838208 | bytes 8388608 | tf_op jit(solution)/shard_map/interior_in/pallas_call | solution.py:106
  15.6 5.2 %interior_cot.1 = (f32[4,64,16,256]{3,2,1,0:T(8,128)S(1)}, bf16[3,768,256]{2,1,0:T(8,128)(2,1)S(1)}) custom-call(bf16[64,4,16,256]{3,2,1,0:T(8,128)(2,1)S(1)} %bitcast.14, bf16[3,3,256,256]{3,2,1,0:T(8,128)(2,1)S(1)} %copy-done.5), custom_call_target="tpu_custom_call" | custom-call | flops 4831838208 | bytes 8388608 | tf_op jit(solution)/shard_map/interior_cot/pallas_call | solution.py:91
  20.9 4.3 %collective-permute-done.1.down_ref = bf16[2,64,16,256]{3,2,1,0:T(8,128)(2,1)S(1)} collective-permute-done((bf16[2,64,16,256]{3,2,1,0:T(8,128)(2,1)}, bf16[2,64,16,256]{3,2,1,0:T(8,128)(2,1)S(1)}, u32[]{:S(2)}, u32[]{:S(2)}) %collective-permute-start.1) | collective-permute-done | bytes 1048608 | tf_op jit(solution)/shard_map/ppermute | solution.py:443
  25.2 2.0 %scan_fwd.1 = (f32[4,64,16,256]{3,2,1,0:T(8,128)S(1)}, f32[64,256]{1,0:T(8,128)S(1)}, f32[64,256]{1,0:T(8,128)S(1)}) custom-call(f32[4,64,16,256]{3,2,1,0:T(8,128)S(1)} %interior_in.1.part_ref, bf16[2,64,16,256]{3,2,1,0:T(8,128)(2,1)S(1)} %collective-permute-done.up_ref, bf16[2,64,16,256]{3,2,1,0:T(8,128)(2,1)S(1)} %collective-permute-done.1.down_ref, ...), custom_call_target="tpu_custom_call" | custom-call | flops 805306368 | bytes 12582912 | tf_op jit(solution)/shard_map/scan_fwd/pallas_call | solution.py:180
  27.3 2.2 %scan_back.1 = (f32[4,64,16,256]{3,2,1,0:T(8,128)S(1)}, f32[64,256]{1,0:T(8,128)S(1)}, f32[136,256]{1,0:T(8,128)S(1)}) custom-call(f32[4,64,16,256]{3,2,1,0:T(8,128)S(1)} %get-tuple-element.56.part_ref, bf16[2,64,16,256]{3,2,1,0:T(8,128)(2,1)S(1)} %collective-permute-done.up_ref, bf16[2,64,16,256]{3,2,1,0:T(8,128)(2,1)S(1)} %collective-permute-done.1.down_ref, ...), custom_call_target="tpu_custom_call" | custom-call | flops 805306368 | bytes 12582912 | tf_op jit(solution)/shard_map/scan_back/pallas_call | solution.py:180
  30.7 2.7 %collective-permute-done.2.refs_2_.pair_ref = f32[136,256]{1,0:T(8,128)S(1)} collective-permute-done((f32[136,256]{1,0:T(8,128)S(1)}, f32[136,256]{1,0:T(8,128)S(1)}, u32[]{:S(2)}, u32[]{:S(2)}) %collective-permute-start.2) | collective-permute-done | bytes 139296 | tf_op jit(solution)/shard_map/ppermute | solution.py:544
  34.5 11.0 %all_to_all.5.ends_ref = f32[4,72,256]{2,1,0:T(8,128)S(1)} all-to-all(f32[4,72,256]{2,1,0:T(8,128)S(1)} %get-tuple-element.62), channel_id=1, replica_groups=mesh['a'=4,'x'=2,'y'=2,'core'=2] {'a'}, dimensions={0} | all-to-all | bytes 589824 | tf_op jit(solution)/shard_map/all_to_all | solution.py:548
  45.6 7.3 %out_grad.1 = (bf16[4,64,16,256]{3,2,1,0:T(8,128)(2,1)S(1)}, bf16[64,16,256]{2,1,0:T(8,128)(2,1)S(1)}, bf16[64,16,256]{2,1,0:T(8,128)(2,1)S(1)}, bf16[1152,256]{...) custom-call(s32[4]{0:T(128)S(1)} %copy-done.4, f32[4,72,256]{2,1,0:T(8,128)S(1)} %all_to_all.5.ends_ref, ...), custom_call_target="tpu_custom_call" | custom-call | flops 4831838208 | bytes 10485760 | tf_op jit(solution)/shard_map/out_grad/pallas_call | solution.py:349
  52.9 2.0 %collective-permute-done.3.refs_3_ = bf16[1152,256]{1,0:T(8,128)(2,1)S(1)} collective-permute-done((bf16[1152,256]{1,0:T(8,128)(2,1)S(1)}, bf16[1152,256]{1,0:T(8,128)(2,1)S(1)}, u32[]{:S(2)}, u32[]{:S(2)}) %collective-permute-start.3) | collective-permute-done | bytes 589856 | tf_op jit(solution)/shard_map/ppermute | solution.py:553
  55.6 2.3 %collective-permute-start.4 = (bf16[288,256]{1,0:T(8,128)(2,1)S(1)}, bf16[288,256]{1,0:T(8,128)(2,1)S(1)}, u32[]{:S(2)}, u32[]{:S(2)}) collective-permute-start(bf16[288,256]{1,0:T(8,128)(2,1)S(1)} %get-tuple-element.74), channel_id=1, source_target_pairs={{0,2},{2,0},{4,6},{6,4},{1,3},{3,1},{5,7},{7,5},{8,10},{10,8},{12,... | collective-permute-start | bytes 442376 | tf_op jit(solution)/shard_map/ppermute | solution.py:519
  59.1 7.8 %in_grad.1 = (bf16[1152,256]{1,0:T(8,128)(2,1)S(1)}, f32[1152,256]{1,0:T(8,128)S(1)}, f32[8,128]{1,0:T(8,128)S(1)}) custom-call(s32[4]{0:T(128)S(1)} %copy-done.4, f32[4,72,256]{2,1,0:T(8,128)S(1)} %all_to_all.5.ends_ref, f32[136,256]{1,0:T(8,128)S(1)} %collective-permute-done.2.refs_2_.pair_ref, f32[4,64,16,256]{3,2,1,0:T(8,128)S(1)} %get-tuple-element.66.local_ref, ...), custom_call_target="tpu_custom_call" | custom-call | flops 4831838208 | bytes 10485760 | tf_op jit(solution)/shard_map/in_grad/pallas_call | solution.py:360
  70.3 1.7 %collective-permute-start.11 = (bf16[288,256]{1,0:T(8,128)(2,1)S(1)}, bf16[288,256]{1,0:T(8,128)(2,1)S(1)}, u32[]{:S(2)}, u32[]{:S(2)}) collective-permute-start(bf16[288,256]{1,0:T(8,128)(2,1)S(1)} %get-tuple-element.88), channel_id=1, source_target_pairs={{0,2},{2,0},{4,6},{6,4},{1,3},{3,1},{5,7},{7,5},{8,10},{10,8},{12,... | collective-permute-start | bytes 442376 | tf_op jit(solution)/shard_map/ppermute | solution.py:519
  74.7 4.5 %collective-permute-start.9 = (bf16[64,16,256]{2,1,0:T(8,128)(2,1)S(1)}, bf16[64,16,256]{2,1,0:T(8,128)(2,1)S(1)}, u32[]{:S(2)}, u32[]{:S(2)}) collective-permute-start(bf16[64,16,256]{2,1,0:T(8,128)(2,1)S(1)} %get-tuple-element.85), channel_id=1, source_target_pairs={{0,1},{1,2},{2,3},{4,5},{5,6},{6,7},{8,9},{9,10},{10,11},{12,13},{... | collective-permute-start | bytes 1572872 | tf_op jit(solution)/shard_map/ppermute | solution.py:442
  79.3 2.1 %collective-permute-start.10 = (bf16[64,16,256]{2,1,0:T(8,128)(2,1)S(1)}, bf16[64,16,256]{2,1,0:T(8,128)(2,1)S(1)}, u32[]{:S(2)}, u32[]{:S(2)}) collective-permute-start(bf16[64,16,256]{2,1,0:T(8,128)(2,1)S(1)} %get-tuple-element.86), channel_id=1, source_target_pairs={{1,0},{2,1},{3,2},{5,4},{6,5},{7,6},{9,8},{10,9},{11,10},{13,12},{... | collective-permute-start | bytes 1572872 | tf_op jit(solution)/shard_map/ppermute | solution.py:443
  83.4 3.8 %collective-permute-done.15.refs_2_ = bf16[288,256]{1,0:T(8,128)(2,1)S(1)} collective-permute-done((bf16[288,256]{1,0:T(8,128)(2,1)S(1)}, bf16[288,256]{1,0:T(8,128)(2,1)S(1)}, u32[]{:S(2)}, u32[]{:S(2)}) %collective-permute-start.15) | collective-permute-done | bytes 147488 | tf_op jit(solution)/shard_map/ppermute | solution.py:567
  89.3 7.4 %collective-permute-done.16.refs_2_ = bf16[288,256]{1,0:T(8,128)(2,1)S(1)} collective-permute-done((bf16[288,256]{1,0:T(8,128)(2,1)S(1)}, bf16[288,256]{1,0:T(8,128)(2,1)S(1)}, u32[]{:S(2)}, u32[]{:S(2)}) %collective-permute-start.16) | collective-permute-done | bytes 147488 | tf_op jit(solution)/shard_map/ppermute | solution.py:567
  96.8 4.4 %collective-permute-done.17.refs_2_ = bf16[288,256]{1,0:T(8,128)(2,1)S(1)} collective-permute-done((bf16[288,256]{1,0:T(8,128)(2,1)S(1)}, bf16[288,256]{1,0:T(8,128)(2,1)S(1)}, u32[]{:S(2)}, u32[]{:S(2)}) %collective-permute-start.17) | collective-permute-done | bytes 147488 | tf_op jit(solution)/shard_map/ppermute | solution.py:519
  101.2 1.9 %collective-permute-start.23 = (bf16[4,288,256]{2,1,0:T(8,128)(2,1)S(1)}, bf16[4,288,256]{2,1,0:T(8,128)(2,1)S(1)}, u32[]{:S(2)}, u32[]{:S(2)}) collective-permute-start(bf16[4,288,256]{2,1,0:T(8,128)(2,1)S(1)} %get-tuple-element.104.refs_2_), channel_id=1, source_target_pairs={{0,1},{1,0},{2,3},{3,2},{4,5},{5,4},{6,7},{7,6},{8,9},{9,8},{10,11... | collective-permute-start | bytes 1769480 | tf_op jit(solution)/shard_map/ppermute | solution.py:580
  105.8 6.6 %outputs_conv.1 = (bf16[64,4,16,256]{3,2,1,0:T(8,128)(2,1)}, f32[8,128]{1,0:T(8,128)S(1)}) custom-call(bf16[4,64,16,256]{3,2,1,0:T(8,128)(2,1)S(1)} %get-tuple-element.65.low_ref, bf16[64,16,256]{2,1,0:T(8,128)(2,1)S(1)} %collective-permute-done.9.up_ref, bf16[64,16,256]{2,1,0:T(8,128)(2,1)S(1)} %collective-permute-done.10.down_ref, ...), custom_call_target="tpu_custom_call" | custom-call | flops 4831838208 | bytes 8388608 | tf_op jit(solution)/shard_map/outputs_conv/pallas_call | solution.py:393
  113.6 2.1 %out_merge.1 = (f32[2304,256]{1,0:T(8,128)}, f32[8,128]{1,0:T(8,128)S(1)}) custom-call(f32[8,128]{1,0:T(8,128)S(1)} %get-tuple-element.103.refs_0_, s32[4]{0:T(128)S(1)} %copy-done.4, bf16[4,288,256]{2,1,0:T(8,128)(2,1)S(1)} %get-tuple-element.104.refs_2_, bf16[4,288,256]{2,1,0:T(8,128)(2,1)S(1)} %collective-permute-done.23.refs_3_), custom_call_target="tpu_custom_call" | custom-call | flops 34359738368 | bytes 2097152 | tf_op jit(solution)/shard_map/out_merge/pallas_call | solution.py:459
  115.7 2.1 %in_merge.1 = (f32[2304,256]{1,0:T(8,128)}, f32[8,128]{1,0:T(8,128)}) custom-call(f32[8,128]{1,0:T(8,128)S(1)} %get-tuple-element.105.refs_0_, s32[4]{0:T(128)S(1)} %copy-done.4, bf16[4,288,256]{2,1,0:T(8,128)(2,1)S(1)} %get-tuple-element.106.refs_2_, bf16[4,288,256]{2,1,0:T(8,128)(2,1)S(1)} %collective-permute-done.24.refs_3_), custom_call_target="tpu_custom_call" | custom-call | flops 1073741824 | bytes 2097152 | tf_op jit(solution)/shard_map/in_merge/pallas_call | solution.py:459
  (64 shorter events, 19.0 us)
Async XLA Ops:
  4.3 16.6 %collective-permute-start = (bf16[2,64,16,256]{3,2,1,0:T(8,128)(2,1)}, bf16[2,64,16,256]{3,2,1,0:T(8,128)(2,1)S(1)}, u32[]{:S(2)}, u32[]{:S(2)}) collective-permute-start(bf16[2,64,16,256]{3,2,1,0:T(8,128)(2,1)} %get-tuple-element.57), channel_id=1, source_target_pairs={{0,1},{1,2},{2,3},{4,5},{5,6},{6,7},{8,9},{9,10},{10,11},{12,13},{... | collective-permute-start | bytes 3145736 | tf_op jit(solution)/shard_map/ppermute | solution.py:442
  8.9 16.3 %collective-permute-start.1 = (bf16[2,64,16,256]{3,2,1,0:T(8,128)(2,1)}, bf16[2,64,16,256]{3,2,1,0:T(8,128)(2,1)S(1)}, u32[]{:S(2)}, u32[]{:S(2)}) collective-permute-start(bf16[2,64,16,256]{3,2,1,0:T(8,128)(2,1)} %get-tuple-element.58), channel_id=1, source_target_pairs={{1,0},{2,1},{3,2},{5,4},{6,5},{7,6},{9,8},{10,9},{11,10},{13,12},{... | collective-permute-start | bytes 3145736 | tf_op jit(solution)/shard_map/ppermute | solution.py:443
  29.4 4.0 %collective-permute-start.2 = (f32[136,256]{1,0:T(8,128)S(1)}, f32[136,256]{1,0:T(8,128)S(1)}, u32[]{:S(2)}, u32[]{:S(2)}) collective-permute-start(f32[136,256]{1,0:T(8,128)S(1)} %get-tuple-element.61.refs_1_), channel_id=1, source_target_pairs={{0,4},{4,0},{1,5},{5,1},{2,6},{6,2},{3,7},{7,3},{8,12},{12,8},{9,1... | collective-permute-start | bytes 417800 | tf_op jit(solution)/shard_map/ppermute | solution.py:544
  55.6 12.4 %collective-permute-start.4 = (bf16[288,256]{1,0:T(8,128)(2,1)S(1)}, bf16[288,256]{1,0:T(8,128)(2,1)S(1)}, u32[]{:S(2)}, u32[]{:S(2)}) collective-permute-start(bf16[288,256]{1,0:T(8,128)(2,1)S(1)} %get-tuple-element.74), channel_id=1, source_target_pairs={{0,2},{2,0},{4,6},{6,4},{1,3},{3,1},{5,7},{7,5},{8,10},{10,8},{12,... | collective-permute-start | bytes 442376 | tf_op jit(solution)/shard_map/ppermute | solution.py:519
  57.9 10.1 %collective-permute-start.5 = (bf16[288,256]{1,0:T(8,128)(2,1)S(1)}, bf16[288,256]{1,0:T(8,128)(2,1)S(1)}, u32[]{:S(2)}, u32[]{:S(2)}) collective-permute-start(bf16[288,256]{1,0:T(8,128)(2,1)S(1)} %get-tuple-element.75), channel_id=1, source_target_pairs={{0,4},{2,6},{4,0},{6,2},{1,5},{3,7},{5,1},{7,3},{8,12},{10,14},{12... | collective-permute-start | bytes 442376 | tf_op jit(solution)/shard_map/ppermute | solution.py:519
  59.1 8.9 %collective-permute-start.6 = (bf16[288,256]{1,0:T(8,128)(2,1)S(1)}, bf16[288,256]{1,0:T(8,128)(2,1)S(1)}, u32[]{:S(2)}, u32[]{:S(2)}) collective-permute-start(bf16[288,256]{1,0:T(8,128)(2,1)S(1)} %get-tuple-element.76), channel_id=1, source_target_pairs={{0,6},{2,4},{4,2},{6,0},{1,7},{3,5},{5,3},{7,1},{8,14},{10,12},{12... | collective-permute-start | bytes 442376 | tf_op jit(solution)/shard_map/ppermute | solution.py:519
  67.0 2.6 %collective-permute-start.7 = (bf16[1152,256]{1,0:T(8,128)(2,1)S(1)}, bf16[1152,256]{1,0:T(8,128)(2,1)S(1)}, u32[]{:S(2)}, u32[]{:S(2)}) collective-permute-start(bf16[1152,256]{1,0:T(8,128)(2,1)S(1)} %get-tuple-element.79), channel_id=1, source_target_pairs={{0,1},{1,0},{2,3},{3,2},{4,5},{5,4},{6,7},{7,6},{8,9},{9,8},{10,11... | collective-permute-start | bytes 1769480 | tf_op jit(solution)/shard_map/ppermute | solution.py:590
  68.0 5.5 %collective-permute-start.8 = (bf16[288,256]{1,0:T(8,128)(2,1)S(1)}, bf16[288,256]{1,0:T(8,128)(2,1)S(1)}, u32[]{:S(2)}, u32[]{:S(2)}) collective-permute-start(bf16[288,256]{1,0:T(8,128)(2,1)S(1)} %get-tuple-element.81.refs_1_), channel_id=1, source_target_pairs={{0,8},{8,0},{16,24},{24,16},{1,9},{9,1},{17,25},{25,17},{2,10},{10... | collective-permute-start | bytes 442376 | tf_op jit(solution)/shard_map/ppermute | solution.py:567
  70.3 9.0 %collective-permute-start.11 = (bf16[288,256]{1,0:T(8,128)(2,1)S(1)}, bf16[288,256]{1,0:T(8,128)(2,1)S(1)}, u32[]{:S(2)}, u32[]{:S(2)}) collective-permute-start(bf16[288,256]{1,0:T(8,128)(2,1)S(1)} %get-tuple-element.88), channel_id=1, source_target_pairs={{0,2},{2,0},{4,6},{6,4},{1,3},{3,1},{5,7},{7,5},{8,10},{10,8},{12,... | collective-permute-start | bytes 442376 | tf_op jit(solution)/shard_map/ppermute | solution.py:519
  72.0 9.4 %collective-permute-start.12 = (bf16[288,256]{1,0:T(8,128)(2,1)S(1)}, bf16[288,256]{1,0:T(8,128)(2,1)S(1)}, u32[]{:S(2)}, u32[]{:S(2)}) collective-permute-start(bf16[288,256]{1,0:T(8,128)(2,1)S(1)} %get-tuple-element.89), channel_id=1, source_target_pairs={{0,4},{2,6},{4,0},{6,2},{1,5},{3,7},{5,1},{7,3},{8,12},{10,14},{12... | collective-permute-start | bytes 442376 | tf_op jit(solution)/shard_map/ppermute | solution.py:519
  73.2 8.2 %collective-permute-start.13 = (bf16[288,256]{1,0:T(8,128)(2,1)S(1)}, bf16[288,256]{1,0:T(8,128)(2,1)S(1)}, u32[]{:S(2)}, u32[]{:S(2)}) collective-permute-start(bf16[288,256]{1,0:T(8,128)(2,1)S(1)} %get-tuple-element.90), channel_id=1, source_target_pairs={{0,6},{2,4},{4,2},{6,0},{1,7},{3,5},{5,3},{7,1},{8,14},{10,12},{12... | collective-permute-start | bytes 442376 | tf_op jit(solution)/shard_map/ppermute | solution.py:519
  73.6 9.7 %collective-permute-start.14 = (bf16[288,256]{1,0:T(8,128)(2,1)S(1)}, bf16[288,256]{1,0:T(8,128)(2,1)S(1)}, u32[]{:S(2)}, u32[]{:S(2)}) collective-permute-start(bf16[288,256]{1,0:T(8,128)(2,1)S(1)} %get-tuple-element.92.refs_1_), channel_id=1, source_target_pairs={{0,16},{8,24},{16,0},{24,8},{1,17},{9,25},{17,1},{25,9},{2,18},{10... | collective-permute-start | bytes 442376 | tf_op jit(solution)/shard_map/ppermute | solution.py:567
  74.7 29.6 %collective-permute-start.9 = (bf16[64,16,256]{2,1,0:T(8,128)(2,1)S(1)}, bf16[64,16,256]{2,1,0:T(8,128)(2,1)S(1)}, u32[]{:S(2)}, u32[]{:S(2)}) collective-permute-start(bf16[64,16,256]{2,1,0:T(8,128)(2,1)S(1)} %get-tuple-element.85), channel_id=1, source_target_pairs={{0,1},{1,2},{2,3},{4,5},{5,6},{6,7},{8,9},{9,10},{10,11},{12,13},{... | collective-permute-start | bytes 1572872 | tf_op jit(solution)/shard_map/ppermute | solution.py:442
  79.3 26.5 %collective-permute-start.10 = (bf16[64,16,256]{2,1,0:T(8,128)(2,1)S(1)}, bf16[64,16,256]{2,1,0:T(8,128)(2,1)S(1)}, u32[]{:S(2)}, u32[]{:S(2)}) collective-permute-start(bf16[64,16,256]{2,1,0:T(8,128)(2,1)S(1)} %get-tuple-element.86), channel_id=1, source_target_pairs={{1,0},{2,1},{3,2},{5,4},{6,5},{7,6},{9,8},{10,9},{11,10},{13,12},{... | collective-permute-start | bytes 1572872 | tf_op jit(solution)/shard_map/ppermute | solution.py:443
  81.5 5.7 %collective-permute-start.15 = (bf16[288,256]{1,0:T(8,128)(2,1)S(1)}, bf16[288,256]{1,0:T(8,128)(2,1)S(1)}, u32[]{:S(2)}, u32[]{:S(2)}) collective-permute-start(bf16[288,256]{1,0:T(8,128)(2,1)S(1)} %get-tuple-element.94.refs_1_), channel_id=1, source_target_pairs={{0,8},{8,0},{16,24},{24,16},{1,9},{9,1},{17,25},{25,17},{2,10},{10... | collective-permute-start | bytes 442376 | tf_op jit(solution)/shard_map/ppermute | solution.py:567
  87.2 9.5 %collective-permute-start.16 = (bf16[288,256]{1,0:T(8,128)(2,1)S(1)}, bf16[288,256]{1,0:T(8,128)(2,1)S(1)}, u32[]{:S(2)}, u32[]{:S(2)}) collective-permute-start(bf16[288,256]{1,0:T(8,128)(2,1)S(1)} %get-tuple-element.96.refs_1_), channel_id=1, source_target_pairs={{0,16},{8,24},{16,0},{24,8},{1,17},{9,25},{17,1},{25,9},{2,18},{10... | collective-permute-start | bytes 442376 | tf_op jit(solution)/shard_map/ppermute | solution.py:567
  87.9 8.9 %collective-permute-start.19 = (bf16[288,256]{1,0:T(8,128)(2,1)S(1)}, bf16[288,256]{1,0:T(8,128)(2,1)S(1)}, u32[]{:S(2)}, u32[]{:S(2)}) collective-permute-start(bf16[288,256]{1,0:T(8,128)(2,1)S(1)} %get-tuple-element.98.refs_1_), channel_id=1, source_target_pairs={{0,6},{2,4},{4,2},{6,0},{1,7},{3,5},{5,3},{7,1},{8,14},{10,12},{12... | collective-permute-start | bytes 442376 | tf_op jit(solution)/shard_map/ppermute | solution.py:519
  89.1 7.8 %collective-permute-start.18 = (bf16[288,256]{1,0:T(8,128)(2,1)S(1)}, bf16[288,256]{1,0:T(8,128)(2,1)S(1)}, u32[]{:S(2)}, u32[]{:S(2)}) collective-permute-start(bf16[288,256]{1,0:T(8,128)(2,1)S(1)} %get-tuple-element.98.refs_1_), channel_id=1, source_target_pairs={{0,4},{2,6},{4,0},{6,2},{1,5},{3,7},{5,1},{7,3},{8,12},{10,14},{12... | collective-permute-start | bytes 442376 | tf_op jit(solution)/shard_map/ppermute | solution.py:519
  96.7 4.5 %collective-permute-start.17 = (bf16[288,256]{1,0:T(8,128)(2,1)S(1)}, bf16[288,256]{1,0:T(8,128)(2,1)S(1)}, u32[]{:S(2)}, u32[]{:S(2)}) collective-permute-start(bf16[288,256]{1,0:T(8,128)(2,1)S(1)} %get-tuple-element.98.refs_1_), channel_id=1, source_target_pairs={{0,2},{2,0},{4,6},{6,4},{1,3},{3,1},{5,7},{7,5},{8,10},{10,8},{12,... | collective-permute-start | bytes 442376 | tf_op jit(solution)/shard_map/ppermute | solution.py:519
  101.2 12.3 %collective-permute-start.23 = (bf16[4,288,256]{2,1,0:T(8,128)(2,1)S(1)}, bf16[4,288,256]{2,1,0:T(8,128)(2,1)S(1)}, u32[]{:S(2)}, u32[]{:S(2)}) collective-permute-start(bf16[4,288,256]{2,1,0:T(8,128)(2,1)S(1)} %get-tuple-element.104.refs_2_), channel_id=1, source_target_pairs={{0,1},{1,0},{2,3},{3,2},{4,5},{5,4},{6,7},{7,6},{8,9},{9,8},{10,11... | collective-permute-start | bytes 1769480 | tf_op jit(solution)/shard_map/ppermute | solution.py:580
  103.1 9.3 %collective-permute-start.22 = (bf16[288,256]{1,0:T(8,128)(2,1)S(1)}, bf16[288,256]{1,0:T(8,128)(2,1)S(1)}, u32[]{:S(2)}, u32[]{:S(2)}) collective-permute-start(bf16[288,256]{1,0:T(8,128)(2,1)S(1)} %get-tuple-element.102.refs_1_), channel_id=1, source_target_pairs={{0,6},{2,4},{4,2},{6,0},{1,7},{3,5},{5,3},{7,1},{8,14},{10,12},{12... | collective-permute-start | bytes 442376 | tf_op jit(solution)/shard_map/ppermute | solution.py:519
  104.0 8.4 %collective-permute-start.21 = (bf16[288,256]{1,0:T(8,128)(2,1)S(1)}, bf16[288,256]{1,0:T(8,128)(2,1)S(1)}, u32[]{:S(2)}, u32[]{:S(2)}) collective-permute-start(bf16[288,256]{1,0:T(8,128)(2,1)S(1)} %get-tuple-element.102.refs_1_), channel_id=1, source_target_pairs={{0,4},{2,6},{4,0},{6,2},{1,5},{3,7},{5,1},{7,3},{8,12},{10,14},{12... | collective-permute-start | bytes 442376 | tf_op jit(solution)/shard_map/ppermute | solution.py:519
  104.3 8.6 %collective-permute-start.20 = (bf16[288,256]{1,0:T(8,128)(2,1)S(1)}, bf16[288,256]{1,0:T(8,128)(2,1)S(1)}, u32[]{:S(2)}, u32[]{:S(2)}) collective-permute-start(bf16[288,256]{1,0:T(8,128)(2,1)S(1)} %get-tuple-element.102.refs_1_), channel_id=1, source_target_pairs={{0,2},{2,0},{4,6},{6,4},{1,3},{3,1},{5,7},{7,5},{8,10},{10,8},{12,... | collective-permute-start | bytes 442376 | tf_op jit(solution)/shard_map/ppermute | solution.py:519
  113.0 2.7 %collective-permute-start.24 = (bf16[4,288,256]{2,1,0:T(8,128)(2,1)S(1)}, bf16[4,288,256]{2,1,0:T(8,128)(2,1)S(1)}, u32[]{:S(2)}, u32[]{:S(2)}) collective-permute-start(bf16[4,288,256]{2,1,0:T(8,128)(2,1)S(1)} %get-tuple-element.106.refs_2_), channel_id=1, source_target_pairs={{0,1},{1,0},{2,3},{3,2},{4,5},{5,4},{6,7},{7,6},{8,9},{9,8},{10,11... | collective-permute-start | bytes 1769480 | tf_op jit(solution)/shard_map/ppermute | solution.py:580
  (8 other events, 55.6 us)
